TPU v7x, 128 devices: a whole 4x4x4 slice. The times are simulated.
128 devices in a mesh: row: 32 (over z, y, core), col: 4 (over x).
Axes of the slice: x: 4, y: 4, z: 4, core: 2. Of those that a mesh axis runs over, the one named last changes fastest.
Arguments:
- source_vectors: bfloat16 [256, 512, 768], P('row'), may hold values from -5 to 5
- target_vectors: bfloat16 [64, 512, 768], P('row', 'col'), may hold values from -1 to 1
- pair_list: int32 [256, 12], P('row'), may hold values from 0 to 63, as said below
- counts: int32 [256], P('row'), may hold values from 4 to 12, as said below
- owner_map: int32 [64], replicated, may hold values from 0 to 63, as said below
Outputs:
- source_dual: float32 [256, 512], P('row')
- target_dual: float32 [64, 512], P('row', 'col')
Inputs may be any that keep to these rules, and one draw needn't show every extreme that they name: `pair_list`: source blocks 4 m to 4 m + 3 list the same ids in the same order. The 12 ids of one source block differ, and so do all ids listed by the source blocks 8 r, 8 r + 4, ... up to 8 r + 4 for each r; their storage slots owner_map[id] fall at most 1 times into any range of slots 2 o to 2 o + 1, and exactly 1 times into some. Source block s uses the first counts[s] of its listed ids; both ends of the range occur. `owner_map`: A permutation of the storage slots.
All inputs are finite; a program needn't handle non-finite values.
Results may differ from a plain program's by a relative error of at most 0.0003.
Values may be sent and summed in bfloat16 or wider, within the bound.
No kernel may reach another device: no remote copies, remote signals or barrier semaphores. Data moves between devices by JAX's collectives and lax.ppermute only.
A program may use at most 128 MiB of HBM per device.

v0:
```python
import jax
import jax.numpy as jnp
from jax import lax
from jax.sharding import PartitionSpec as P

SHARE = 4
SWEEPS = 3


EPSILON = 0.05
NEGATIVE = -1e30


def combined_all(part, axis, combine):
    gathered = jax.tree.map(lambda a: lax.all_gather(a, axis), part)

    def take(source):
        return jax.tree.map(lambda a: lax.dynamic_index_in_dim(a, source, 0, False), gathered)

    return lax.fori_loop(
        1, lax.axis_size(axis), lambda source, state: combine(state, take(source)), take(0)
    )


def fold_pair(earlier_pair, later_pair):
    highest = jnp.maximum(earlier_pair[0], later_pair[0])
    return (
        highest,
        earlier_pair[1] * jnp.exp(earlier_pair[0] - highest)
        + later_pair[1] * jnp.exp(later_pair[0] - highest),
    )


def with_dustbin(maxima, totals):
    highest = jnp.maximum(maxima, 0.0)
    return -EPSILON * (highest + jnp.log(totals * jnp.exp(maxima - highest) + jnp.exp(-highest)))


def masked_fold(chosen, maxima, totals):
    spread = jnp.where(chosen[:, :, None], maxima[None, :, :], NEGATIVE)
    highest = jnp.max(spread, axis=1)
    weights = jnp.where(
        chosen[:, :, None],
        totals[None, :, :] * jnp.exp(maxima[None, :, :] - highest[:, None, :]),
        0.0,
    )
    return (highest, jnp.sum(weights, axis=1))


def shards(source_vectors, target_vectors, pair_list, counts, owner_map):
    row_count = lax.axis_size("row")
    source_blocks, block_rows, feature_width = source_vectors.shape
    target_blocks, quarter, _ = target_vectors.shape
    listed = pair_list.shape[1]
    capacity = target_blocks // 2
    slot_total = row_count * capacity
    group_count = source_blocks // SHARE
    group_total = group_count * listed
    all_targets = owner_map.shape[0]
    lead_pairs = pair_list.reshape(group_count, SHARE, listed)[:, 0, :].reshape(group_total)
    lookup = lead_pairs[:, None] == jnp.arange(all_targets, dtype=jnp.int32)[None, :]
    stored = jnp.sum(jnp.where(lookup, owner_map[None, :], 0), axis=1)
    owner_row = stored // target_blocks
    local_index = stored % target_blocks
    entry_ids = jnp.arange(group_total, dtype=jnp.int32)
    earlier = (owner_row[:, None] == owner_row[None, :]) & (entry_ids[None, :] < entry_ids[:, None])
    slot_of = owner_row * capacity + jnp.sum(earlier.astype(jnp.int32), axis=1)
    alive_entry = jnp.arange(listed, dtype=jnp.int32)[None, :] < counts[:, None]
    alive_group = jnp.any(alive_entry.reshape(group_count, SHARE, listed), axis=1).reshape(
        group_total
    )
    slot_match = slot_of[None, :] == jnp.arange(slot_total, dtype=jnp.int32)[:, None]
    slot_alive = jnp.any(slot_match & alive_group[None, :], axis=1)
    slot_local = jnp.sum(jnp.where(slot_match, local_index[None, :], 0), axis=1)
    slot_entry = jnp.sum(jnp.where(slot_match, entry_ids[None, :], 0), axis=1)
    wanted = lax.all_to_all(
        slot_local.reshape(row_count, capacity), "row", split_axis=0, concat_axis=0, tiled=True
    )
    served = target_vectors[wanted]
    fetched = lax.all_to_all(served, "row", split_axis=0, concat_axis=0, tiled=True).reshape(
        slot_total, quarter, feature_width
    )
    entry_slots = jnp.broadcast_to(
        slot_of.reshape(group_count, listed)[:, None, :], (group_count, SHARE, listed)
    ).reshape(source_blocks, listed)

    def block_scores(inputs):
        source_rows, slots_here = inputs
        return jnp.einsum(
            "id,kjd->kij", source_rows, fetched[slots_here], preferred_element_type=jnp.float32
        )

    scores = lax.map(block_scores, (source_vectors, entry_slots))
    entry_duals = jnp.zeros((source_blocks, listed, quarter), jnp.float32)
    source_dual = jnp.zeros((source_blocks, block_rows), jnp.float32)
    target_dual = jnp.zeros((target_blocks, quarter), jnp.float32)
    for sweep_index in range(SWEEPS):
        logits = (entry_duals[:, :, None, :] + scores) / EPSILON
        logits = jnp.where(alive_entry[:, :, None, None], logits, NEGATIVE)
        row_highest = jnp.max(logits, axis=(1, 3))
        row_sum = jnp.sum(jnp.exp(logits - row_highest[:, None, :, None]), axis=(1, 3))
        row_highest, row_sum = combined_all((row_highest, row_sum), "col", fold_pair)
        source_dual = with_dustbin(row_highest, row_sum)
        columns = (source_dual[:, None, :, None] + scores) / EPSILON
        column_highest = jnp.max(columns, axis=2)
        column_sum = jnp.sum(jnp.exp(columns - column_highest[:, :, None, :]), axis=2)
        column_highest = jnp.where(alive_entry[:, :, None], column_highest, NEGATIVE)
        column_sum = jnp.where(alive_entry[:, :, None], column_sum, 0.0)
        member_highest = column_highest.reshape(group_count, SHARE, listed, quarter)
        member_sum = column_sum.reshape(group_count, SHARE, listed, quarter)
        group_highest = jnp.max(member_highest, axis=1)
        group_sum = jnp.sum(
            member_sum * jnp.exp(member_highest - group_highest[:, None, :, :]), axis=1
        )
        flat_highest = group_highest.reshape(group_total, quarter)[slot_entry]
        flat_sum = group_sum.reshape(group_total, quarter)[slot_entry]
        slot_highest = jnp.where(slot_alive[:, None], flat_highest, NEGATIVE)
        slot_sum = jnp.where(slot_alive[:, None], flat_sum, 0.0)
        back_highest, back_sum, back_ids = (
            lax.all_to_all(
                slot_highest.reshape(row_count, capacity, quarter),
                "row",
                split_axis=0,
                concat_axis=0,
                tiled=True,
            ),
            lax.all_to_all(
                slot_sum.reshape(row_count, capacity, quarter),
                "row",
                split_axis=0,
                concat_axis=0,
                tiled=True,
            ),
            lax.all_to_all(
                slot_local.astype(jnp.float32).reshape(row_count, capacity),
                "row",
                split_axis=0,
                concat_axis=0,
                tiled=True,
            ),
        )
        owned_by = (
            jnp.arange(target_blocks, dtype=jnp.float32)[:, None]
            == back_ids.reshape(slot_total)[None, :]
        )
        owned_highest, owned_sum = masked_fold(
            owned_by,
            back_highest.reshape(slot_total, quarter),
            back_sum.reshape(slot_total, quarter),
        )
        target_dual = with_dustbin(owned_highest, owned_sum)
        if sweep_index + 1 < SWEEPS:
            sending = target_dual[back_ids.astype(jnp.int32)]
            slot_duals = lax.all_to_all(
                sending, "row", split_axis=0, concat_axis=0, tiled=True
            ).reshape(slot_total, quarter)
            entry_duals = slot_duals[entry_slots]
    return (source_dual, target_dual)


def solution(mesh):
    return jax.shard_map(
        shards,
        mesh=mesh,
        in_specs=(P("row", None, None), P("row", "col", None), P("row", None), P("row"), P()),
        out_specs=(P("row", None), P("row", "col")),
        check_vma=False,
    )
```

profile of v0, /device:TPU:1, one launch (start us, length us, event | category | flops | bytes accessed | tf_op | source)
XLA Modules:
  0.0 475.7 jit_solution(3531690759818001698)
XLA Ops:
  3.3 9.6 %all-to-all-start.1 = ((s32[32,1,1]{2,1,0:T(1,128)}), s32[32,1,1]{2,1,0:T(1,128)S(1)}, u32[]{:S(2)}, u32[]{:S(2)}) async-start(s32[32,1,1]{2,1,0:T(1,128)} %copy.28), calls=%async_computation.1 | async-start | bytes 32768 | tf_op jit(solution)/shard_map/all_to_all | solution.py:76
  37.9 71.3 %all-to-all-done.2 = bf16[32,1,128,768]{3,2,1,0:T(8,128)(2,1)} async-done(((bf16[32,1,128,768]{3,2,1,0:T(8,128)(2,1)}), bf16[32,1,128,768]{3,2,1,0:T(8,128)(2,1)}, u32[]{:S(2)}, u32[]{:S(2)}) %all-to-all-start.2) | async-done | bytes 6291488 | tf_op jit(solution)/shard_map/all_to_all | solution.py:80
  109.2 61.9 %while.61 = (s32[]{:T(128)}, f32[8,12,512,128]{2,3,1,0:T(8,128)}, s32[8,12]{1,0:T(8,128)S(1)}, bf16[32,128,768]{2,1,0:T(8,128)(2,1)}, bf16[8,512,768]{2,1,0:T(8,128)(2,1)}, /*index=5*/s32[]{:T(128)}) while((s32[]{:T(128)}, f32[8,12,512,128]{2,3,1,0:T(8,128)}, s32[8,12]{1,0:T(8,128)S(1)}, bf16[32,128,768]{2,1,0:T(8,128)(2,1)}, ...), condition=%wide.region_6.7_spmd, body=%wide.region_5.6_spmd.sunk | while | flops 1207960576 | bytes 11015433 | solution.py:93
  171.1 10.5 %fusion.11 = f32[8,512]{1,0:T(8,128)S(1)} fusion(f32[8,12,512,128]{2,3,1,0:T(8,128)} %get-tuple-element.428, pred[8,12]{1,0:T(8,128)(4,1)S(1)} %iota_compare_fusion.4), kind=kLoop, calls=%fused_computation.48 | loop fusion | flops 18870272 | bytes 25182304 | tf_op jit(solution)/shard_map/reduce_max | solution.py:100
  192.0 9.3 %all-gather = f32[32,512]{1,0:T(8,128)S(1)} all-gather(f32[8,512]{1,0:T(8,128)S(1)} %fusion.11), channel_id=2, replica_groups=mesh['row'=32,'col'=4] {'col'}, dimensions={0}, use_global_device_ids=true | all-gather | bytes 81920 | tf_op jit(solution)/shard_map/all_gather | solution.py:15
  201.3 9.0 %all-gather.1 = f32[32,512]{1,0:T(8,128)S(1)} all-gather(f32[8,512]{1,0:T(8,128)S(1)} %exponential_reduce_fusion.5), channel_id=3, replica_groups=mesh['row'=32,'col'=4] {'col'}, dimensions={0}, use_global_device_ids=true | all-gather | bytes 81920 | tf_op jit(solution)/shard_map/all_gather | solution.py:15
  210.5 9.8 %fusion.12 = f32[8,12,128]{2,1,0:T(8,128)S(1)} fusion(f32[8,12,512,128]{2,3,1,0:T(8,128)} %get-tuple-element.428, f32[8,512]{1,0:T(8,128)S(1)} %fusion.22), kind=kLoop, calls=%fused_computation.49 | loop fusion | flops 18862080 | bytes 25231360 | tf_op jit(solution)/shard_map/reduce_max | solution.py:105
  220.3 11.6 %exponential_reduce_fusion.4 = f32[8,12,128]{2,1,0:T(8,128)S(1)} fusion(f32[8,12,512,128]{2,3,1,0:T(8,128)} %get-tuple-element.428, f32[8,12,128]{2,1,0:T(8,128)S(1)} %fusion.12, f32[8,512]{1,0:T(8,128)S(1)} %fusion.22), kind=kLoop, calls=%fused_computation.44 | loop fusion | flops 25153536 | bytes 25280512 | tf_op jit(solution)/shard_map/reduce_sum | solution.py:106
  233.9 14.5 %all-to-all-start.3 = ((f32[32,1,128]{2,1,0:T(1,128)}), f32[32,1,128]{2,1,0:T(1,128)S(1)}, u32[]{:S(2)}, u32[]{:S(2)}) async-start(f32[32,1,128]{2,1,0:T(1,128)} %bitcast.23), calls=%async_computation.3 | async-start | bytes 32768 | tf_op jit(solution)/shard_map/all_to_all | solution.py:120
  248.5 7.0 %all-to-all-done.3 = f32[32,1,128]{2,1,0:T(1,128)S(1)} async-done(((f32[32,1,128]{2,1,0:T(1,128)}), f32[32,1,128]{2,1,0:T(1,128)S(1)}, u32[]{:S(2)}, u32[]{:S(2)}) %all-to-all-start.3) | async-done | bytes 16416 | tf_op jit(solution)/shard_map/all_to_all | solution.py:120
  279.7 10.3 %fusion.15 = f32[8,512]{1,0:T(8,128)S(1)} fusion(f32[8,12,512,128]{2,3,1,0:T(8,128)} %get-tuple-element.428, f32[8,12,128]{2,1,0:T(8,128)S(1)} %reshape.546, pred[8,12]{1,0:T(8,128)(4,1)S(1)} %iota_compare_fusion.4), kind=kLoop, calls=%fused_computation.52 | loop fusion | flops 25161728 | bytes 25231456 | tf_op jit(solution)/shard_map/reduce_max | solution.py:100
  290.0 11.6 %exponential_reduce_fusion.3 = f32[8,512]{1,0:T(8,128)S(1)} fusion(f32[8,12,512,128]{2,3,1,0:T(8,128)} %get-tuple-element.428, f32[8,512]{1,0:T(8,128)S(1)} %fusion.15, f32[8,12,128]{2,1,0:T(8,128)S(1)} %reshape.546, pred[8,12]{1,0:T(8,128)(4,1)S(1)} %iota_compare_fusion.4), kind=kLoop, calls=%fused_computation.42 | loop fusion | flops 31453184 | bytes 25247840 | tf_op jit(solution)/shard_map/reduce_sum | solution.py:101
  301.6 9.0 %all-gather.2 = f32[32,512]{1,0:T(8,128)S(1)} all-gather(f32[8,512]{1,0:T(8,128)S(1)} %fusion.15), channel_id=4, replica_groups=mesh['row'=32,'col'=4] {'col'}, dimensions={0}, use_global_device_ids=true | all-gather | bytes 81920 | tf_op jit(solution)/shard_map/all_gather | solution.py:15
  310.6 9.0 %all-gather.3 = f32[32,512]{1,0:T(8,128)S(1)} all-gather(f32[8,512]{1,0:T(8,128)S(1)} %exponential_reduce_fusion.3), channel_id=5, replica_groups=mesh['row'=32,'col'=4] {'col'}, dimensions={0}, use_global_device_ids=true | all-gather | bytes 81920 | tf_op jit(solution)/shard_map/all_gather | solution.py:15
  319.8 9.8 %fusion.13 = f32[8,12,128]{2,1,0:T(8,128)S(1)} fusion(f32[8,12,512,128]{2,3,1,0:T(8,128)} %get-tuple-element.428, f32[8,512]{1,0:T(8,128)S(1)} %fusion.28), kind=kLoop, calls=%fused_computation.50 | loop fusion | flops 18862080 | bytes 25231360 | tf_op jit(solution)/shard_map/reduce_max | solution.py:105
  329.6 11.6 %exponential_reduce_fusion.2 = f32[8,12,128]{2,1,0:T(8,128)S(1)} fusion(f32[8,12,512,128]{2,3,1,0:T(8,128)} %get-tuple-element.428, f32[8,12,128]{2,1,0:T(8,128)S(1)} %fusion.13, f32[8,512]{1,0:T(8,128)S(1)} %fusion.28), kind=kLoop, calls=%fused_computation.40 | loop fusion | flops 25153536 | bytes 25280512 | tf_op jit(solution)/shard_map/reduce_sum | solution.py:106
  343.2 16.4 %all_to_all.59 = f32[32,1,128]{2,1,0:T(1,128)S(1)} all-to-all(f32[32,1,128]{2,1,0:T(1,128)S(1)} %bitcast.154), channel_id=1, replica_groups=mesh['row'=32,'col'=4] {'row'}, dimensions={0} | all-to-all | bytes 32768 | tf_op jit(solution)/shard_map/all_to_all | solution.py:120
  383.8 10.3 %fusion.16 = f32[8,512]{1,0:T(8,128)S(1)} fusion(f32[8,12,512,128]{2,3,1,0:T(8,128)} %get-tuple-element.428, f32[8,12,128]{2,1,0:T(8,128)S(1)} %reshape.578, pred[8,12]{1,0:T(8,128)(4,1)S(1)} %iota_compare_fusion.4), kind=kLoop, calls=%fused_computation.53 | loop fusion | flops 25161728 | bytes 25231456 | tf_op jit(solution)/shard_map/reduce_max | solution.py:100
  394.2 11.6 %exponential_reduce_fusion.1 = f32[8,512]{1,0:T(8,128)S(1)} fusion(f32[8,12,512,128]{2,3,1,0:T(8,128)} %get-tuple-element.428, f32[8,512]{1,0:T(8,128)S(1)} %fusion.16, f32[8,12,128]{2,1,0:T(8,128)S(1)} %reshape.578, pred[8,12]{1,0:T(8,128)(4,1)S(1)} %iota_compare_fusion.4), kind=kLoop, calls=%fused_computation.38 | loop fusion | flops 31453184 | bytes 25247840 | tf_op jit(solution)/shard_map/reduce_sum | solution.py:101
  405.8 9.0 %all-gather.4 = f32[32,512]{1,0:T(8,128)S(1)} all-gather(f32[8,512]{1,0:T(8,128)S(1)} %fusion.16), channel_id=6, replica_groups=mesh['row'=32,'col'=4] {'col'}, dimensions={0}, use_global_device_ids=true | all-gather | bytes 81920 | tf_op jit(solution)/shard_map/all_gather | solution.py:15
  414.8 9.0 %all-gather.5 = f32[32,512]{1,0:T(8,128)S(1)} all-gather(f32[8,512]{1,0:T(8,128)S(1)} %exponential_reduce_fusion.1), channel_id=7, replica_groups=mesh['row'=32,'col'=4] {'col'}, dimensions={0}, use_global_device_ids=true | all-gather | bytes 81920 | tf_op jit(solution)/shard_map/all_gather | solution.py:15
  423.9 9.8 %fusion.14 = f32[8,12,128]{2,1,0:T(8,128)S(1)} fusion(f32[8,12,512,128]{2,3,1,0:T(8,128)} %get-tuple-element.428, f32[8,512]{1,0:T(8,128)S(1)} %fusion.34), kind=kLoop, calls=%fused_computation.51 | loop fusion | flops 18862080 | bytes 25231360 | tf_op jit(solution)/shard_map/reduce_max | solution.py:105
  433.8 11.6 %exponential_reduce_fusion = f32[8,12,128]{2,1,0:T(8,128)S(1)} fusion(f32[8,12,512,128]{2,3,1,0:T(8,128)} %get-tuple-element.428, f32[8,12,128]{2,1,0:T(8,128)S(1)} %fusion.14, f32[8,512]{1,0:T(8,128)S(1)} %fusion.34), kind=kLoop, calls=%fused_computation.36 | loop fusion | flops 25153536 | bytes 25280512 | tf_op jit(solution)/shard_map/reduce_sum | solution.py:106
  447.4 16.4 %all_to_all.60 = f32[32,1,128]{2,1,0:T(1,128)S(1)} all-to-all(f32[32,1,128]{2,1,0:T(1,128)S(1)} %bitcast.153), channel_id=1, replica_groups=mesh['row'=32,'col'=4] {'row'}, dimensions={0} | all-to-all | bytes 32768 | tf_op jit(solution)/shard_map/all_to_all | solution.py:120
  (144 shorter events, 166.6 us)
Async XLA Ops:
  0.6 24.0 %copy-start = (bf16[2,128,768]{2,1,0:T(8,128)(2,1)S(1)}, bf16[2,128,768]{2,1,0:T(8,128)(2,1)}, u32[]{:S(2)}) copy-start(bf16[2,128,768]{2,1,0:T(8,128)(2,1)} %param.14) | copy-start | bytes 1179652
  0.6 35.7 %copy-start.3 = (s32[8]{0:T(128)S(1)}, s32[8]{0:T(128)}, u32[]{:S(2)}) copy-start(s32[8]{0:T(128)} %param.16) | copy-start | bytes 100
  3.3 16.5 %all-to-all-start.1 = ((s32[32,1,1]{2,1,0:T(1,128)}), s32[32,1,1]{2,1,0:T(1,128)S(1)}, u32[]{:S(2)}, u32[]{:S(2)}) async-start(s32[32,1,1]{2,1,0:T(1,128)} %copy.28), calls=%async_computation.1 | async-start | bytes 32768 | tf_op jit(solution)/shard_map/all_to_all | solution.py:76
  19.8 11.2 %all-to-all-start = ((f32[32,1,1]{2,1,0:T(1,128)}), f32[32,1,1]{2,1,0:T(1,128)S(1)}, u32[]{:S(2)}, u32[]{:S(2)}) async-start(f32[32,1,1]{2,1,0:T(1,128)} %copy.27), calls=%async_computation | async-start | bytes 32768 | tf_op jit(solution)/shard_map/all_to_all | solution.py:134
  31.0 78.2 %all-to-all-start.2 = ((bf16[32,1,128,768]{3,2,1,0:T(8,128)(2,1)}), bf16[32,1,128,768]{3,2,1,0:T(8,128)(2,1)}, u32[]{:S(2)}, u32[]{:S(2)}) async-start(bf16[32,1,128,768]{3,2,1,0:T(8,128)(2,1)} %bitcast.135), calls=%async_computation.2 | async-start | bytes 12582912 | tf_op jit(solution)/shard_map/all_to_all | solution.py:80
  171.1 15.4 %copy-start.1 = (f32[8,12,512,128]{2,3,1,0:T(8,128)S(1)}, f32[8,12,512,128]{2,3,1,0:T(8,128)}, u32[]{:S(2)}) copy-start(f32[8,12,512,128]{2,3,1,0:T(8,128)} %get-tuple-element.428) | copy-start | bytes 75497472
  233.9 21.6 %all-to-all-start.3 = ((f32[32,1,128]{2,1,0:T(1,128)}), f32[32,1,128]{2,1,0:T(1,128)S(1)}, u32[]{:S(2)}, u32[]{:S(2)}) async-start(f32[32,1,128]{2,1,0:T(1,128)} %bitcast.23), calls=%async_computation.3 | async-start | bytes 32768 | tf_op jit(solution)/shard_map/all_to_all | solution.py:120
  255.5 11.1 %all-to-all-start.4 = ((f32[32,1,128]{2,1,0:T(1,128)}), f32[32,1,128]{2,1,0:T(1,128)S(1)}, u32[]{:S(2)}, u32[]{:S(2)}) async-start(f32[32,1,128]{2,1,0:T(1,128)} %bitcast.27), calls=%async_computation.4 | async-start | bytes 32768 | tf_op jit(solution)/shard_map/all_to_all | solution.py:127
  267.9 11.1 %all-to-all-start.5 = ((f32[32,1,128]{2,1,0:T(1,128)}), f32[32,1,128]{2,1,0:T(1,128)S(1)}, u32[]{:S(2)}, u32[]{:S(2)}) async-start(f32[32,1,128]{2,1,0:T(1,128)} %bitcast.30), calls=%async_computation.5 | async-start | bytes 32768 | tf_op jit(solution)/shard_map/all_to_all | solution.py:154
  359.7 11.1 %all-to-all-start.7 = ((f32[32,1,128]{2,1,0:T(1,128)}), f32[32,1,128]{2,1,0:T(1,128)S(1)}, u32[]{:S(2)}, u32[]{:S(2)}) async-start(f32[32,1,128]{2,1,0:T(1,128)} %bitcast.41), calls=%async_computation.7 | async-start | bytes 32768 | tf_op jit(solution)/shard_map/all_to_all | solution.py:127
  372.1 11.1 %all-to-all-start.8 = ((f32[32,1,128]{2,1,0:T(1,128)}), f32[32,1,128]{2,1,0:T(1,128)S(1)}, u32[]{:S(2)}, u32[]{:S(2)}) async-start(f32[32,1,128]{2,1,0:T(1,128)} %bitcast.44), calls=%async_computation.8 | async-start | bytes 32768 | tf_op jit(solution)/shard_map/all_to_all | solution.py:154
  423.9 21.5 %copy-start.2 = (f32[8,512]{1,0:T(8,128)}, f32[8,512]{1,0:T(8,128)S(1)}, u32[]{:S(2)}) copy-start(f32[8,512]{1,0:T(8,128)S(1)} %fusion.34) | copy-start | bytes 49156
  463.8 11.2 %all-to-all-start.10 = ((f32[32,1,128]{2,1,0:T(1,128)}), f32[32,1,128]{2,1,0:T(1,128)S(1)}, u32[]{:S(2)}, u32[]{:S(2)}) async-start(f32[32,1,128]{2,1,0:T(1,128)} %bitcast.54), calls=%async_computation.10 | async-start | bytes 32768 | tf_op jit(solution)/shard_map/all_to_all | solution.py:127
where the time goes:
time: 478 us; the launch traced here: 476 us
  other arithmetic  131 us (27%)
  waiting for transfers between devices  122 us (26%)
  blocking collectives  87 us (18%)
  starting transfers between devices  54.1 us (11%)
  local copies, waits for them, and re-layouts  46.1 us (10%)
  matrix products  33.9 us (7%)
    all_to_all x1, waiting for transfers between devices, shards(): lax.all_to_all(served, 'row', split_axis=0, concat_axis=0, tiled=True)  71.3 us
    all_gather x6, blocking collectives, combined_all(): gathered = jax.tree.map(lambda a: lax.all_gather(a, axis), part)  54.2 us
    reduce_sum x3, other arithmetic, shards(): jnp.sum(jnp.exp(columns - column_highest[:, :, None, :]), axis=2)  34.7 us
    dot_general x8, matrix products, block_scores(): jnp.einsum('id,kjd->kij', source_rows, fetched[slots_here], preferred_ele...  33.9 us
    all_to_all x2, blocking collectives, shards(): lax.all_to_all(slot_highest.reshape(row_count, capacity, quarter), 'row',...  32.8 us
    reduce_max x3, other arithmetic, shards(): row_highest = jnp.max(logits, axis=(1, 3))  31.2 us
    reduce_max x3, other arithmetic, shards(): column_highest = jnp.max(columns, axis=2)  29.5 us
    reduce_sum x3, other arithmetic, shards(): jnp.sum(jnp.exp(logits - row_highest[:, None, :, None]), axis=(1, 3))  28.7 us
  transfers between devices with their start and end apart: 9, of which 9 were waited for; matrix products, arithmetic and copies ran while one was open for 1% of the time, Pallas kernels for 0%

commit v1 on v0

v1 whole, which is shorter than its diff:
```python
import functools

import jax
import jax.numpy as jnp
import numpy as np
from jax import lax
from jax.experimental import pallas as pl
from jax.experimental.pallas import tpu as pltpu
from jax.sharding import PartitionSpec as P

SHARE = 4
SWEEPS = 3
EPSILON = 0.05
CHUNKS = (64, 64)
LOG2E = 1.4426950408889634
LN2 = 0.6931471805599453
SCALE = LOG2E / EPSILON
NEGATIVE = -1e30
MIB = 2**20


def row_perm(dz, dy, dc):
    return [
        ((z * 4 + y) * 2 + c, (((z + dz) % 4) * 4 + (y + dy) % 4) * 2 + (c ^ dc))
        for z in range(4)
        for y in range(4)
        for c in range(2)
    ]


def send(x, dz, dy, dc):
    return lax.ppermute(x, "row", row_perm(dz, dy, dc))


RING = (0, -1, 1, 2)


def ring_gather(own, dz, dy):
    half = own.shape[1] // 2
    before = send(own, dz, dy, 0)
    after = send(own, -dz, -dy, 0)
    far_low = send(before[:, :half], dz, dy, 0)
    far_high = send(after[:, half:], -dz, -dy, 0)
    far = jnp.concatenate([far_low, far_high], axis=1)
    return jnp.concatenate([own, before, after, far], axis=0)


def ring_spread(four, dz, dy):
    before = send(four, dz, dy, 0)
    after = send(four, -dz, -dy, 0)
    far_low = send(before[:2], dz, dy, 0)
    far_high = send(after[2:], -dz, -dy, 0)
    return [four, before, after, far_low, far_high]


def gather_plane(blocks):
    first = ring_gather(blocks[:1], 0, 1)
    second = ring_gather(blocks[1:], 1, 0)
    mine = ring_spread(first, 1, 0) + ring_spread(second, 0, 1)
    return mine + [send(piece, 0, 0, 1) for piece in mine]


def piece_layout():
    entries = []
    for core in range(2):
        for which in range(2):
            for part in range(5):
                across = (0, -1, 1, 2, 2)[part]
                for index, along in enumerate((RING, RING, RING, RING[:2], RING[2:])[part]):
                    dz, dy = (across, along) if which == 0 else (along, across)
                    entries.append(((core * 2 + which) * 5 + part, index, dz, dy, core, which))
    return entries


def make_score_kernel(rows):
    def kernel(dest, counts, source, *refs):
        pieces = refs[:20]
        kernel_out, peak_out, high_out, total_out, held, sums, sems = refs[20:]
        layout = piece_layout()
        step = pl.program_id(0)
        group = step // SHARE
        listed = kernel_out.shape[1]

        def fetch(piece, index, entry):
            return pltpu.make_async_copy(
                pieces[piece].at[index], held.at[pl.ds(entry * rows, rows)], sems.at[entry]
            )

        @pl.when(step == 0)
        def _():
            for number, (piece, index, *_) in enumerate(layout):

                @pl.when(dest[number] >= 0)
                def _():
                    fetch(piece, index, dest[number]).start()

        for g in range(2):

            @pl.when(step == SHARE * g)
            def _():
                for k in range(listed):
                    fetch(0, 0, g * listed + k).wait()

        live = counts[step]

        def batch(first, size):
            base = pl.multiple_of((group * listed + first) * rows, rows)
            scores = lax.dot_general(
                held[pl.ds(base, size * rows), :],
                source[0],
                (((1,), (1,)), ((), ())),
                preferred_element_type=jnp.float32,
            )
            for p in range(size):
                one = scores[p * rows : (p + 1) * rows] * SCALE
                peak = jnp.max(one, axis=0, keepdims=True)
                raised = jnp.exp2(one - peak)
                kernel_out[0, first + p] = raised
                peak_out[0, pl.ds(first + p, 1), :] = peak
                sums[pl.ds(first + p, 1), :] = jnp.sum(raised, axis=0, keepdims=True)

        big = 512 // rows
        small = 128 // rows
        bigs = live // big
        done = bigs * big

        def big_step(q, carry):
            batch(q * big, big)
            return carry

        def small_step(q, carry):
            batch(done + q * small, small)
            return carry

        lax.fori_loop(0, bigs, big_step, 0)
        lax.fori_loop(0, (live - done + small - 1) // small, small_step, 0)
        alive = lax.broadcasted_iota(jnp.int32, sums.shape, 0) < live
        peaks = jnp.where(alive, peak_out[0], NEGATIVE)
        peak_out[0] = peaks
        high = jnp.max(peaks, axis=0, keepdims=True)
        total = jnp.sum(
            jnp.where(alive, sums[...] * jnp.exp2(peaks - high), 0.0), axis=0, keepdims=True
        )
        high_out[pl.ds(step, 1), :] = high
        total_out[pl.ds(step, 1), :] = total

    return kernel


def score_stage(rows, dest, counts, source_vectors, pieces, listed):
    blocks, block_rows, width = source_vectors.shape
    padded = 16
    return pl.pallas_call(
        make_score_kernel(rows),
        grid_spec=pltpu.PrefetchScalarGridSpec(
            num_scalar_prefetch=2,
            grid=(blocks,),
            in_specs=[pl.BlockSpec((1, block_rows, width), lambda s, *_: (s, 0, 0))]
            + [pl.BlockSpec(memory_space=pl.ANY)] * len(pieces),
            out_specs=[
                pl.BlockSpec((1, listed, rows, block_rows), lambda s, *_: (s, 0, 0, 0)),
                pl.BlockSpec((1, padded, block_rows), lambda s, *_: (s, 0, 0)),
                pl.BlockSpec((blocks, block_rows), lambda s, *_: (0, 0)),
                pl.BlockSpec((blocks, block_rows), lambda s, *_: (0, 0)),
            ],
            scratch_shapes=[
                pltpu.VMEM((2 * listed * rows, width), jnp.bfloat16),
                pltpu.VMEM((padded, block_rows), jnp.float32),
                pltpu.SemaphoreType.DMA((2 * listed,)),
            ],
        ),
        out_shape=[
            jax.ShapeDtypeStruct((blocks, listed, rows, block_rows), jnp.float32),
            jax.ShapeDtypeStruct((blocks, padded, block_rows), jnp.float32),
            jax.ShapeDtypeStruct((blocks, block_rows), jnp.float32),
            jax.ShapeDtypeStruct((blocks, block_rows), jnp.float32),
        ],
        compiler_params=pltpu.CompilerParams(vmem_limit_bytes=24 * MIB),
        cost_estimate=pl.CostEstimate(
            flops=2 * blocks * listed * rows * block_rows * width,
            bytes_accessed=4 * blocks * listed * rows * block_rows,
            transcendentals=0,
        ),
        name="scores",
    )(dest, counts, source_vectors, *pieces)


def column_kernel(chunks, final, counts, slots, level, part, near, far, back, *refs):
    n = len(chunks)
    matrices, peaks = refs[:n], refs[n : 2 * n]
    sums_out = refs[2 * n]
    weights, columns = refs[-2:]
    blocks, block_rows = part.shape
    listed = matrices[0].shape[1]
    total = part[...] + near[...] + far[...] + back[...] + jnp.exp2(-level[...])
    inverse = 1.0 / total
    if final:
        refs[2 * n + 1][...] = -EPSILON * LN2 * (level[...] + jnp.log2(total))
    for c in range(n):
        for s in range(blocks):
            weights[c, s] = jnp.exp2(peaks[c][s] - level[s : s + 1, :]) * inverse[s : s + 1, :]
    sums_out[...] = jnp.zeros_like(sums_out)
    for g in range(blocks // SHARE):
        longest = functools.reduce(jnp.maximum, [counts[g * SHARE + m] for m in range(SHARE)])

        def one_entry(k, carry):
            for c, rows in enumerate(chunks):
                start = sum(chunks[:c])
                columns[start : start + rows, :] = jnp.zeros((rows, 128), jnp.float32)
            for m in range(SHARE):
                s = g * SHARE + m

                @pl.when(k < counts[s])
                def _():
                    for c, rows in enumerate(chunks):
                        start = sum(chunks[:c])
                        w = weights[c, s, pl.ds(k, 1), :]
                        spread = [
                            jnp.broadcast_to(w[:, 128 * l : 128 * l + 128], (8, 128))
                            for l in range(block_rows // 128)
                        ]
                        for j in range(0, rows, 8):
                            piece = columns[start + j : start + j + 8, :]
                            for l, ws in enumerate(spread):
                                piece = piece + matrices[c][s, k, j : j + 8, 128 * l : 128 * l + 128] * ws
                            columns[start + j : start + j + 8, :] = piece

            row = jnp.sum(columns[...].T, axis=0, keepdims=True)
            sums_out[pl.ds(slots[g * listed + k], 1), :] = row
            return carry

        lax.fori_loop(0, longest, one_entry, 0)


def column_pass(chunks, final, counts, slots, targets, level, parts, matrices, peaks):
    blocks, block_rows = level.shape
    n = len(chunks)
    vmem = pl.BlockSpec(memory_space=pltpu.VMEM)
    smem = pl.BlockSpec(memory_space=pltpu.SMEM)
    out_shape = [jax.ShapeDtypeStruct((targets, 128), jnp.float32)]
    if final:
        out_shape.append(jax.ShapeDtypeStruct((blocks, block_rows), jnp.float32))
    return pl.pallas_call(
        functools.partial(column_kernel, chunks, final),
        in_specs=[smem, smem] + [vmem] * (5 + 2 * n),
        out_specs=[vmem] * len(out_shape),
        out_shape=out_shape,
        scratch_shapes=[
            pltpu.VMEM((n,) + peaks[0].shape, jnp.float32),
            pltpu.VMEM((sum(chunks), 128), jnp.float32),
        ],
        compiler_params=pltpu.CompilerParams(vmem_limit_bytes=8 * MIB),
        name="columns",
    )(counts, slots, level, *parts, *matrices, *peaks)


def row_kernel(chunks, counts, slots, level, sums, *refs):
    n = len(chunks)
    matrices, peaks = refs[:n], refs[n : 2 * n]
    out, weights, gathered, spread = refs[2 * n :]
    blocks, block_rows = out.shape
    listed = matrices[0].shape[1]
    for e in range(2 * listed):
        gathered[e : e + 1, :] = sums[pl.ds(slots[e], 1), :]
    factors = (1.0 / (1.0 + gathered[...])).T
    for e in range(2 * listed):
        spread[e] = jnp.broadcast_to(factors[:, e : e + 1], (128, 128))
    for c in range(n):
        for s in range(blocks):
            weights[c, s] = jnp.exp2(peaks[c][s] - level[s : s + 1, :])
    lanes = block_rows // 128
    for s in range(blocks):
        g = s // SHARE

        def one_entry(k, total):
            for c, rows in enumerate(chunks):
                start = sum(chunks[:c])
                acc = [jnp.zeros((8, 128), jnp.float32) for _ in range(lanes)]
                for j in range(0, rows, 8):
                    v = spread[g * listed + k, start + j : start + j + 8, :]
                    for l in range(lanes):
                        acc[l] = acc[l] + matrices[c][s, k, j : j + 8, 128 * l : 128 * l + 128] * v
                w = weights[c, s, pl.ds(k, 1), :]
                total = tuple(t + a * w[:, 128 * l : 128 * l + 128] for l, (t, a) in enumerate(zip(total, acc)))
            return total

        total = lax.fori_loop(
            0, counts[s], one_entry, tuple(jnp.zeros((8, 128), jnp.float32) for _ in range(lanes))
        )
        out[s : s + 1, :] = jnp.concatenate([jnp.sum(t, axis=0, keepdims=True) for t in total], axis=1)


def row_pass(chunks, counts, slots, level, sums, matrices, peaks):
    blocks, block_rows = level.shape
    listed = matrices[0].shape[1]
    n = len(chunks)
    vmem = pl.BlockSpec(memory_space=pltpu.VMEM)
    smem = pl.BlockSpec(memory_space=pltpu.SMEM)
    return pl.pallas_call(
        functools.partial(row_kernel, chunks),
        in_specs=[smem, smem] + [vmem] * (2 + 2 * n),
        out_specs=vmem,
        out_shape=jax.ShapeDtypeStruct((blocks, block_rows), jnp.float32),
        scratch_shapes=[
            pltpu.VMEM((n,) + peaks[0].shape, jnp.float32),
            pltpu.VMEM((128, 128), jnp.float32),
            pltpu.VMEM((2 * listed, 128, 128), jnp.float32),
        ],
        compiler_params=pltpu.CompilerParams(vmem_limit_bytes=8 * MIB),
        name="rows",
    )(counts, slots, level, sums, *matrices, *peaks)


def from_columns(x):
    return [x] + [lax.ppermute(x, "col", [(i, (i + d) % 4) for i in range(4)]) for d in (1, 2, 3)]


def sum_over_rows(x):
    x = x + send(x, 0, 0, 1)
    x = x + send(x, 0, 1, 0) + send(x, 0, 2, 0) + send(x, 0, 3, 0)
    return x + send(x, 1, 0, 0) + send(x, 2, 0, 0) + send(x, 3, 0, 0)


def shards(source_vectors, target_vectors, pair_list, counts, owner_map):
    blocks = source_vectors.shape[0]
    target_blocks, quarter, _ = target_vectors.shape
    listed = pair_list.shape[1]
    targets = owner_map.shape[0]
    lead = pair_list.reshape(blocks // SHARE, SHARE, listed)[:, 0, :].reshape(-1)
    lookup = lead[:, None] == jnp.arange(targets, dtype=jnp.int32)[None, :]
    slots = jnp.sum(jnp.where(lookup, owner_map[None, :], 0), axis=1)
    me = lax.axis_index("row")
    z, y, core = me // 8, (me // 2) % 4, me % 2
    layout = np.array(piece_layout(), np.int32)
    owner = (((z + layout[:, 2]) % 4) * 4 + (y + layout[:, 3]) % 4) * 2 + (core ^ layout[:, 4])
    held_slot = owner * target_blocks + layout[:, 5]
    entry_ids = jnp.arange(2 * listed, dtype=jnp.int32)
    dest = jnp.max(jnp.where(held_slot[:, None] == slots[None, :], entry_ids[None, :], -1), axis=1)

    matrices, peaks, highs, totals = [], [], [], []
    start = 0
    for rows in CHUNKS:
        pieces = gather_plane(target_vectors[:, start : start + rows])
        start += rows
        matrix, peak, high, total = score_stage(rows, dest, counts, source_vectors, pieces, listed)
        matrices.append(matrix)
        peaks.append(peak)
        highs.append(high)
        totals.append(total)
    high = functools.reduce(jnp.maximum, highs)
    total = sum(t * jnp.exp2(h - high) for t, h in zip(totals, highs))
    both = from_columns(jnp.stack([high, total]))
    level = jnp.maximum(functools.reduce(jnp.maximum, [b[0] for b in both]), 0.0)
    parts = [b[1] * jnp.exp2(b[0] - level) for b in both]

    for sweep_index in range(SWEEPS):
        final = sweep_index == SWEEPS - 1
        sums = column_pass(
            CHUNKS, final, counts, slots, targets, level, parts, matrices, peaks
        )
        if final:
            break
        sums = sum_over_rows(sums[0])
        parts = from_columns(row_pass(CHUNKS, counts, slots, level, sums, matrices, peaks))
    sums, source_dual = sums
    row_count = targets // target_blocks
    back = lax.all_to_all(
        sums.reshape(row_count, target_blocks, quarter), "row", split_axis=0, concat_axis=0, tiled=True
    )
    target_dual = -EPSILON * jnp.log(1.0 + jnp.sum(back, axis=0))
    return source_dual, target_dual


def solution(mesh):
    return jax.shard_map(
        shards,
        mesh=mesh,
        in_specs=(P("row", None, None), P("row", "col", None), P("row", None), P("row"), P()),
        out_specs=(P("row", None), P("row", "col")),
        check_vma=False,
    )
```

time: 478 us -> 229 us (0.48)
  other arithmetic: 131 us -> 2.48 us
  blocking collectives: 87 us -> 15.9 us
  waiting for transfers between devices: 122 us -> 58.6 us
  Pallas kernels: 0 us -> 54.3 us
  matrix products: 33.9 us -> 0 us
  local copies, waits for them, and re-layouts: 46.1 us -> 14 us
  starting transfers between devices: 54.1 us -> 81.9 us
    all_to_all x9 -> x0, waiting for transfers between devices: 122 us -> none  [the longest x1 71.3 us: shards(): lax.all_to_all(served, 'row', split_axis=0, concat_axis=0, tiled=True)]
    ppermute x0 -> x75, starting transfers between devices: none -> 81.9 us  [the longest x66 74.1 us: send(): return lax.ppermute(x, 'row', row_perm(dz, dy, dc))]
    reduce_sum x15 -> x2, other arithmetic: 65.1 us -> 0.88 us  [the longest x1 0.83 us: shards(): slots = jnp.sum(jnp.where(lookup, owner_map[None, :], 0), axis=1)]
    reduce_max x12 -> x1, other arithmetic: 61.3 us -> 0.09 us  [shards(): jnp.max(jnp.where(held_slot[:, None] == slots[None, :], entry_ids[None, :...]
    ppermute x0 -> x75, waiting for transfers between devices: none -> 58.6 us  [the longest x66 47.3 us: send(): return lax.ppermute(x, 'row', row_perm(dz, dy, dc))]
    pallas_call x0 -> x7, Pallas kernels: none -> 54.3 us  [the longest x2 31.2 us: score_stage(): pl.pallas_call(make_score_kernel(rows), grid_spec=pltpu.PrefetchScalarGri...]
    all_gather x6 -> x0, blocking collectives: 54.2 us -> none  [combined_all(): gathered = jax.tree.map(lambda a: lax.all_gather(a, axis), part)]
    all_to_all x9 -> x0, starting transfers between devices: 54.1 us -> none  [the longest x1 14.5 us: shards(): lax.all_to_all(slot_highest.reshape(row_count, capacity, quarter), 'row',...]
  transfers between devices with their start and end apart: 9 -> 75, of which waited for: 9 -> 35; matrix products, arithmetic and copies ran while one was open for 1% -> 1% of each run, Pallas kernels for 0% -> 7%
where the time goes in v1:
time: 229 us; the launch traced here: 228 us
  starting transfers between devices  81.9 us (36%)
  waiting for transfers between devices  58.6 us (26%)
  Pallas kernels  54.3 us (24%)
  blocking collectives  15.9 us (7%)
  local copies, waits for them, and re-layouts  14 us (6%)
  other arithmetic  2.48 us (1%)
    ppermute x66, starting transfers between devices, send(): return lax.ppermute(x, 'row', row_perm(dz, dy, dc))  74.1 us
    ppermute x66, waiting for transfers between devices, send(): return lax.ppermute(x, 'row', row_perm(dz, dy, dc))  47.3 us
    pallas_call x2, Pallas kernels, score_stage(): pl.pallas_call(make_score_kernel(rows), grid_spec=pltpu.PrefetchScalarGri...  31.2 us
    pallas_call x3, Pallas kernels, column_pass(): pl.pallas_call(functools.partial(column_kernel, chunks, final), in_specs=...  16.3 us
    all_to_all x1, blocking collectives, shards(): lax.all_to_all(sums.reshape(row_count, target_blocks, quarter), 'row', sp...  15.9 us
    unnamed x56, local copies, waits for them, and re-layouts  12 us
    ppermute x9, waiting for transfers between devices, from_columns(): lax.ppermute(x, 'col', [(i, (i + d) % 4) for i in range(4)])  11.3 us
    ppermute x9, starting transfers between devices, from_columns(): lax.ppermute(x, 'col', [(i, (i + d) % 4) for i in range(4)])  7.83 us
  transfers between devices with their start and end apart: 75, of which 35 were waited for; matrix products, arithmetic and copies ran while one was open for 1% of the time, Pallas kernels for 7%

profile of v1, /device:TPU:1, one launch (start us, length us, event | category | flops | bytes accessed | tf_op | source)
XLA Modules:
  0.0 228.4 jit_solution(13076137032514962660)
XLA Ops:
  1.7 3.6 %collective-permute-start.27 = (bf16[1,64,768]{2,1,0:T(8,128)(2,1)S(1)}, bf16[1,64,768]{2,1,0:T(8,128)(2,1)S(1)}, u32[]{:S(2)}, u32[]{:S(2)}) collective-permute-start(bf16[1,64,768]{2,1,0:T(8,128)(2,1)S(1)} %get-tuple-element.29), channel_id=1, source_target_pairs={{0,24},{4,28},{8,0},{12,4},{16,8},{20,12},{24,16},{28,20},{32,56},... | collective-permute-start | bytes 294920 | tf_op jit(solution)/shard_map/ppermute | solution.py:32
  7.0 3.0 %collective-permute-start.29 = (bf16[1,32,768]{2,1,0:T(8,128)(2,1)S(1)}, bf16[1,32,768]{2,1,0:T(8,128)(2,1)S(1)}, u32[]{:S(2)}, u32[]{:S(2)}) collective-permute-start(bf16[1,32,768]{2,1,0:T(8,128)(2,1)S(1)} %slice.127), channel_id=1, source_target_pairs={{0,24},{4,28},{8,0},{12,4},{16,8},{20,12},{24,16},{28,20},{32,56},... | collective-permute-start | bytes 147464 | tf_op jit(solution)/shard_map/ppermute | solution.py:32
  10.1 3.8 %collective-permute-start.9 = (bf16[1,64,768]{2,1,0:T(8,128)(2,1)S(1)}, bf16[1,64,768]{2,1,0:T(8,128)(2,1)S(1)}, u32[]{:S(2)}, u32[]{:S(2)}) collective-permute-start(bf16[1,64,768]{2,1,0:T(8,128)(2,1)S(1)} %get-tuple-element.26), channel_id=1, source_target_pairs={{0,96},{4,100},{8,104},{12,108},{16,112},{20,116},{24,120},{28,124... | collective-permute-start | bytes 294920 | tf_op jit(solution)/shard_map/ppermute | solution.py:32
  14.3 3.3 %collective-permute-start.42 = (bf16[4,64,768]{2,1,0:T(8,128)(2,1)S(1)}, bf16[4,64,768]{2,1,0:T(8,128)(2,1)S(1)}, u32[]{:S(2)}, u32[]{:S(2)}) collective-permute-start(bf16[4,64,768]{2,1,0:T(8,128)(2,1)S(1)} %maximum_maximum_fusion.2.refs_0_), channel_id=1, source_target_pairs={{0,4},{4,0},{8,12},{12,8},{16,20},{20,16},{24,28},{28,24},{32,36},... | collective-permute-start | bytes 1179656 | tf_op jit(solution)/shard_map/ppermute | solution.py:32
  29.3 5.9 %collective-permute-done.11 = bf16[1,32,768]{2,1,0:T(8,128)(2,1)S(1)} collective-permute-done((bf16[1,32,768]{2,1,0:T(8,128)(2,1)S(1)}, bf16[1,32,768]{2,1,0:T(8,128)(2,1)S(1)}, u32[]{:S(2)}, u32[]{:S(2)}) %collective-permute-start.11) | collective-permute-done | bytes 49184 | tf_op jit(solution)/shard_map/ppermute | solution.py:32
  39.4 3.5 %collective-permute-start.47 = (bf16[4,64,768]{2,1,0:T(8,128)(2,1)S(1)}, bf16[4,64,768]{2,1,0:T(8,128)(2,1)S(1)}, u32[]{:S(2)}, u32[]{:S(2)}) collective-permute-start(bf16[4,64,768]{2,1,0:T(8,128)(2,1)S(1)} %maximum_maximum_fusion.3.refs_5_), channel_id=1, source_target_pairs={{0,4},{4,0},{8,12},{12,8},{16,20},{20,16},{24,28},{28,24},{32,36},... | collective-permute-start | bytes 1179656 | tf_op jit(solution)/shard_map/ppermute | solution.py:32
  50.0 2.8 %collective-permute-done.39.refs_7_ = bf16[4,64,768]{2,1,0:T(8,128)(2,1)S(1)} collective-permute-done((bf16[4,64,768]{2,1,0:T(8,128)(2,1)S(1)}, bf16[4,64,768]{2,1,0:T(8,128)(2,1)S(1)}, u32[]{:S(2)}, u32[]{:S(2)}) %collective-permute-start.39) | collective-permute-done | bytes 393248 | tf_op jit(solution)/shard_map/ppermute | solution.py:32
  62.4 3.8 %collective-permute-done.13.refs_7_ = bf16[4,64,768]{2,1,0:T(8,128)(2,1)S(1)} collective-permute-done((bf16[4,64,768]{2,1,0:T(8,128)(2,1)S(1)}, bf16[4,64,768]{2,1,0:T(8,128)(2,1)S(1)}, u32[]{:S(2)}, u32[]{:S(2)}) %collective-permute-start.13) | collective-permute-done | bytes 393248 | tf_op jit(solution)/shard_map/ppermute | solution.py:32
  72.7 3.0 %collective-permute-start.15 = (bf16[2,64,768]{2,1,0:T(8,128)(2,1)S(1)}, bf16[2,64,768]{2,1,0:T(8,128)(2,1)S(1)}, u32[]{:S(2)}, u32[]{:S(2)}) collective-permute-start(bf16[2,64,768]{2,1,0:T(8,128)(2,1)S(1)} %slice.125), channel_id=1, source_target_pairs={{0,24},{4,28},{8,0},{12,4},{16,8},{20,12},{24,16},{28,20},{32,56},... | collective-permute-start | bytes 589832 | tf_op jit(solution)/shard_map/ppermute | solution.py:32
  76.8 3.6 %collective-permute-done.6.refs_3_ = bf16[2,64,768]{2,1,0:T(8,128)(2,1)S(1)} collective-permute-done((bf16[2,64,768]{2,1,0:T(8,128)(2,1)S(1)}, bf16[2,64,768]{2,1,0:T(8,128)(2,1)S(1)}, u32[]{:S(2)}, u32[]{:S(2)}) %collective-permute-start.6) | collective-permute-done | bytes 196640 | tf_op jit(solution)/shard_map/ppermute | solution.py:32
  95.1 2.8 %copy-done.8 = bf16[8,512,768]{2,1,0:T(8,128)(2,1)S(1)} copy-done((bf16[8,512,768]{2,1,0:T(8,128)(2,1)S(1)}, bf16[8,512,768]{2,1,0:T(8,128)(2,1)}, u32[]{:S(2)}) %copy-start.8) | copy-done | bytes 6291480
  102.6 15.7 %scores.2 = (f32[8,12,64,512]{3,2,1,0:T(8,128)S(1)}, f32[8,16,512]{2,1,0:T(8,128)S(1)}, f32[8,512]{1,0:T(8,128)S(1)}, f32[8,512]{1,0:T(8,128)S(1)}) custom-call(s32[64]{0:T(128)S(1)} %select_reduce_fusion.dest, s32[8]{0:T(128)S(1)} %copy-done.6, bf16[8,512,768]{2,1,0:T(8,128)(2,1)S(1)} %copy-done.8, bf16[4,64,768]{2,1,0:T(8,128)(2,1)S(1)} %maximum_maximum_fusion.refs_0_, ...), custom_call_target="tpu_custom_call" | custom-call | flops 4831838208 | bytes 12582912 | tf_op jit(solution)/shard_map/scores/pallas_call | solution.py:153
  118.4 15.5 %scores.3 = (f32[8,12,64,512]{3,2,1,0:T(8,128)S(1)}, f32[8,16,512]{2,1,0:T(8,128)S(1)}, f32[8,512]{1,0:T(8,128)S(1)}, f32[8,512]{1,0:T(8,128)S(1)}) custom-call(s32[64]{0:T(128)S(1)} %select_reduce_fusion.dest, s32[8]{0:T(128)S(1)} %copy-done.7, bf16[8,512,768]{2,1,0:T(8,128)(2,1)S(1)} %copy-done.9, bf16[4,64,768]{2,1,0:T(8,128)(2,1)S(1)} %maximum_maximum_fusion.2.refs_0_, ...), custom_call_target="tpu_custom_call" | custom-call | flops 4831838208 | bytes 12582912 | tf_op jit(solution)/shard_map/scores/pallas_call | solution.py:153
  137.7 3.8 %collective-permute-done.53 = f32[2,8,512]{2,1,0:T(8,128)S(1)} collective-permute-done((f32[2,8,512]{2,1,0:T(8,128)S(1)}, f32[2,8,512]{2,1,0:T(8,128)S(1)}, u32[]{:S(2)}, u32[]{:S(2)}) %collective-permute-start.53) | collective-permute-done | bytes 32800 | tf_op jit(solution)/shard_map/ppermute | solution.py:315
  142.2 5.2 %columns.3 = f32[64,128]{1,0:T(8,128)S(1)} custom-call(s32[8]{0:T(128)S(1)} %copy-done.7, s32[24]{0:T(128)S(1)} %select_reduce_fusion.1.slots, f32[8,512]{1,0:T(8,128)S(1)} %get-tuple-element.23.level, f32[8,512]{1,0:T(8,128)S(1)} %get-tuple-element.32.part, f32[8,512]{1,0:T(8,128)S(1)} %get-tuple-element.31.near, f32[8,512]{1,0:T(8,128)S(1)} %get-tuple-element.30.far, ...), custom_call_target="tpu_custom_call" | custom-call | tf_op jit(solution)/shard_map/columns/pallas_call | solution.py:243
  154.5 5.0 %collective-permute-start.61 = (f32[64,128]{1,0:T(8,128)S(1)}, f32[64,128]{1,0:T(8,128)S(1)}, u32[]{:S(2)}, u32[]{:S(2)}) collective-permute-start(f32[64,128]{1,0:T(8,128)S(1)} %add_add_fusion.3), channel_id=1, source_target_pairs={{0,96},{4,100},{8,104},{12,108},{16,112},{20,116},{24,120},{28,124... | collective-permute-start | bytes 98312 | tf_op jit(solution)/shard_map/ppermute | solution.py:32
  166.1 3.4 %rows.2.part = f32[8,512]{1,0:T(8,128)S(1)} custom-call(s32[8]{0:T(128)S(1)} %copy-done.7, s32[24]{0:T(128)S(1)} %select_reduce_fusion.1.slots, f32[8,512]{1,0:T(8,128)S(1)} %get-tuple-element.23.level, f32[64,128]{1,0:T(8,128)S(1)} %add_add_fusion.2.sums, f32[8,12,64,512]{3,2,1,0:T(8,128)S(1)} %get-tuple-element.16.refs_0_, ...), custom_call_target="tpu_custom_call" | custom-call | tf_op jit(solution)/shard_map/rows/pallas_call | solution.py:299
  174.6 5.2 %columns.4 = f32[64,128]{1,0:T(8,128)S(1)} custom-call(s32[8]{0:T(128)S(1)} %copy-done.7, s32[24]{0:T(128)S(1)} %select_reduce_fusion.1.slots, f32[8,512]{1,0:T(8,128)S(1)} %get-tuple-element.23.level, f32[8,512]{1,0:T(8,128)S(1)} %rows.2.part, f32[8,512]{1,0:T(8,128)S(1)} %collective-permute-done.62.near, f32[8,512]{1,0:T(8,128)S(1)} %collective-permute-done.63.far, ...), custom_call_target="tpu_custom_call" | custom-call | tf_op jit(solution)/shard_map/columns/pallas_call | solution.py:243
  179.8 4.1 %collective-permute-start.65 = (f32[64,128]{1,0:T(8,128)S(1)}, f32[64,128]{1,0:T(8,128)S(1)}, u32[]{:S(2)}, u32[]{:S(2)}) collective-permute-start(f32[64,128]{1,0:T(8,128)S(1)} %columns.4), channel_id=1, source_target_pairs={{0,4},{4,0},{8,12},{12,8},{16,20},{20,16},{24,28},{28,24},{32,36},... | collective-permute-start | bytes 98312 | tf_op jit(solution)/shard_map/ppermute | solution.py:32
  187.5 3.3 %collective-permute-done.67 = f32[64,128]{1,0:T(8,128)S(1)} collective-permute-done((f32[64,128]{1,0:T(8,128)S(1)}, f32[64,128]{1,0:T(8,128)S(1)}, u32[]{:S(2)}, u32[]{:S(2)}) %collective-permute-start.67) | collective-permute-done | bytes 32800 | tf_op jit(solution)/shard_map/ppermute | solution.py:32
  196.7 3.4 %rows.3.part = f32[8,512]{1,0:T(8,128)S(1)} custom-call(s32[8]{0:T(128)S(1)} %copy-done.7, s32[24]{0:T(128)S(1)} %select_reduce_fusion.1.slots, f32[8,512]{1,0:T(8,128)S(1)} %get-tuple-element.23.level, f32[64,128]{1,0:T(8,128)S(1)} %add_add_fusion.sums, f32[8,12,64,512]{3,2,1,0:T(8,128)S(1)} %get-tuple-element.16.refs_0_, ...), custom_call_target="tpu_custom_call" | custom-call | tf_op jit(solution)/shard_map/rows/pallas_call | solution.py:299
  202.7 3.0 %collective-permute-done.73.far = f32[8,512]{1,0:T(8,128)S(1)} collective-permute-done((f32[8,512]{1,0:T(8,128)S(1)}, f32[8,512]{1,0:T(8,128)S(1)}, u32[]{:S(2)}, u32[]{:S(2)}) %collective-permute-start.73) | collective-permute-done | bytes 16416 | tf_op jit(solution)/shard_map/ppermute | solution.py:315
  206.1 5.8 %columns.5 = (f32[64,128]{1,0:T(8,128)S(1)}, f32[8,512]{1,0:T(8,128)}) custom-call(s32[8]{0:T(128)S(1)} %copy-done.7, s32[24]{0:T(128)S(1)} %select_reduce_fusion.1.slots, f32[8,512]{1,0:T(8,128)S(1)} %get-tuple-element.23.level, f32[8,512]{1,0:T(8,128)S(1)} %rows.3.part, f32[8,512]{1,0:T(8,128)S(1)} %collective-permute-done.72.near, ...), custom_call_target="tpu_custom_call" | custom-call | tf_op jit(solution)/shard_map/columns/pallas_call | solution.py:243
  211.9 15.9 %all_to_all.5 = f32[32,2,128]{2,1,0:T(2,128)S(1)} all-to-all(f32[32,2,128]{2,1,0:T(2,128)S(1)} %bitcast.37), channel_id=1, replica_groups=mesh['row'=32,'col'=4] {'row'}, dimensions={0} | all-to-all | bytes 65536 | tf_op jit(solution)/shard_map/all_to_all | solution.py:367
  (228 shorter events, 98.7 us)
Async XLA Ops:
  10.1 10.8 %collective-permute-start.9 = (bf16[1,64,768]{2,1,0:T(8,128)(2,1)S(1)}, bf16[1,64,768]{2,1,0:T(8,128)(2,1)S(1)}, u32[]{:S(2)}, u32[]{:S(2)}) collective-permute-start(bf16[1,64,768]{2,1,0:T(8,128)(2,1)S(1)} %get-tuple-element.26), channel_id=1, source_target_pairs={{0,96},{4,100},{8,104},{12,108},{16,112},{20,116},{24,120},{28,124... | collective-permute-start | bytes 294920 | tf_op jit(solution)/shard_map/ppermute | solution.py:32
  14.3 30.0 %collective-permute-start.42 = (bf16[4,64,768]{2,1,0:T(8,128)(2,1)S(1)}, bf16[4,64,768]{2,1,0:T(8,128)(2,1)S(1)}, u32[]{:S(2)}, u32[]{:S(2)}) collective-permute-start(bf16[4,64,768]{2,1,0:T(8,128)(2,1)S(1)} %maximum_maximum_fusion.2.refs_0_), channel_id=1, source_target_pairs={{0,4},{4,0},{8,12},{12,8},{16,20},{20,16},{24,28},{28,24},{32,36},... | collective-permute-start | bytes 1179656 | tf_op jit(solution)/shard_map/ppermute | solution.py:32
  24.5 20.7 %collective-permute-start.31 = (bf16[4,64,768]{2,1,0:T(8,128)(2,1)S(1)}, bf16[4,64,768]{2,1,0:T(8,128)(2,1)S(1)}, u32[]{:S(2)}, u32[]{:S(2)}) collective-permute-start(bf16[4,64,768]{2,1,0:T(8,128)(2,1)S(1)} %maximum_maximum_fusion.2.refs_0_), channel_id=1, source_target_pairs={{0,96},{4,100},{8,104},{12,108},{16,112},{20,116},{24,120},{28,124... | collective-permute-start | bytes 1179656 | tf_op jit(solution)/shard_map/ppermute | solution.py:32
  26.6 8.6 %collective-permute-start.11 = (bf16[1,32,768]{2,1,0:T(8,128)(2,1)S(1)}, bf16[1,32,768]{2,1,0:T(8,128)(2,1)S(1)}, u32[]{:S(2)}, u32[]{:S(2)}) collective-permute-start(bf16[1,32,768]{2,1,0:T(8,128)(2,1)S(1)} %slice.123), channel_id=1, source_target_pairs={{0,96},{4,100},{8,104},{12,108},{16,112},{20,116},{24,120},{28,124... | collective-permute-start | bytes 147464 | tf_op jit(solution)/shard_map/ppermute | solution.py:32
  28.0 8.7 %collective-permute-start.36 = (bf16[1,32,768]{2,1,0:T(8,128)(2,1)S(1)}, bf16[1,32,768]{2,1,0:T(8,128)(2,1)S(1)}, u32[]{:S(2)}, u32[]{:S(2)}) collective-permute-start(bf16[1,32,768]{2,1,0:T(8,128)(2,1)S(1)} %slice.130), channel_id=1, source_target_pairs={{0,32},{4,36},{8,40},{12,44},{16,48},{20,52},{24,56},{28,60},{32,6... | collective-permute-start | bytes 147464 | tf_op jit(solution)/shard_map/ppermute | solution.py:32
  39.4 10.6 %collective-permute-start.47 = (bf16[4,64,768]{2,1,0:T(8,128)(2,1)S(1)}, bf16[4,64,768]{2,1,0:T(8,128)(2,1)S(1)}, u32[]{:S(2)}, u32[]{:S(2)}) collective-permute-start(bf16[4,64,768]{2,1,0:T(8,128)(2,1)S(1)} %maximum_maximum_fusion.3.refs_5_), channel_id=1, source_target_pairs={{0,4},{4,0},{8,12},{12,8},{16,20},{20,16},{24,28},{28,24},{32,36},... | collective-permute-start | bytes 1179656 | tf_op jit(solution)/shard_map/ppermute | solution.py:32
  42.9 9.9 %collective-permute-start.39 = (bf16[4,64,768]{2,1,0:T(8,128)(2,1)S(1)}, bf16[4,64,768]{2,1,0:T(8,128)(2,1)S(1)}, u32[]{:S(2)}, u32[]{:S(2)}) collective-permute-start(bf16[4,64,768]{2,1,0:T(8,128)(2,1)S(1)} %maximum_maximum_fusion.3.refs_5_), channel_id=1, source_target_pairs={{0,24},{4,28},{8,0},{12,4},{16,8},{20,12},{24,16},{28,20},{32,56},... | collective-permute-start | bytes 1179656 | tf_op jit(solution)/shard_map/ppermute | solution.py:32
  45.0 11.6 %collective-permute-start.38 = (bf16[4,64,768]{2,1,0:T(8,128)(2,1)S(1)}, bf16[4,64,768]{2,1,0:T(8,128)(2,1)S(1)}, u32[]{:S(2)}, u32[]{:S(2)}) collective-permute-start(bf16[4,64,768]{2,1,0:T(8,128)(2,1)S(1)} %maximum_maximum_fusion.3.refs_5_), channel_id=1, source_target_pairs={{0,8},{4,12},{8,16},{12,20},{16,24},{20,28},{24,0},{28,4},{32,40},... | collective-permute-start | bytes 1179656 | tf_op jit(solution)/shard_map/ppermute | solution.py:32
  45.2 11.8 %collective-permute-start.16 = (bf16[4,64,768]{2,1,0:T(8,128)(2,1)S(1)}, bf16[4,64,768]{2,1,0:T(8,128)(2,1)S(1)}, u32[]{:S(2)}, u32[]{:S(2)}) collective-permute-start(bf16[4,64,768]{2,1,0:T(8,128)(2,1)S(1)} %maximum_maximum_fusion.refs_0_), channel_id=1, source_target_pairs={{0,4},{4,0},{8,12},{12,8},{16,20},{20,16},{24,28},{28,24},{32,36},... | collective-permute-start | bytes 1179656 | tf_op jit(solution)/shard_map/ppermute | solution.py:32
  47.7 10.5 %collective-permute-start.5 = (bf16[4,64,768]{2,1,0:T(8,128)(2,1)S(1)}, bf16[4,64,768]{2,1,0:T(8,128)(2,1)S(1)}, u32[]{:S(2)}, u32[]{:S(2)}) collective-permute-start(bf16[4,64,768]{2,1,0:T(8,128)(2,1)S(1)} %maximum_maximum_fusion.refs_0_), channel_id=1, source_target_pairs={{0,96},{4,100},{8,104},{12,108},{16,112},{20,116},{24,120},{28,124... | collective-permute-start | bytes 1179656 | tf_op jit(solution)/shard_map/ppermute | solution.py:32
  50.0 10.6 %collective-permute-start.4 = (bf16[4,64,768]{2,1,0:T(8,128)(2,1)S(1)}, bf16[4,64,768]{2,1,0:T(8,128)(2,1)S(1)}, u32[]{:S(2)}, u32[]{:S(2)}) collective-permute-start(bf16[4,64,768]{2,1,0:T(8,128)(2,1)S(1)} %maximum_maximum_fusion.refs_0_), channel_id=1, source_target_pairs={{0,32},{4,36},{8,40},{12,44},{16,48},{20,52},{24,56},{28,60},{32,6... | collective-permute-start | bytes 1179656 | tf_op jit(solution)/shard_map/ppermute | solution.py:32
  56.6 9.5 %collective-permute-start.13 = (bf16[4,64,768]{2,1,0:T(8,128)(2,1)S(1)}, bf16[4,64,768]{2,1,0:T(8,128)(2,1)S(1)}, u32[]{:S(2)}, u32[]{:S(2)}) collective-permute-start(bf16[4,64,768]{2,1,0:T(8,128)(2,1)S(1)} %maximum_maximum_fusion.1.refs_5_), channel_id=1, source_target_pairs={{0,24},{4,28},{8,0},{12,4},{16,8},{20,12},{24,16},{28,20},{32,56},... | collective-permute-start | bytes 1179656 | tf_op jit(solution)/shard_map/ppermute | solution.py:32
  57.0 11.1 %collective-permute-start.12 = (bf16[4,64,768]{2,1,0:T(8,128)(2,1)S(1)}, bf16[4,64,768]{2,1,0:T(8,128)(2,1)S(1)}, u32[]{:S(2)}, u32[]{:S(2)}) collective-permute-start(bf16[4,64,768]{2,1,0:T(8,128)(2,1)S(1)} %maximum_maximum_fusion.1.refs_5_), channel_id=1, source_target_pairs={{0,8},{4,12},{8,16},{12,20},{16,24},{20,28},{24,0},{28,4},{32,40},... | collective-permute-start | bytes 1179656 | tf_op jit(solution)/shard_map/ppermute | solution.py:32
  58.2 12.2 %collective-permute-start.33 = (bf16[2,64,768]{2,1,0:T(8,128)(2,1)S(1)}, bf16[2,64,768]{2,1,0:T(8,128)(2,1)}, u32[]{:S(2)}, u32[]{:S(2)}) collective-permute-start(bf16[2,64,768]{2,1,0:T(8,128)(2,1)S(1)} %slice.129), channel_id=1, source_target_pairs={{0,96},{4,100},{8,104},{12,108},{16,112},{20,116},{24,120},{28,124... | collective-permute-start | bytes 589832 | tf_op jit(solution)/shard_map/ppermute | solution.py:32
  60.6 12.1 %collective-permute-start.32 = (bf16[2,64,768]{2,1,0:T(8,128)(2,1)S(1)}, bf16[2,64,768]{2,1,0:T(8,128)(2,1)}, u32[]{:S(2)}, u32[]{:S(2)}) collective-permute-start(bf16[2,64,768]{2,1,0:T(8,128)(2,1)S(1)} %slice.128), channel_id=1, source_target_pairs={{0,32},{4,36},{8,40},{12,44},{16,48},{20,52},{24,56},{28,60},{32,6... | collective-permute-start | bytes 589832 | tf_op jit(solution)/shard_map/ppermute | solution.py:32
  60.6 12.0 %collective-permute-start.41 = (bf16[2,64,768]{2,1,0:T(8,128)(2,1)S(1)}, bf16[2,64,768]{2,1,0:T(8,128)(2,1)S(1)}, u32[]{:S(2)}, u32[]{:S(2)}) collective-permute-start(bf16[2,64,768]{2,1,0:T(8,128)(2,1)S(1)} %slice.133), channel_id=1, source_target_pairs={{0,24},{4,28},{8,0},{12,4},{16,8},{20,12},{24,16},{28,20},{32,56},... | collective-permute-start | bytes 589832 | tf_op jit(solution)/shard_map/ppermute | solution.py:32
  66.1 9.6 %collective-permute-start.40 = (bf16[2,64,768]{2,1,0:T(8,128)(2,1)S(1)}, bf16[2,64,768]{2,1,0:T(8,128)(2,1)S(1)}, u32[]{:S(2)}, u32[]{:S(2)}) collective-permute-start(bf16[2,64,768]{2,1,0:T(8,128)(2,1)S(1)} %slice.132), channel_id=1, source_target_pairs={{0,8},{4,12},{8,16},{12,20},{16,24},{20,28},{24,0},{28,4},{32,40},... | collective-permute-start | bytes 589832 | tf_op jit(solution)/shard_map/ppermute | solution.py:32
  70.4 15.5 %collective-permute-start.44 = (bf16[4,64,768]{2,1,0:T(8,128)(2,1)S(1)}, bf16[4,64,768]{2,1,0:T(8,128)(2,1)}, u32[]{:S(2)}, u32[]{:S(2)}) collective-permute-start(bf16[4,64,768]{2,1,0:T(8,128)(2,1)S(1)} %collective-permute-done.31.refs_2_), channel_id=1, source_target_pairs={{0,4},{4,0},{8,12},{12,8},{16,20},{20,16},{24,28},{28,24},{32,36},... | collective-permute-start | bytes 1179656 | tf_op jit(solution)/shard_map/ppermute | solution.py:32
  75.9 9.4 %collective-permute-start.46 = (bf16[2,64,768]{2,1,0:T(8,128)(2,1)}, bf16[2,64,768]{2,1,0:T(8,128)(2,1)}, u32[]{:S(2)}, u32[]{:S(2)}) collective-permute-start(bf16[2,64,768]{2,1,0:T(8,128)(2,1)} %collective-permute-done.33.refs_4_), channel_id=1, source_target_pairs={{0,4},{4,0},{8,12},{12,8},{16,20},{20,16},{24,28},{28,24},{32,36},... | collective-permute-start | bytes 589832 | tf_op jit(solution)/shard_map/ppermute | solution.py:32
  90.2 28.2 %collective-permute-start.43 = (bf16[4,64,768]{2,1,0:T(8,128)(2,1)S(1)}, bf16[4,64,768]{2,1,0:T(8,128)(2,1)S(1)}, u32[]{:S(2)}, u32[]{:S(2)}) collective-permute-start(bf16[4,64,768]{2,1,0:T(8,128)(2,1)S(1)} %collective-permute-done.30.refs_1_), channel_id=1, source_target_pairs={{0,4},{4,0},{8,12},{12,8},{16,20},{20,16},{24,28},{28,24},{32,36},... | collective-permute-start | bytes 1179656 | tf_op jit(solution)/shard_map/ppermute | solution.py:32
  90.4 28.0 %collective-permute-start.49 = (bf16[4,64,768]{2,1,0:T(8,128)(2,1)S(1)}, bf16[4,64,768]{2,1,0:T(8,128)(2,1)S(1)}, u32[]{:S(2)}, u32[]{:S(2)}) collective-permute-start(bf16[4,64,768]{2,1,0:T(8,128)(2,1)S(1)} %collective-permute-done.39.refs_7_), channel_id=1, source_target_pairs={{0,4},{4,0},{8,12},{12,8},{16,20},{20,16},{24,28},{28,24},{32,36},... | collective-permute-start | bytes 1179656 | tf_op jit(solution)/shard_map/ppermute | solution.py:32
  90.8 27.6 %collective-permute-start.48 = (bf16[4,64,768]{2,1,0:T(8,128)(2,1)S(1)}, bf16[4,64,768]{2,1,0:T(8,128)(2,1)S(1)}, u32[]{:S(2)}, u32[]{:S(2)}) collective-permute-start(bf16[4,64,768]{2,1,0:T(8,128)(2,1)S(1)} %collective-permute-done.38.refs_6_), channel_id=1, source_target_pairs={{0,4},{4,0},{8,12},{12,8},{16,20},{20,16},{24,28},{28,24},{32,36},... | collective-permute-start | bytes 1179656 | tf_op jit(solution)/shard_map/ppermute | solution.py:32
  90.9 27.4 %collective-permute-start.51 = (bf16[2,64,768]{2,1,0:T(8,128)(2,1)}, bf16[2,64,768]{2,1,0:T(8,128)(2,1)S(1)}, u32[]{:S(2)}, u32[]{:S(2)}) collective-permute-start(bf16[2,64,768]{2,1,0:T(8,128)(2,1)} %copy-done.18), channel_id=1, source_target_pairs={{0,4},{4,0},{8,12},{12,8},{16,20},{20,16},{24,28},{28,24},{32,36},... | collective-permute-start | bytes 589832 | tf_op jit(solution)/shard_map/ppermute | solution.py:32
  91.3 27.1 %collective-permute-start.50 = (bf16[2,64,768]{2,1,0:T(8,128)(2,1)}, bf16[2,64,768]{2,1,0:T(8,128)(2,1)S(1)}, u32[]{:S(2)}, u32[]{:S(2)}) collective-permute-start(bf16[2,64,768]{2,1,0:T(8,128)(2,1)} %copy-done.20), channel_id=1, source_target_pairs={{0,4},{4,0},{8,12},{12,8},{16,20},{20,16},{24,28},{28,24},{32,36},... | collective-permute-start | bytes 589832 | tf_op jit(solution)/shard_map/ppermute | solution.py:32
  (79 other events, 630.6 us)

commit v2 on v1

v2 whole, which is shorter than its diff:
```python
import functools

import jax
import jax.numpy as jnp
import numpy as np
from jax import lax
from jax.experimental import pallas as pl
from jax.experimental.pallas import tpu as pltpu
from jax.sharding import PartitionSpec as P

SHARE = 4
SWEEPS = 3
EPSILON = 0.05
LOG2E = 1.4426950408889634
LN2 = 0.6931471805599453
SCALE = LOG2E / EPSILON
NEGATIVE = -1e30
MIB = 2**20


def row_perm(dz, dy, dc):
    return [
        ((z * 4 + y) * 2 + c, (((z + dz) % 4) * 4 + (y + dy) % 4) * 2 + (c ^ dc))
        for z in range(4)
        for y in range(4)
        for c in range(2)
    ]


def send(x, dz, dy, dc):
    return lax.ppermute(x, "row", row_perm(dz, dy, dc))


RING = (0, -1, 1, 2)
STAGES = 3


def tie(*arrays):
    return lax.optimization_barrier(arrays)


def ring_gather(own, dz, dy):
    parts = [own, send(own, dz, dy, 0), send(own, -dz, -dy, 0), send(own, 2 * dz, 2 * dy, 0)]
    return jnp.concatenate(parts, axis=0)


def piece_layout():
    first = [(core, which, 0, RING) for core in range(2) for which in range(2)]
    second = [(core, which, d, RING) for core in range(2) for which in range(2) for d in (-1, 1)]
    third = [
        (core, which, 2, half) for core in range(2) for which in range(2) for half in (RING[:2], RING[2:])
    ]
    stages = []
    for pieces in (first, second, third):
        entries = []
        for piece, (core, which, across, ring) in enumerate(pieces):
            for index, along in enumerate(ring):
                dz, dy = (across, along) if which == 0 else (along, across)
                entries.append((piece, index, dz, dy, core, which))
        stages.append(entries)
    return stages


def score_kernel(stage, listed, dest, segments, lives, source, *refs):
    layout = piece_layout()[stage]
    number = max(entry[0] for entry in layout) + 1
    pieces, refs = refs[:number], refs[number:]
    if stage > 0:
        (_, peak_in, sum_in), refs = refs[:3], refs[3:]
    matrix, peak_out, sum_out = refs[:3]
    if stage == STAGES - 1:
        high_out, total_out = refs[3:5]
    held, raised, tally, fetch_sems, store_sems = refs[-5:]
    step = pl.program_id(0)
    group = step // SHARE
    rows = held.shape[0] // (2 * listed + 4)
    buffers = raised.shape[0]

    def fetch(piece, index, entry):
        return pltpu.make_async_copy(
            pieces[piece].at[index], held.at[pl.ds(entry * rows, rows)], fetch_sems.at[entry]
        )

    def store(buffer, entry):
        return pltpu.make_async_copy(raised.at[buffer], matrix.at[step, entry], store_sems.at[buffer])

    @pl.when(step == 0)
    def _():
        tally[0] = 0
        for position, (piece, index, *_) in enumerate(layout):

            @pl.when(dest[position] >= 0)
            def _():
                fetch(piece, index, dest[position]).start()

    for g in range(2):

        @pl.when(step == SHARE * g)
        def _():
            def arrive(entry, carry):
                fetch(0, 0, g * listed + entry).wait()
                return carry

            lax.fori_loop(segments[g * (STAGES + 1) + stage], segments[g * (STAGES + 1) + stage + 1], arrive, 0)

    if stage > 0:
        peak_out[...] = peak_in[...]
        sum_out[...] = sum_in[...]
    else:
        peak_out[...] = jnp.full(peak_out.shape, NEGATIVE, jnp.float32)
        sum_out[...] = jnp.zeros(sum_out.shape, jnp.float32)
    begin = segments[group * (STAGES + 1) + stage]
    live = lives[step * STAGES + stage]

    def batch(first, size, spare):
        base = pl.multiple_of((group * listed + begin + first) * rows, rows)
        scores = lax.dot_general(
            held[pl.ds(base, size * rows), :],
            source[0],
            (((1,), (1,)), ((), ())),
            preferred_element_type=jnp.float32,
        )

        def finish(p):
            count = tally[0] + first + p
            buffer = lax.rem(count, buffers)

            @pl.when(count >= buffers)
            def _():
                store(buffer, 0).wait()

            one = scores[p * rows : (p + 1) * rows] * SCALE
            peak = jnp.max(one, axis=0, keepdims=True)
            lifted = jnp.exp2(one - peak)
            raised[buffer] = lifted
            peak_out[0, pl.ds(begin + first + p, 1), :] = peak
            sum_out[0, pl.ds(begin + first + p, 1), :] = jnp.sum(lifted, axis=0, keepdims=True)
            store(buffer, begin + first + p).start()

        for p in range(size):
            if p < size - spare:
                finish(p)
            else:
                pl.when(first + p < live)(functools.partial(finish, p))

    def four(q, carry):
        batch(4 * q, 4, 0)
        return carry

    def two(q, carry):
        batch(4 * (live // 4) + 2 * q, 2, 1)
        return carry

    lax.fori_loop(0, live // 4, four, 0)
    lax.fori_loop(0, (live % 4 + 1) // 2, two, 0)
    tally[0] = tally[0] + live

    @pl.when(step == pl.num_programs(0) - 1)
    def _():
        for buffer in range(buffers):

            @pl.when(tally[0] > buffer)
            def _():
                store(buffer, 0).wait()

    if stage == STAGES - 1:
        high = jnp.max(peak_out[0], axis=0, keepdims=True)
        high_out[pl.ds(step, 1), :] = high
        total_out[pl.ds(step, 1), :] = jnp.sum(
            sum_out[0] * jnp.exp2(peak_out[0] - high), axis=0, keepdims=True
        )


def score_stage(stage, listed, dest, segments, lives, source_vectors, pieces, earlier):
    blocks, block_rows, width = source_vectors.shape
    rows = pieces[0].shape[1]
    padded = 16
    hbm = pl.BlockSpec(memory_space=pltpu.HBM)
    small = pl.BlockSpec((1, padded, block_rows), lambda s, *_: (s, 0, 0))
    whole = pl.BlockSpec((blocks, block_rows), lambda s, *_: (0, 0))
    last = stage == STAGES - 1
    share = (0.25, 0.5, 0.25)[stage]
    return pl.pallas_call(
        functools.partial(score_kernel, stage, listed),
        grid_spec=pltpu.PrefetchScalarGridSpec(
            num_scalar_prefetch=3,
            grid=(blocks,),
            in_specs=[pl.BlockSpec((1, block_rows, width), lambda s, *_: (s, 0, 0))]
            + [hbm] * len(pieces)
            + [hbm, small, small][: len(earlier)],
            out_specs=[hbm, small, small] + [whole, whole] * last,
            scratch_shapes=[
                pltpu.VMEM(((2 * listed + 4) * rows, width), jnp.bfloat16),
                pltpu.VMEM((8, rows, block_rows), jnp.float32),
                pltpu.SMEM((1,), jnp.int32),
                pltpu.SemaphoreType.DMA((2 * listed,)),
                pltpu.SemaphoreType.DMA((8,)),
            ],
        ),
        out_shape=[
            jax.ShapeDtypeStruct((blocks, listed, rows, block_rows), jnp.float32),
            jax.ShapeDtypeStruct((blocks, padded, block_rows), jnp.float32),
            jax.ShapeDtypeStruct((blocks, padded, block_rows), jnp.float32),
        ]
        + [jax.ShapeDtypeStruct((blocks, block_rows), jnp.float32)] * 2 * last,
        input_output_aliases={4 + len(pieces): 0} if earlier else {},
        compiler_params=pltpu.CompilerParams(vmem_limit_bytes=24 * MIB),
        cost_estimate=pl.CostEstimate(
            flops=int(2 * blocks * listed * rows * block_rows * width * share),
            bytes_accessed=int(4 * blocks * listed * rows * block_rows * share),
            transcendentals=0,
        ),
        name="scores",
    )(dest, segments, lives, source_vectors, *pieces, *earlier)


def column_kernel(final, counts, slots, order, level, part, near, far, back, matrix, peaks, *refs):
    sums_out = refs[0]
    weights, columns = refs[-2:]
    blocks, block_rows = part.shape
    listed, rows = matrix.shape[1:3]
    total = part[...] + near[...] + far[...] + back[...] + jnp.exp2(-level[...])
    inverse = 1.0 / total
    if final:
        refs[1][...] = -EPSILON * LN2 * (level[...] + jnp.log2(total))
    for s in range(blocks):
        weights[s] = jnp.exp2(peaks[s] - level[s : s + 1, :]) * inverse[s : s + 1, :]
    sums_out[...] = jnp.zeros_like(sums_out)
    for g in range(blocks // SHARE):

        def one_entry(k, carry):
            columns[...] = jnp.zeros_like(columns)
            for m in range(SHARE):
                s = g * SHARE + m

                @pl.when(order[(blocks + s) * listed + k] > 0)
                def _():
                    w = weights[s, pl.ds(k, 1), :]
                    spread = [
                        jnp.broadcast_to(w[:, 128 * l : 128 * l + 128], (8, 128))
                        for l in range(block_rows // 128)
                    ]
                    for j in range(0, rows, 8):
                        piece = columns[j : j + 8, :]
                        for l, ws in enumerate(spread):
                            piece = piece + matrix[s, k, j : j + 8, 128 * l : 128 * l + 128] * ws
                        columns[j : j + 8, :] = piece

            row = jnp.sum(columns[...].T, axis=0, keepdims=True)
            sums_out[pl.ds(slots[g * listed + k], 1), :] = row
            return carry

        lax.fori_loop(0, listed, one_entry, 0)


def column_pass(final, counts, slots, order, targets, level, parts, matrix, peaks):
    blocks, block_rows = level.shape
    rows = matrix.shape[2]
    vmem = pl.BlockSpec(memory_space=pltpu.VMEM)
    smem = pl.BlockSpec(memory_space=pltpu.SMEM)
    out_shape = [jax.ShapeDtypeStruct((targets, rows), jnp.float32)]
    if final:
        out_shape.append(jax.ShapeDtypeStruct((blocks, block_rows), jnp.float32))
    return pl.pallas_call(
        functools.partial(column_kernel, final),
        in_specs=[smem] * 3 + [vmem] * 7,
        out_specs=[vmem] * len(out_shape),
        out_shape=out_shape,
        scratch_shapes=[
            pltpu.VMEM(peaks.shape, jnp.float32),
            pltpu.VMEM((rows, 128), jnp.float32),
        ],
        compiler_params=pltpu.CompilerParams(vmem_limit_bytes=8 * MIB),
        name="columns",
    )(counts, slots, order, level, *parts, matrix, peaks)


def row_kernel(counts, slots, order, level, sums, matrix, peaks, out, weights, gathered, spread):
    blocks, block_rows = out.shape
    listed, rows = matrix.shape[1:3]
    for e in range(2 * listed):
        gathered[e : e + 1, :] = sums[pl.ds(slots[e], 1), :]
    factors = (1.0 / (1.0 + gathered[...])).T
    for e in range(2 * listed):
        spread[e] = jnp.broadcast_to(factors[:, e : e + 1], (rows, 128))
    for s in range(blocks):
        weights[s] = jnp.exp2(peaks[s] - level[s : s + 1, :])
    lanes = block_rows // 128
    for s in range(blocks):
        g = s // SHARE

        def one_entry(t, total):
            k = order[s * listed + t]
            acc = [jnp.zeros((8, 128), jnp.float32) for _ in range(lanes)]
            for j in range(0, rows, 8):
                v = spread[g * listed + k, j : j + 8, :]
                for l in range(lanes):
                    acc[l] = acc[l] + matrix[s, k, j : j + 8, 128 * l : 128 * l + 128] * v
            w = weights[s, pl.ds(k, 1), :]
            return tuple(t + a * w[:, 128 * l : 128 * l + 128] for l, (t, a) in enumerate(zip(total, acc)))

        total = lax.fori_loop(
            0, counts[s], one_entry, tuple(jnp.zeros((8, 128), jnp.float32) for _ in range(lanes))
        )
        out[s : s + 1, :] = jnp.concatenate([jnp.sum(t, axis=0, keepdims=True) for t in total], axis=1)


def row_pass(counts, slots, order, level, sums, matrix, peaks):
    blocks, block_rows = level.shape
    listed, rows = matrix.shape[1:3]
    vmem = pl.BlockSpec(memory_space=pltpu.VMEM)
    smem = pl.BlockSpec(memory_space=pltpu.SMEM)
    return pl.pallas_call(
        row_kernel,
        in_specs=[smem] * 3 + [vmem] * 4,
        out_specs=vmem,
        out_shape=jax.ShapeDtypeStruct((blocks, block_rows), jnp.float32),
        scratch_shapes=[
            pltpu.VMEM(peaks.shape, jnp.float32),
            pltpu.VMEM((128, rows), jnp.float32),
            pltpu.VMEM((2 * listed, rows, 128), jnp.float32),
        ],
        compiler_params=pltpu.CompilerParams(vmem_limit_bytes=8 * MIB),
        name="rows",
    )(counts, slots, order, level, sums, matrix, peaks)


def from_columns(x):
    return [x] + [lax.ppermute(x, "col", [(i, (i + d) % 4) for i in range(4)]) for d in (1, 2, 3)]


def sum_over_rows(x):
    x = x + send(x, 0, 0, 1)
    x = x + send(x, 0, 1, 0) + send(x, 0, 2, 0) + send(x, 0, 3, 0)
    return x + send(x, 1, 0, 0) + send(x, 2, 0, 0) + send(x, 3, 0, 0)


def tables(pair_list, counts, owner_map, target_blocks):
    blocks, listed = pair_list.shape
    groups = blocks // SHARE
    targets = owner_map.shape[0]
    lead = pair_list.reshape(groups, SHARE, listed)[:, 0, :]
    lookup = lead[:, :, None] == jnp.arange(targets, dtype=jnp.int32)
    stored = jnp.sum(jnp.where(lookup, owner_map, 0), axis=2)
    me = lax.axis_index("row")
    z, y, core = me // 8, (me // 2) % 4, me % 2
    stages = piece_layout()
    layout = np.array([entry for stage in stages for entry in stage], np.int32)
    stage_at = np.array([n for n, stage in enumerate(stages) for _ in stage], np.int32)
    owner = (((z + layout[:, 2]) % 4) * 4 + (y + layout[:, 3]) % 4) * 2 + (core ^ layout[:, 4])
    held_slot = owner * target_blocks + layout[:, 5]
    match = held_slot[:, None, None] == stored[None]
    stage_of = jnp.sum(jnp.where(match, stage_at[:, None, None], 0), axis=0)
    ids = jnp.arange(listed, dtype=jnp.int32)
    rank = stage_of * listed + ids
    place = jnp.sum((rank[:, None, :] < rank[:, :, None]).astype(jnp.int32), axis=2)
    offset = jnp.arange(groups, dtype=jnp.int32)[:, None] * listed
    dest = jnp.sum(jnp.where(match, offset + place + 1, 0), axis=(1, 2)) - 1
    bounds = jnp.arange(STAGES + 1, dtype=jnp.int32)
    segments = jnp.sum((stage_of[:, None, :] < bounds[:, None]).astype(jnp.int32), axis=2)
    alive = ids[None, :] < counts[:, None]
    stage_rows = jnp.repeat(stage_of, SHARE, axis=0)
    lives = jnp.sum((alive[:, None, :] & (stage_rows[:, None, :] == bounds[:STAGES, None])).astype(jnp.int32), axis=2)
    at_place = place[:, None, :] == ids[None, :, None]
    slots = jnp.sum(jnp.where(at_place, stored[:, None, :], 0), axis=2)
    alive_at = jnp.any(jnp.repeat(at_place, SHARE, axis=0) & alive[:, None, :], axis=2)
    turn = jnp.sum((alive_at[:, None, :] & (ids[None, :] < ids[:, None])[None]).astype(jnp.int32), axis=2)
    order = jnp.sum(
        jnp.where(alive_at[:, None, :] & (turn[:, None, :] == ids[None, :, None]), ids[None, None, :], 0), axis=2
    )
    order = jnp.concatenate([order.reshape(-1), alive_at.astype(jnp.int32).reshape(-1)])
    cuts = np.cumsum([len(stage) for stage in stages])[:-1]
    return slots.reshape(-1), jnp.split(dest, cuts), segments.reshape(-1), lives.reshape(-1), order


def shards(source_vectors, target_vectors, pair_list, counts, owner_map):
    target_blocks, quarter, _ = target_vectors.shape
    listed = pair_list.shape[1]
    targets = owner_map.shape[0]
    slots, dest, segments, lives, order = tables(pair_list, counts, owner_map, target_blocks)

    def across(pieces):
        return pieces + [send(piece, 0, 0, 1) for piece in pieces]

    def stage(number, pieces, earlier):
        return score_stage(
            number, listed, dest[number], segments, lives, source_vectors, across(pieces), earlier
        )

    first = [ring_gather(target_vectors[:1], 0, 1), ring_gather(target_vectors[1:], 1, 0)]
    second = [
        send(first[0], 1, 0, 0),
        send(first[0], -1, 0, 0),
        send(first[1], 0, 1, 0),
        send(first[1], 0, -1, 0),
    ]
    done = stage(0, first, [])
    *second, peaks = tie(*second, done[1])
    third = [
        send(second[0][:2], 1, 0, 0),
        send(second[1][2:], -1, 0, 0),
        send(second[2][:2], 0, 1, 0),
        send(second[3][2:], 0, -1, 0),
    ]
    done = stage(1, second, [done[0], peaks, done[2]])
    *third, peaks = tie(*third, done[1])
    matrix, peaks, _, high, total = stage(2, third, [done[0], peaks, done[2]])

    both = from_columns(jnp.stack([high, total]))
    level = jnp.maximum(functools.reduce(jnp.maximum, [b[0] for b in both]), 0.0)
    parts = [b[1] * jnp.exp2(b[0] - level) for b in both]

    for sweep_index in range(SWEEPS):
        final = sweep_index == SWEEPS - 1
        sums = column_pass(final, counts, slots, order, targets, level, parts, matrix, peaks)
        if final:
            break
        sums = sum_over_rows(sums[0])
        parts = from_columns(row_pass(counts, slots, order, level, sums, matrix, peaks))
    sums, source_dual = sums
    row_count = targets // target_blocks
    back = lax.all_to_all(
        sums.reshape(row_count, target_blocks, quarter), "row", split_axis=0, concat_axis=0, tiled=True
    )
    target_dual = -EPSILON * jnp.log(1.0 + jnp.sum(back, axis=0))
    return source_dual, target_dual


def solution(mesh):
    return jax.shard_map(
        shards,
        mesh=mesh,
        in_specs=(P("row", None, None), P("row", "col", None), P("row", None), P("row"), P()),
        out_specs=(P("row", None), P("row", "col")),
        check_vma=False,
    )
```

time: 229 us -> 198 us (0.86)
  waiting for transfers between devices: 58.6 us -> 19.1 us
  local copies, waits for them, and re-layouts: 14 us -> 29.6 us
  starting transfers between devices: 81.9 us -> 67.3 us
  other arithmetic: 2.48 us -> 8.02 us
    ppermute x66 -> x38, waiting for transfers between devices: 47.3 us -> 13.7 us  [send(): return lax.ppermute(x, 'row', row_perm(dz, dy, dc))]
    ppermute x66 -> x38, starting transfers between devices: 74.1 us -> 55.5 us  [send(): return lax.ppermute(x, 'row', row_perm(dz, dy, dc))]
    unnamed x56 -> x32, local copies, waits for them, and re-layouts: 12 us -> 23.2 us
    ppermute x9, waiting for transfers between devices: 11.3 us -> 5.39 us  [from_columns(): lax.ppermute(x, 'col', [(i, (i + d) % 4) for i in range(4)])]
    ppermute x9, starting transfers between devices: 7.83 us -> 11.8 us  [from_columns(): lax.ppermute(x, 'col', [(i, (i + d) % 4) for i in range(4)])]
    reduce_sum x1 -> x9, other arithmetic: 0.83 us -> 4.36 us  [the longest x1 1 us: tables(): stage_of = jnp.sum(jnp.where(match, stage_at[:, None, None], 0), axis=0)]
    pallas_call x7 -> x8, Pallas kernels: 54.3 us -> 54.3 us  [the longest x3 32.7 us: score_stage(): pl.pallas_call(functools.partial(score_kernel, stage, listed), grid_spec=...]
  transfers between devices with their start and end apart: 75 -> 47, of which waited for: 35 -> 23; matrix products, arithmetic and copies ran while one was open for 1% -> 6% of each run, Pallas kernels for 7% -> 13%
where the time goes in v2:
time: 198 us; the launch traced here: 197 us
  starting transfers between devices  67.3 us (34%)
  Pallas kernels  54.3 us (27%)
  local copies, waits for them, and re-layouts  29.6 us (15%)
  waiting for transfers between devices  19.1 us (10%)
  blocking collectives  17.4 us (9%)
  other arithmetic  8.02 us (4%)
    ppermute x38, starting transfers between devices, send(): return lax.ppermute(x, 'row', row_perm(dz, dy, dc))  55.5 us
    pallas_call x3, Pallas kernels, score_stage(): pl.pallas_call(functools.partial(score_kernel, stage, listed), grid_spec=...  32.7 us
    unnamed x32, local copies, waits for them, and re-layouts  23.2 us
    all_to_all x1, blocking collectives, shards(): lax.all_to_all(sums.reshape(row_count, target_blocks, quarter), 'row', sp...  17.4 us
    pallas_call x3, Pallas kernels, column_pass(): pl.pallas_call(functools.partial(column_kernel, final), in_specs=[smem] *...  15.8 us
    ppermute x38, waiting for transfers between devices, send(): return lax.ppermute(x, 'row', row_perm(dz, dy, dc))  13.7 us
    ppermute x9, starting transfers between devices, from_columns(): lax.ppermute(x, 'col', [(i, (i + d) % 4) for i in range(4)])  11.8 us
    pallas_call x2, Pallas kernels, row_pass(): pl.pallas_call(row_kernel, in_specs=[smem] * 3 + [vmem] * 4, out_specs=vm...  5.77 us
  transfers between devices with their start and end apart: 47, of which 23 were waited for; matrix products, arithmetic and copies ran while one was open for 6% of the time, Pallas kernels for 13%

profile of v2, /device:TPU:1, one launch (start us, length us, event | category | flops | bytes accessed | tf_op | source)
XLA Modules:
  0.0 196.7 jit_solution(6557249474831205726)
XLA Ops:
  1.7 2.5 %collective-permute-start.5 = (bf16[1,128,768]{2,1,0:T(8,128)(2,1)S(1)}, bf16[1,128,768]{2,1,0:T(8,128)(2,1)S(1)}, u32[]{:S(2)}, u32[]{:S(2)}) collective-permute-start(bf16[1,128,768]{2,1,0:T(8,128)(2,1)S(1)} %get-tuple-element.48), channel_id=1, source_target_pairs={{0,32},{4,36},{8,40},{12,44},{16,48},{20,52},{24,56},{28,60},{32,6... | collective-permute-start | bytes 589832 | tf_op jit(solution)/shard_map/ppermute | solution.py:31
  16.6 2.4 %collective-permute-start.11 = (bf16[4,128,768]{2,1,0:T(8,128)(2,1)S(1)}, bf16[4,128,768]{2,1,0:T(8,128)(2,1)}, u32[]{:S(2)}, u32[]{:S(2)}) collective-permute-start(bf16[4,128,768]{2,1,0:T(8,128)(2,1)S(1)} %pad_maximum_fusion.1.refs_1_), channel_id=1, source_target_pairs={{0,4},{4,0},{8,12},{12,8},{16,20},{20,16},{24,28},{28,24},{32,36},... | collective-permute-start | bytes 2359304 | tf_op jit(solution)/shard_map/ppermute | solution.py:31
  21.0 3.2 %collective-permute-start.10 = (bf16[4,128,768]{2,1,0:T(8,128)(2,1)S(1)}, bf16[4,128,768]{2,1,0:T(8,128)(2,1)S(1)}, u32[]{:S(2)}, u32[]{:S(2)}) collective-permute-start(bf16[4,128,768]{2,1,0:T(8,128)(2,1)S(1)} %pad_maximum_fusion.refs_0_), channel_id=1, source_target_pairs={{0,4},{4,0},{8,12},{12,8},{16,20},{20,16},{24,28},{28,24},{32,36},... | collective-permute-start | bytes 2359304 | tf_op jit(solution)/shard_map/ppermute | solution.py:31
  24.3 2.6 %collective-permute-start.9 = (bf16[4,128,768]{2,1,0:T(8,128)(2,1)S(1)}, bf16[4,128,768]{2,1,0:T(8,128)(2,1)S(1)}, u32[]{:S(2)}, u32[]{:S(2)}) collective-permute-start(bf16[4,128,768]{2,1,0:T(8,128)(2,1)S(1)} %pad_maximum_fusion.1.refs_1_), channel_id=1, source_target_pairs={{0,24},{4,28},{8,0},{12,4},{16,8},{20,12},{24,16},{28,20},{32,56},... | collective-permute-start | bytes 2359304 | tf_op jit(solution)/shard_map/ppermute | solution.py:31
  29.8 2.8 %copy-done.2 = bf16[8,512,768]{2,1,0:T(8,128)(2,1)S(1)} copy-done((bf16[8,512,768]{2,1,0:T(8,128)(2,1)S(1)}, bf16[8,512,768]{2,1,0:T(8,128)(2,1)}, u32[]{:S(2)}) %copy-start.2) | copy-done | bytes 6291480
  32.6 10.7 %scores.3 = (f32[8,12,128,512]{3,2,1,0:T(8,128)}, f32[8,16,512]{2,1,0:T(8,128)S(1)}, f32[8,16,512]{2,1,0:T(8,128)S(1)}) custom-call(s32[16]{0:T(128)S(1)} %get-tuple-element.53.dest, s32[8]{0:T(128)S(1)} %reshape.101.segments, s32[24]{0:T(128)S(1)} %reshape.102.lives, bf16[8,512,768]{2,1,0:T(8,128)(2,1)S(1)} %copy-done.2, ...), custom_call_target="tpu_custom_call" | custom-call | flops 2415919104 | bytes 6291456 | tf_op jit(solution)/shard_map/scores/pallas_call | solution.py:183
  51.9 2.8 %collective-permute-start.13 = (bf16[2,128,768]{2,1,0:T(8,128)(2,1)S(1)}, bf16[2,128,768]{2,1,0:T(8,128)(2,1)}, u32[]{:S(2)}, u32[]{:S(2)}) collective-permute-start(bf16[2,128,768]{2,1,0:T(8,128)(2,1)S(1)} %slice.50), channel_id=1, source_target_pairs={{0,96},{4,100},{8,104},{12,108},{16,112},{20,116},{24,120},{28,124... | collective-permute-start | bytes 1179656 | tf_op jit(solution)/shard_map/ppermute | solution.py:31
  54.8 2.7 %collective-permute-start.15 = (bf16[2,128,768]{2,1,0:T(8,128)(2,1)S(1)}, bf16[2,128,768]{2,1,0:T(8,128)(2,1)}, u32[]{:S(2)}, u32[]{:S(2)}) collective-permute-start(bf16[2,128,768]{2,1,0:T(8,128)(2,1)S(1)} %slice.52), channel_id=1, source_target_pairs={{0,24},{4,28},{8,0},{12,4},{16,8},{20,12},{24,16},{28,20},{32,56},... | collective-permute-start | bytes 1179656 | tf_op jit(solution)/shard_map/ppermute | solution.py:31
  57.5 2.8 %copy-done.3 = bf16[8,512,768]{2,1,0:T(8,128)(2,1)S(1)} copy-done((bf16[8,512,768]{2,1,0:T(8,128)(2,1)S(1)}, bf16[8,512,768]{2,1,0:T(8,128)(2,1)}, u32[]{:S(2)}) %copy-start.3) | copy-done | bytes 6291480
  62.2 15.3 %scores.4 = (f32[8,12,128,512]{3,2,1,0:T(8,128)}, f32[8,16,512]{2,1,0:T(8,128)S(1)}, f32[8,16,512]{2,1,0:T(8,128)S(1)}) custom-call(s32[32]{0:T(128)S(1)} %split.11.dest, s32[8]{0:T(128)S(1)} %reshape.101.segments, s32[24]{0:T(128)S(1)} %reshape.102.lives, bf16[8,512,768]{2,1,0:T(8,128)(2,1)S(1)} %copy-done.3, ...), custom_call_target="tpu_custom_call", output_to_operand_aliasing={{0}: (12, {})} | custom-call | flops 4831838208 | bytes 12582912 | tf_op jit(solution)/shard_map/scores/pallas_call | solution.py:183
  85.7 2.8 %copy-done.4 = bf16[8,512,768]{2,1,0:T(8,128)(2,1)S(1)} copy-done((bf16[8,512,768]{2,1,0:T(8,128)(2,1)S(1)}, bf16[8,512,768]{2,1,0:T(8,128)(2,1)}, u32[]{:S(2)}) %copy-start.4) | copy-done | bytes 6291480
  90.4 6.7 %scores.5 = (f32[8,12,128,512]{3,2,1,0:T(8,128)}, f32[8,16,512]{2,1,0:T(8,128)S(1)}, f32[8,16,512]{2,1,0:T(8,128)}, f32[8,512]{1,0:T(8,128)S(1)}, f32[8,512]{1,0:T(8,128)S(1)}) custom-call(s32[16]{0:T(128)S(1)} %get-tuple-element.54.dest, s32[8]{0:T(128)S(1)} %reshape.101.segments, s32[24]{0:T(128)S(1)} %reshape.102.lives, ...), custom_call_target="tpu_custom_call", output_to_operand_aliasing={{0}: (12, {})} | custom-call | flops 2415919104 | bytes 6291456 | tf_op jit(solution)/shard_map/scores/pallas_call | solution.py:183
  98.4 2.5 %collective-permute-start.25 = (f32[2,8,512]{2,1,0:T(8,128)S(1)}, f32[2,8,512]{2,1,0:T(8,128)S(1)}, u32[]{:S(2)}, u32[]{:S(2)}) collective-permute-start(f32[2,8,512]{2,1,0:T(8,128)S(1)} %pad_maximum_fusion.2), channel_id=1, source_target_pairs={{0,2},{1,3},{2,0},{3,1},{4,6},{5,7},{6,4},{7,5},{8,10},{9,11},{10,... | collective-permute-start | bytes 98312 | tf_op jit(solution)/shard_map/ppermute | solution.py:329
  103.7 8.1 %copy-done = f32[8,12,128,512]{3,2,1,0:T(8,128)S(1)} copy-done((f32[8,12,128,512]{3,2,1,0:T(8,128)S(1)}, f32[8,12,128,512]{3,2,1,0:T(8,128)}, u32[]{:S(2)}) %copy-start) | copy-done | bytes 25165848
  111.9 5.1 %columns.3 = f32[64,128]{1,0:T(8,128)S(1)} custom-call(s32[8]{0:T(128)S(1)} %copy-done.13, s32[24]{0:T(128)S(1)} %reshape.99.slots, s32[192]{0:T(256)S(1)} %pad_add_fusion.order, f32[8,512]{1,0:T(8,128)S(1)} %get-tuple-element.47.level, f32[8,512]{1,0:T(8,128)S(1)} %get-tuple-element.52.part, f32[8,512]{1,0:T(8,128)S(1)} %get-tuple-element.51.near, ...), custom_call_target="tpu_custom_call" | custom-call | tf_op jit(solution)/shard_map/columns/pallas_call | solution.py:264
  116.9 5.0 %collective-permute-start.27 = (f32[64,128]{1,0:T(8,128)S(1)}, f32[64,128]{1,0:T(8,128)S(1)}, u32[]{:S(2)}, u32[]{:S(2)}) collective-permute-start(f32[64,128]{1,0:T(8,128)S(1)} %columns.3), channel_id=1, source_target_pairs={{0,4},{4,0},{8,12},{12,8},{16,20},{20,16},{24,28},{28,24},{32,36},... | collective-permute-start | bytes 98312 | tf_op jit(solution)/shard_map/ppermute | solution.py:31
  122.9 2.6 %collective-permute-start.30 = (f32[64,128]{1,0:T(8,128)S(1)}, f32[64,128]{1,0:T(8,128)S(1)}, u32[]{:S(2)}, u32[]{:S(2)}) collective-permute-start(f32[64,128]{1,0:T(8,128)S(1)} %add.132), channel_id=1, source_target_pairs={{0,24},{4,28},{8,0},{12,4},{16,8},{20,12},{24,16},{28,20},{32,56},... | collective-permute-start | bytes 98312 | tf_op jit(solution)/shard_map/ppermute | solution.py:31
  133.0 2.9 %rows.2.part = f32[8,512]{1,0:T(8,128)S(1)} custom-call(s32[8]{0:T(128)S(1)} %copy-done.13, s32[24]{0:T(128)S(1)} %reshape.99.slots, s32[192]{0:T(256)S(1)} %pad_add_fusion.order, f32[8,512]{1,0:T(8,128)S(1)} %get-tuple-element.47.level, f32[64,128]{1,0:T(8,128)S(1)} %add_add_fusion.2.sums, f32[8,12,128,512]{3,2,1,0:T(8,128)S(1)} %copy-done.1, ...), custom_call_target="tpu_custom_call" | custom-call | tf_op jit(solution)/shard_map/rows/pallas_call | solution.py:313
  136.0 3.5 %collective-permute-start.35 = (f32[8,512]{1,0:T(8,128)S(1)}, f32[8,512]{1,0:T(8,128)S(1)}, u32[]{:S(2)}, u32[]{:S(2)}) collective-permute-start(f32[8,512]{1,0:T(8,128)S(1)} %rows.2.part), channel_id=1, source_target_pairs={{0,2},{1,3},{2,0},{3,1},{4,6},{5,7},{6,4},{7,5},{8,10},{9,11},{10,... | collective-permute-start | bytes 49160 | tf_op jit(solution)/shard_map/ppermute | solution.py:329
  142.1 5.1 %columns.4 = f32[64,128]{1,0:T(8,128)S(1)} custom-call(s32[8]{0:T(128)S(1)} %copy-done.13, s32[24]{0:T(128)S(1)} %reshape.99.slots, s32[192]{0:T(256)S(1)} %pad_add_fusion.order, f32[8,512]{1,0:T(8,128)S(1)} %get-tuple-element.47.level, f32[8,512]{1,0:T(8,128)S(1)} %rows.2.part, f32[8,512]{1,0:T(8,128)S(1)} %collective-permute-done.34.near, ...), custom_call_target="tpu_custom_call" | custom-call | tf_op jit(solution)/shard_map/columns/pallas_call | solution.py:264
  147.2 5.2 %collective-permute-start.37 = (f32[64,128]{1,0:T(8,128)S(1)}, f32[64,128]{1,0:T(8,128)S(1)}, u32[]{:S(2)}, u32[]{:S(2)}) collective-permute-start(f32[64,128]{1,0:T(8,128)S(1)} %columns.4), channel_id=1, source_target_pairs={{0,4},{4,0},{8,12},{12,8},{16,20},{20,16},{24,28},{28,24},{32,36},... | collective-permute-start | bytes 98312 | tf_op jit(solution)/shard_map/ppermute | solution.py:31
  165.4 2.9 %rows.3.part = f32[8,512]{1,0:T(8,128)S(1)} custom-call(s32[8]{0:T(128)S(1)} %copy-done.13, s32[24]{0:T(128)S(1)} %reshape.99.slots, s32[192]{0:T(256)S(1)} %pad_add_fusion.order, f32[8,512]{1,0:T(8,128)S(1)} %get-tuple-element.47.level, f32[64,128]{1,0:T(8,128)S(1)} %add_add_fusion.sums, f32[8,12,128,512]{3,2,1,0:T(8,128)S(1)} %copy-done.1, ...), custom_call_target="tpu_custom_call" | custom-call | tf_op jit(solution)/shard_map/rows/pallas_call | solution.py:313
  173.1 5.6 %columns.5 = (f32[64,128]{1,0:T(8,128)S(1)}, f32[8,512]{1,0:T(8,128)}) custom-call(s32[8]{0:T(128)S(1)} %copy-done.13, s32[24]{0:T(128)S(1)} %reshape.99.slots, s32[192]{0:T(256)S(1)} %pad_add_fusion.order, f32[8,512]{1,0:T(8,128)S(1)} %get-tuple-element.47.level, f32[8,512]{1,0:T(8,128)S(1)} %rows.3.part, f32[8,512]{1,0:T(8,128)S(1)} %collective-permute-done.44.near, ...), custom_call_target="tpu_custom_call" | custom-call | tf_op jit(solution)/shard_map/columns/pallas_call | solution.py:264
  178.7 17.4 %all_to_all.5 = f32[32,2,128]{2,1,0:T(2,128)S(1)} all-to-all(f32[32,2,128]{2,1,0:T(2,128)S(1)} %bitcast.43), channel_id=1, replica_groups=mesh['row'=32,'col'=4] {'row'}, dimensions={0} | all-to-all | bytes 65536 | tf_op jit(solution)/shard_map/all_to_all | solution.py:422
  (172 shorter events, 72.5 us)
Async XLA Ops:
  1.7 13.2 %collective-permute-start.5 = (bf16[1,128,768]{2,1,0:T(8,128)(2,1)S(1)}, bf16[1,128,768]{2,1,0:T(8,128)(2,1)S(1)}, u32[]{:S(2)}, u32[]{:S(2)}) collective-permute-start(bf16[1,128,768]{2,1,0:T(8,128)(2,1)S(1)} %get-tuple-element.48), channel_id=1, source_target_pairs={{0,32},{4,36},{8,40},{12,44},{16,48},{20,52},{24,56},{28,60},{32,6... | collective-permute-start | bytes 589832 | tf_op jit(solution)/shard_map/ppermute | solution.py:31
  4.2 12.3 %collective-permute-start.6 = (bf16[1,128,768]{2,1,0:T(8,128)(2,1)S(1)}, bf16[1,128,768]{2,1,0:T(8,128)(2,1)S(1)}, u32[]{:S(2)}, u32[]{:S(2)}) collective-permute-start(bf16[1,128,768]{2,1,0:T(8,128)(2,1)S(1)} %get-tuple-element.48), channel_id=1, source_target_pairs={{0,96},{4,100},{8,104},{12,108},{16,112},{20,116},{24,120},{28,124... | collective-permute-start | bytes 589832 | tf_op jit(solution)/shard_map/ppermute | solution.py:31
  6.4 10.1 %collective-permute-start.7 = (bf16[1,128,768]{2,1,0:T(8,128)(2,1)S(1)}, bf16[1,128,768]{2,1,0:T(8,128)(2,1)S(1)}, u32[]{:S(2)}, u32[]{:S(2)}) collective-permute-start(bf16[1,128,768]{2,1,0:T(8,128)(2,1)S(1)} %get-tuple-element.48), channel_id=1, source_target_pairs={{0,64},{4,68},{8,72},{12,76},{16,80},{20,84},{24,88},{28,92},{32,9... | collective-permute-start | bytes 589832 | tf_op jit(solution)/shard_map/ppermute | solution.py:31
  7.6 12.4 %collective-permute-start = (bf16[1,128,768]{2,1,0:T(8,128)(2,1)S(1)}, bf16[1,128,768]{2,1,0:T(8,128)(2,1)S(1)}, u32[]{:S(2)}, u32[]{:S(2)}) collective-permute-start(bf16[1,128,768]{2,1,0:T(8,128)(2,1)S(1)} %get-tuple-element.49), channel_id=1, source_target_pairs={{0,8},{4,12},{8,16},{12,20},{16,24},{20,28},{24,0},{28,4},{32,40},... | collective-permute-start | bytes 589832 | tf_op jit(solution)/shard_map/ppermute | solution.py:31
  8.9 11.1 %collective-permute-start.1 = (bf16[1,128,768]{2,1,0:T(8,128)(2,1)S(1)}, bf16[1,128,768]{2,1,0:T(8,128)(2,1)S(1)}, u32[]{:S(2)}, u32[]{:S(2)}) collective-permute-start(bf16[1,128,768]{2,1,0:T(8,128)(2,1)S(1)} %get-tuple-element.49), channel_id=1, source_target_pairs={{0,24},{4,28},{8,0},{12,4},{16,8},{20,12},{24,16},{28,20},{32,56},... | collective-permute-start | bytes 589832 | tf_op jit(solution)/shard_map/ppermute | solution.py:31
  14.8 6.0 %collective-permute-start.2 = (bf16[1,128,768]{2,1,0:T(8,128)(2,1)S(1)}, bf16[1,128,768]{2,1,0:T(8,128)(2,1)S(1)}, u32[]{:S(2)}, u32[]{:S(2)}) collective-permute-start(bf16[1,128,768]{2,1,0:T(8,128)(2,1)S(1)} %get-tuple-element.49), channel_id=1, source_target_pairs={{0,16},{4,20},{8,24},{12,28},{16,0},{20,4},{24,8},{28,12},{32,48},... | collective-permute-start | bytes 589832 | tf_op jit(solution)/shard_map/ppermute | solution.py:31
  16.6 11.1 %collective-permute-start.11 = (bf16[4,128,768]{2,1,0:T(8,128)(2,1)S(1)}, bf16[4,128,768]{2,1,0:T(8,128)(2,1)}, u32[]{:S(2)}, u32[]{:S(2)}) collective-permute-start(bf16[4,128,768]{2,1,0:T(8,128)(2,1)S(1)} %pad_maximum_fusion.1.refs_1_), channel_id=1, source_target_pairs={{0,4},{4,0},{8,12},{12,8},{16,20},{20,16},{24,28},{28,24},{32,36},... | collective-permute-start | bytes 2359304 | tf_op jit(solution)/shard_map/ppermute | solution.py:31
  21.0 8.8 %collective-permute-start.10 = (bf16[4,128,768]{2,1,0:T(8,128)(2,1)S(1)}, bf16[4,128,768]{2,1,0:T(8,128)(2,1)S(1)}, u32[]{:S(2)}, u32[]{:S(2)}) collective-permute-start(bf16[4,128,768]{2,1,0:T(8,128)(2,1)S(1)} %pad_maximum_fusion.refs_0_), channel_id=1, source_target_pairs={{0,4},{4,0},{8,12},{12,8},{16,20},{20,16},{24,28},{28,24},{32,36},... | collective-permute-start | bytes 2359304 | tf_op jit(solution)/shard_map/ppermute | solution.py:31
  24.2 20.4 %collective-permute-start.8 = (bf16[4,128,768]{2,1,0:T(8,128)(2,1)S(1)}, bf16[4,128,768]{2,1,0:T(8,128)(2,1)S(1)}, u32[]{:S(2)}, u32[]{:S(2)}) collective-permute-start(bf16[4,128,768]{2,1,0:T(8,128)(2,1)S(1)} %pad_maximum_fusion.1.refs_1_), channel_id=1, source_target_pairs={{0,8},{4,12},{8,16},{12,20},{16,24},{20,28},{24,0},{28,4},{32,40},... | collective-permute-start | bytes 2359304 | tf_op jit(solution)/shard_map/ppermute | solution.py:31
  24.3 20.4 %collective-permute-start.9 = (bf16[4,128,768]{2,1,0:T(8,128)(2,1)S(1)}, bf16[4,128,768]{2,1,0:T(8,128)(2,1)S(1)}, u32[]{:S(2)}, u32[]{:S(2)}) collective-permute-start(bf16[4,128,768]{2,1,0:T(8,128)(2,1)S(1)} %pad_maximum_fusion.1.refs_1_), channel_id=1, source_target_pairs={{0,24},{4,28},{8,0},{12,4},{16,8},{20,12},{24,16},{28,20},{32,56},... | collective-permute-start | bytes 2359304 | tf_op jit(solution)/shard_map/ppermute | solution.py:31
  26.9 19.7 %collective-permute-start.3 = (bf16[4,128,768]{2,1,0:T(8,128)(2,1)S(1)}, bf16[4,128,768]{2,1,0:T(8,128)(2,1)S(1)}, u32[]{:S(2)}, u32[]{:S(2)}) collective-permute-start(bf16[4,128,768]{2,1,0:T(8,128)(2,1)S(1)} %pad_maximum_fusion.refs_0_), channel_id=1, source_target_pairs={{0,32},{4,36},{8,40},{12,44},{16,48},{20,52},{24,56},{28,60},{32,6... | collective-permute-start | bytes 2359304 | tf_op jit(solution)/shard_map/ppermute | solution.py:31
  27.7 18.9 %collective-permute-start.4 = (bf16[4,128,768]{2,1,0:T(8,128)(2,1)S(1)}, bf16[4,128,768]{2,1,0:T(8,128)(2,1)}, u32[]{:S(2)}, u32[]{:S(2)}) collective-permute-start(bf16[4,128,768]{2,1,0:T(8,128)(2,1)S(1)} %pad_maximum_fusion.refs_0_), channel_id=1, source_target_pairs={{0,96},{4,100},{8,104},{12,108},{16,112},{20,116},{24,120},{28,124... | collective-permute-start | bytes 2359304 | tf_op jit(solution)/shard_map/ppermute | solution.py:31
  46.6 5.4 %collective-permute-start.16 = (bf16[4,128,768]{2,1,0:T(8,128)(2,1)S(1)}, bf16[4,128,768]{2,1,0:T(8,128)(2,1)S(1)}, u32[]{:S(2)}, u32[]{:S(2)}) collective-permute-start(bf16[4,128,768]{2,1,0:T(8,128)(2,1)S(1)} %collective-permute-done.3.refs_0_), channel_id=1, source_target_pairs={{0,4},{4,0},{8,12},{12,8},{16,20},{20,16},{24,28},{28,24},{32,36},... | collective-permute-start | bytes 2359304 | tf_op jit(solution)/shard_map/ppermute | solution.py:31
  48.1 6.7 %collective-permute-start.17 = (bf16[4,128,768]{2,1,0:T(8,128)(2,1)}, bf16[4,128,768]{2,1,0:T(8,128)(2,1)}, u32[]{:S(2)}, u32[]{:S(2)}) collective-permute-start(bf16[4,128,768]{2,1,0:T(8,128)(2,1)} %collective-permute-done.4.refs_1_), channel_id=1, source_target_pairs={{0,4},{4,0},{8,12},{12,8},{16,20},{20,16},{24,28},{28,24},{32,36},... | collective-permute-start | bytes 2359304 | tf_op jit(solution)/shard_map/ppermute | solution.py:31
  48.1 6.7 %collective-permute-start.18 = (bf16[4,128,768]{2,1,0:T(8,128)(2,1)S(1)}, bf16[4,128,768]{2,1,0:T(8,128)(2,1)}, u32[]{:S(2)}, u32[]{:S(2)}) collective-permute-start(bf16[4,128,768]{2,1,0:T(8,128)(2,1)S(1)} %collective-permute-done.8.refs_2_), channel_id=1, source_target_pairs={{0,4},{4,0},{8,12},{12,8},{16,20},{20,16},{24,28},{28,24},{32,36},... | collective-permute-start | bytes 2359304 | tf_op jit(solution)/shard_map/ppermute | solution.py:31
  48.6 8.9 %collective-permute-start.19 = (bf16[4,128,768]{2,1,0:T(8,128)(2,1)S(1)}, bf16[4,128,768]{2,1,0:T(8,128)(2,1)}, u32[]{:S(2)}, u32[]{:S(2)}) collective-permute-start(bf16[4,128,768]{2,1,0:T(8,128)(2,1)S(1)} %collective-permute-done.9.refs_3_), channel_id=1, source_target_pairs={{0,4},{4,0},{8,12},{12,8},{16,20},{20,16},{24,28},{28,24},{32,36},... | collective-permute-start | bytes 2359304 | tf_op jit(solution)/shard_map/ppermute | solution.py:31
  51.8 27.1 %collective-permute-start.12 = (bf16[2,128,768]{2,1,0:T(8,128)(2,1)S(1)}, bf16[2,128,768]{2,1,0:T(8,128)(2,1)S(1)}, u32[]{:S(2)}, u32[]{:S(2)}) collective-permute-start(bf16[2,128,768]{2,1,0:T(8,128)(2,1)S(1)} %slice.49), channel_id=1, source_target_pairs={{0,32},{4,36},{8,40},{12,44},{16,48},{20,52},{24,56},{28,60},{32,6... | collective-permute-start | bytes 1179656 | tf_op jit(solution)/shard_map/ppermute | solution.py:31
  51.9 27.0 %collective-permute-start.13 = (bf16[2,128,768]{2,1,0:T(8,128)(2,1)S(1)}, bf16[2,128,768]{2,1,0:T(8,128)(2,1)}, u32[]{:S(2)}, u32[]{:S(2)}) collective-permute-start(bf16[2,128,768]{2,1,0:T(8,128)(2,1)S(1)} %slice.50), channel_id=1, source_target_pairs={{0,96},{4,100},{8,104},{12,108},{16,112},{20,116},{24,120},{28,124... | collective-permute-start | bytes 1179656 | tf_op jit(solution)/shard_map/ppermute | solution.py:31
  54.8 24.2 %collective-permute-start.14 = (bf16[2,128,768]{2,1,0:T(8,128)(2,1)S(1)}, bf16[2,128,768]{2,1,0:T(8,128)(2,1)}, u32[]{:S(2)}, u32[]{:S(2)}) collective-permute-start(bf16[2,128,768]{2,1,0:T(8,128)(2,1)S(1)} %slice.51), channel_id=1, source_target_pairs={{0,8},{4,12},{8,16},{12,20},{16,24},{20,28},{24,0},{28,4},{32,40},... | collective-permute-start | bytes 1179656 | tf_op jit(solution)/shard_map/ppermute | solution.py:31
  54.8 24.2 %collective-permute-start.15 = (bf16[2,128,768]{2,1,0:T(8,128)(2,1)S(1)}, bf16[2,128,768]{2,1,0:T(8,128)(2,1)}, u32[]{:S(2)}, u32[]{:S(2)}) collective-permute-start(bf16[2,128,768]{2,1,0:T(8,128)(2,1)S(1)} %slice.52), channel_id=1, source_target_pairs={{0,24},{4,28},{8,0},{12,4},{16,8},{20,12},{24,16},{28,20},{32,56},... | collective-permute-start | bytes 1179656 | tf_op jit(solution)/shard_map/ppermute | solution.py:31
  79.0 6.7 %collective-permute-start.20 = (bf16[2,128,768]{2,1,0:T(8,128)(2,1)S(1)}, bf16[2,128,768]{2,1,0:T(8,128)(2,1)S(1)}, u32[]{:S(2)}, u32[]{:S(2)}) collective-permute-start(bf16[2,128,768]{2,1,0:T(8,128)(2,1)S(1)} %collective-permute-done.12.refs_0_), channel_id=1, source_target_pairs={{0,4},{4,0},{8,12},{12,8},{16,20},{20,16},{24,28},{28,24},{32,36},... | collective-permute-start | bytes 1179656 | tf_op jit(solution)/shard_map/ppermute | solution.py:31
  97.1 5.1 %collective-permute-start.24 = (f32[2,8,512]{2,1,0:T(8,128)S(1)}, f32[2,8,512]{2,1,0:T(8,128)S(1)}, u32[]{:S(2)}, u32[]{:S(2)}) collective-permute-start(f32[2,8,512]{2,1,0:T(8,128)S(1)} %pad_maximum_fusion.2), channel_id=1, source_target_pairs={{0,1},{1,2},{2,3},{3,0},{4,5},{5,6},{6,7},{7,4},{8,9},{9,10},{10,1... | collective-permute-start | bytes 98312 | tf_op jit(solution)/shard_map/ppermute | solution.py:329
  116.9 5.9 %collective-permute-start.27 = (f32[64,128]{1,0:T(8,128)S(1)}, f32[64,128]{1,0:T(8,128)S(1)}, u32[]{:S(2)}, u32[]{:S(2)}) collective-permute-start(f32[64,128]{1,0:T(8,128)S(1)} %columns.3), channel_id=1, source_target_pairs={{0,4},{4,0},{8,12},{12,8},{16,20},{20,16},{24,28},{28,24},{32,36},... | collective-permute-start | bytes 98312 | tf_op jit(solution)/shard_map/ppermute | solution.py:31
  147.2 6.1 %collective-permute-start.37 = (f32[64,128]{1,0:T(8,128)S(1)}, f32[64,128]{1,0:T(8,128)S(1)}, u32[]{:S(2)}, u32[]{:S(2)}) collective-permute-start(f32[64,128]{1,0:T(8,128)S(1)} %columns.4), channel_id=1, source_target_pairs={{0,4},{4,0},{8,12},{12,8},{16,20},{20,16},{24,28},{28,24},{32,36},... | collective-permute-start | bytes 98312 | tf_op jit(solution)/shard_map/ppermute | solution.py:31
  (39 other events, 198.2 us)

commit v3 on v2

--- a/solution.py
+++ b/solution.py
@@ -66,109 +66,84 @@
     number = max(entry[0] for entry in layout) + 1
     pieces, refs = refs[:number], refs[number:]
     if stage > 0:
-        (_, peak_in, sum_in), refs = refs[:3], refs[3:]
+        refs = refs[3:]
     matrix, peak_out, sum_out = refs[:3]
     if stage == STAGES - 1:
         high_out, total_out = refs[3:5]
-    held, raised, tally, fetch_sems, store_sems = refs[-5:]
-    step = pl.program_id(0)
-    group = step // SHARE
-    rows = held.shape[0] // (2 * listed + 4)
-    buffers = raised.shape[0]
+    held, streamed, fetch_sems, stream_sems = refs[-4:]
+    blocks = source.shape[0]
+    rows = matrix.shape[2]
+
+    def stream(s):
+        return pltpu.make_async_copy(source.at[s], streamed.at[lax.rem(s, 2)], stream_sems.at[lax.rem(s, 2)])
+
+    stream(0).start()
 
     def fetch(piece, index, entry):
         return pltpu.make_async_copy(
             pieces[piece].at[index], held.at[pl.ds(entry * rows, rows)], fetch_sems.at[entry]
         )
 
-    def store(buffer, entry):
-        return pltpu.make_async_copy(raised.at[buffer], matrix.at[step, entry], store_sems.at[buffer])
-
-    @pl.when(step == 0)
-    def _():
-        tally[0] = 0
-        for position, (piece, index, *_) in enumerate(layout):
-
-            @pl.when(dest[position] >= 0)
-            def _():
-                fetch(piece, index, dest[position]).start()
-
-    for g in range(2):
-
-        @pl.when(step == SHARE * g)
+    for position, (piece, index, *_) in enumerate(layout):
+
+        @pl.when(dest[position] >= 0)
+        def _():
+            fetch(piece, index, dest[position]).start()
+
+    if stage == 0:
+        peak_out[...] = jnp.full(peak_out.shape, NEGATIVE, jnp.float32)
+        sum_out[...] = jnp.zeros(sum_out.shape, jnp.float32)
+
+    def one_block(s, carry):
+        group = s // SHARE
+        begin = segments[group * (STAGES + 1) + stage]
+        live = lives[s * STAGES + stage]
+
+        @pl.when(lax.rem(s, SHARE) == 0)
         def _():
             def arrive(entry, carry):
-                fetch(0, 0, g * listed + entry).wait()
+                fetch(0, 0, group * listed + entry).wait()
                 return carry
 
-            lax.fori_loop(segments[g * (STAGES + 1) + stage], segments[g * (STAGES + 1) + stage + 1], arrive, 0)
-
-    if stage > 0:
-        peak_out[...] = peak_in[...]
-        sum_out[...] = sum_in[...]
-    else:
-        peak_out[...] = jnp.full(peak_out.shape, NEGATIVE, jnp.float32)
-        sum_out[...] = jnp.zeros(sum_out.shape, jnp.float32)
-    begin = segments[group * (STAGES + 1) + stage]
-    live = lives[step * STAGES + stage]
-
-    def batch(first, size, spare):
-        base = pl.multiple_of((group * listed + begin + first) * rows, rows)
-        scores = lax.dot_general(
-            held[pl.ds(base, size * rows), :],
-            source[0],
-            (((1,), (1,)), ((), ())),
-            preferred_element_type=jnp.float32,
-        )
-
-        def finish(p):
-            count = tally[0] + first + p
-            buffer = lax.rem(count, buffers)
-
-            @pl.when(count >= buffers)
-            def _():
-                store(buffer, 0).wait()
-
-            one = scores[p * rows : (p + 1) * rows] * SCALE
-            peak = jnp.max(one, axis=0, keepdims=True)
-            lifted = jnp.exp2(one - peak)
-            raised[buffer] = lifted
-            peak_out[0, pl.ds(begin + first + p, 1), :] = peak
-            sum_out[0, pl.ds(begin + first + p, 1), :] = jnp.sum(lifted, axis=0, keepdims=True)
-            store(buffer, begin + first + p).start()
-
-        for p in range(size):
-            if p < size - spare:
-                finish(p)
-            else:
-                pl.when(first + p < live)(functools.partial(finish, p))
-
-    def four(q, carry):
-        batch(4 * q, 4, 0)
+            lax.fori_loop(begin, segments[group * (STAGES + 1) + stage + 1], arrive, 0)
+
+        @pl.when(s + 1 < blocks)
+        def _():
+            stream(s + 1).start()
+
+        stream(s).wait()
+
+        def batch(first, size):
+            base = pl.multiple_of((group * listed + begin + first) * rows, rows)
+            scores = lax.dot_general(
+                held[pl.ds(base, size * rows), :],
+                streamed[lax.rem(s, 2)],
+                (((1,), (1,)), ((), ())),
+                preferred_element_type=jnp.float32,
+            )
+            for p in range(size):
+                one = scores[p * rows : (p + 1) * rows] * SCALE
+                peak = jnp.max(one, axis=0, keepdims=True)
+                lifted = jnp.exp2(one - peak)
+                matrix[s, begin + first + p] = lifted
+                peak_out[s, pl.ds(begin + first + p, 1), :] = peak
+                sum_out[s, pl.ds(begin + first + p, 1), :] = jnp.sum(lifted, axis=0, keepdims=True)
+
+        def four(q, carry):
+            batch(4 * q, 4)
+            return carry
+
+        lax.fori_loop(0, live // 4, four, 0)
+        for size in (1, 2, 3):
+            pl.when(lax.rem(live, 4) == size)(functools.partial(batch, live - size, size))
         return carry
 
-    def two(q, carry):
-        batch(4 * (live // 4) + 2 * q, 2, 1)
-        return carry
-
-    lax.fori_loop(0, live // 4, four, 0)
-    lax.fori_loop(0, (live % 4 + 1) // 2, two, 0)
-    tally[0] = tally[0] + live
-
-    @pl.when(step == pl.num_programs(0) - 1)
-    def _():
-        for buffer in range(buffers):
-
-            @pl.when(tally[0] > buffer)
-            def _():
-                store(buffer, 0).wait()
-
+    lax.fori_loop(0, blocks, one_block, 0)
     if stage == STAGES - 1:
-        high = jnp.max(peak_out[0], axis=0, keepdims=True)
-        high_out[pl.ds(step, 1), :] = high
-        total_out[pl.ds(step, 1), :] = jnp.sum(
-            sum_out[0] * jnp.exp2(peak_out[0] - high), axis=0, keepdims=True
-        )
+        for s in range(blocks):
+            high = jnp.max(peak_out[s], axis=0, keepdims=True)
+            high_out[s : s + 1, :] = high
+            total_out[s : s + 1, :] = jnp.sum(sum_out[s] * jnp.exp2(peak_out[s] - high), axis=0, keepdims=True)
 
 
 def score_stage(stage, listed, dest, segments, lives, source_vectors, pieces, earlier):
@@ -176,35 +151,27 @@
     rows = pieces[0].shape[1]
     padded = 16
     hbm = pl.BlockSpec(memory_space=pltpu.HBM)
-    small = pl.BlockSpec((1, padded, block_rows), lambda s, *_: (s, 0, 0))
-    whole = pl.BlockSpec((blocks, block_rows), lambda s, *_: (0, 0))
+    vmem = pl.BlockSpec(memory_space=pltpu.VMEM)
+    smem = pl.BlockSpec(memory_space=pltpu.SMEM)
     last = stage == STAGES - 1
     share = (0.25, 0.5, 0.25)[stage]
+    small = jax.ShapeDtypeStruct((blocks, padded, block_rows), jnp.float32)
+    whole = jax.ShapeDtypeStruct((blocks, block_rows), jnp.float32)
+    if earlier:
+        earlier = [pltpu.with_memory_space_constraint(earlier[0], pltpu.VMEM)] + earlier[1:]
     return pl.pallas_call(
         functools.partial(score_kernel, stage, listed),
-        grid_spec=pltpu.PrefetchScalarGridSpec(
-            num_scalar_prefetch=3,
-            grid=(blocks,),
-            in_specs=[pl.BlockSpec((1, block_rows, width), lambda s, *_: (s, 0, 0))]
-            + [hbm] * len(pieces)
-            + [hbm, small, small][: len(earlier)],
-            out_specs=[hbm, small, small] + [whole, whole] * last,
-            scratch_shapes=[
-                pltpu.VMEM(((2 * listed + 4) * rows, width), jnp.bfloat16),
-                pltpu.VMEM((8, rows, block_rows), jnp.float32),
-                pltpu.SMEM((1,), jnp.int32),
-                pltpu.SemaphoreType.DMA((2 * listed,)),
-                pltpu.SemaphoreType.DMA((8,)),
-            ],
-        ),
-        out_shape=[
-            jax.ShapeDtypeStruct((blocks, listed, rows, block_rows), jnp.float32),
-            jax.ShapeDtypeStruct((blocks, padded, block_rows), jnp.float32),
-            jax.ShapeDtypeStruct((blocks, padded, block_rows), jnp.float32),
-        ]
-        + [jax.ShapeDtypeStruct((blocks, block_rows), jnp.float32)] * 2 * last,
-        input_output_aliases={4 + len(pieces): 0} if earlier else {},
-        compiler_params=pltpu.CompilerParams(vmem_limit_bytes=24 * MIB),
+        in_specs=[smem] * 3 + [hbm] * (1 + len(pieces)) + [vmem] * len(earlier),
+        out_specs=[vmem] * (3 + 2 * last),
+        out_shape=[pltpu.VMEM((blocks, listed, rows, block_rows), jnp.float32), small, small] + [whole] * 2 * last,
+        scratch_shapes=[
+            pltpu.VMEM((2 * listed * rows, width), jnp.bfloat16),
+            pltpu.VMEM((2, block_rows, width), jnp.bfloat16),
+            pltpu.SemaphoreType.DMA((2 * listed,)),
+            pltpu.SemaphoreType.DMA((2,)),
+        ],
+        input_output_aliases={4 + len(pieces) + n: n for n in range(len(earlier))},
+        compiler_params=pltpu.CompilerParams(vmem_limit_bytes=12 * MIB),
         cost_estimate=pl.CostEstimate(
             flops=int(2 * blocks * listed * rows * block_rows * width * share),
             bytes_accessed=int(4 * blocks * listed * rows * block_rows * share),
@@ -377,10 +344,12 @@
     target_blocks, quarter, _ = target_vectors.shape
     listed = pair_list.shape[1]
     targets = owner_map.shape[0]
+    source_vectors = pltpu.with_memory_space_constraint(source_vectors, pltpu.HBM)
     slots, dest, segments, lives, order = tables(pair_list, counts, owner_map, target_blocks)
 
     def across(pieces):
-        return pieces + [send(piece, 0, 0, 1) for piece in pieces]
+        pieces = pieces + [send(piece, 0, 0, 1) for piece in pieces]
+        return [pltpu.with_memory_space_constraint(piece, pltpu.HBM) for piece in pieces]
 
     def stage(number, pieces, earlier):
         return score_stage(
@@ -388,6 +357,8 @@
         )
 
     first = [ring_gather(target_vectors[:1], 0, 1), ring_gather(target_vectors[1:], 1, 0)]
+    *first, slots, segments, lives, order, early, later, latest = tie(*first, slots, segments, lives, order, *dest)
+    dest = [early, later, latest]
     second = [
         send(first[0], 1, 0, 0),
         send(first[0], -1, 0, 0),
@@ -405,6 +376,7 @@
     done = stage(1, second, [done[0], peaks, done[2]])
     *third, peaks = tie(*third, done[1])
     matrix, peaks, _, high, total = stage(2, third, [done[0], peaks, done[2]])
+    matrix = pltpu.with_memory_space_constraint(matrix, pltpu.VMEM)
 
     both = from_columns(jnp.stack([high, total]))
     level = jnp.maximum(functools.reduce(jnp.maximum, [b[0] for b in both]), 0.0)

time: 198 us -> 176 us (0.89)
  local copies, waits for them, and re-layouts: 29.6 us -> 6.59 us
  waiting for transfers between devices: 19.1 us -> 30.7 us
  Pallas kernels: 54.3 us -> 48.5 us
  starting transfers between devices: 67.3 us -> 63.7 us
    unnamed x32 -> x42, local copies, waits for them, and re-layouts: 23.2 us -> 2.53 us
    ppermute x38, waiting for transfers between devices: 13.7 us -> 24.9 us  [send(): return lax.ppermute(x, 'row', row_perm(dz, dy, dc))]
    pallas_call x3, Pallas kernels: 32.7 us -> 28.2 us  [score_stage(): pl.pallas_call(functools.partial(score_kernel, stage, listed), in_specs=[...]
    ppermute x38, starting transfers between devices: 55.5 us -> 51.8 us  [send(): return lax.ppermute(x, 'row', row_perm(dz, dy, dc))]
  transfers between devices with their start and end apart: 47 -> 47, of which waited for: 23 -> 29; matrix products, arithmetic and copies ran while one was open for 6% -> 5% of each run, Pallas kernels for 13% -> 11%
where the time goes in v3:
time: 176 us
  starting transfers between devices  63.7 us (36%)
  Pallas kernels  48.5 us (28%)
  waiting for transfers between devices  30.7 us (17%)
  blocking collectives  18.3 us (10%)
  other arithmetic  6.75 us (4%)
  local copies, waits for them, and re-layouts  6.59 us (4%)
    ppermute x38, starting transfers between devices, send(): return lax.ppermute(x, 'row', row_perm(dz, dy, dc))  51.8 us
    pallas_call x3, Pallas kernels, score_stage(): pl.pallas_call(functools.partial(score_kernel, stage, listed), in_specs=[...  28.2 us
    ppermute x38, waiting for transfers between devices, send(): return lax.ppermute(x, 'row', row_perm(dz, dy, dc))  24.9 us
    all_to_all x1, blocking collectives, shards(): lax.all_to_all(sums.reshape(row_count, target_blocks, quarter), 'row', sp...  18.3 us
    pallas_call x3, Pallas kernels, column_pass(): pl.pallas_call(functools.partial(column_kernel, final), in_specs=[smem] *...  15.1 us
    ppermute x9, starting transfers between devices, from_columns(): lax.ppermute(x, 'col', [(i, (i + d) % 4) for i in range(4)])  11.9 us
    ppermute x9, waiting for transfers between devices, from_columns(): lax.ppermute(x, 'col', [(i, (i + d) % 4) for i in range(4)])  5.89 us
    pallas_call x2, Pallas kernels, row_pass(): pl.pallas_call(row_kernel, in_specs=[smem] * 3 + [vmem] * 4, out_specs=vm...  5.24 us
  transfers between devices with their start and end apart: 47, of which 29 were waited for; matrix products, arithmetic and copies ran while one was open for 5% of the time, Pallas kernels for 11%

profile of v3, /device:TPU:1, one launch (start us, length us, event | category | flops | bytes accessed | tf_op | source)
XLA Modules:
  0.0 175.7 jit_solution(9302771420638488434)
XLA Ops:
  1.7 2.5 %collective-permute-start.3 = (bf16[1,128,768]{2,1,0:T(8,128)(2,1)S(1)}, bf16[1,128,768]{2,1,0:T(8,128)(2,1)S(1)}, u32[]{:S(2)}, u32[]{:S(2)}) collective-permute-start(bf16[1,128,768]{2,1,0:T(8,128)(2,1)S(1)} %get-tuple-element.66), channel_id=1, source_target_pairs={{0,32},{4,36},{8,40},{12,44},{16,48},{20,52},{24,56},{28,60},{32,6... | collective-permute-start | bytes 589832 | tf_op jit(solution)/shard_map/ppermute | solution.py:31
  4.2 2.2 %collective-permute-start.4 = (bf16[1,128,768]{2,1,0:T(8,128)(2,1)S(1)}, bf16[1,128,768]{2,1,0:T(8,128)(2,1)S(1)}, u32[]{:S(2)}, u32[]{:S(2)}) collective-permute-start(bf16[1,128,768]{2,1,0:T(8,128)(2,1)S(1)} %get-tuple-element.66), channel_id=1, source_target_pairs={{0,96},{4,100},{8,104},{12,108},{16,112},{20,116},{24,120},{28,124... | collective-permute-start | bytes 589832 | tf_op jit(solution)/shard_map/ppermute | solution.py:31
  21.0 4.2 %collective-permute-done.2 = bf16[1,128,768]{2,1,0:T(8,128)(2,1)S(1)} collective-permute-done((bf16[1,128,768]{2,1,0:T(8,128)(2,1)S(1)}, bf16[1,128,768]{2,1,0:T(8,128)(2,1)S(1)}, u32[]{:S(2)}, u32[]{:S(2)}) %collective-permute-start.2) | collective-permute-done | bytes 196640 | tf_op jit(solution)/shard_map/ppermute | solution.py:31
  25.3 3.2 %collective-permute-start.10 = (bf16[4,128,768]{2,1,0:T(8,128)(2,1)S(1)}, bf16[4,128,768]{2,1,0:T(8,128)(2,1)S(1)}, u32[]{:S(2)}, u32[]{:S(2)}) collective-permute-start(bf16[4,128,768]{2,1,0:T(8,128)(2,1)S(1)} %pad_maximum_fusion.refs_0_), channel_id=1, source_target_pairs={{0,4},{4,0},{8,12},{12,8},{16,20},{20,16},{24,28},{28,24},{32,36},... | collective-permute-start | bytes 2359304 | tf_op jit(solution)/shard_map/ppermute | solution.py:31
  31.4 2.6 %collective-permute-start.9 = (bf16[4,128,768]{2,1,0:T(8,128)(2,1)S(1)}, bf16[4,128,768]{2,1,0:T(8,128)(2,1)S(1)}, u32[]{:S(2)}, u32[]{:S(2)}) collective-permute-start(bf16[4,128,768]{2,1,0:T(8,128)(2,1)S(1)} %pad_maximum_fusion.1.refs_1_), channel_id=1, source_target_pairs={{0,24},{4,28},{8,0},{12,4},{16,8},{20,12},{24,16},{28,20},{32,56},... | collective-permute-start | bytes 2359304 | tf_op jit(solution)/shard_map/ppermute | solution.py:31
  34.9 9.2 %scores.3 = (f32[8,12,128,512]{3,2,1,0:T(8,128)S(1)}, f32[8,16,512]{2,1,0:T(8,128)S(1)}, f32[8,16,512]{2,1,0:T(8,128)S(1)}) custom-call(s32[16]{0:T(128)S(1)} %get-tuple-element.40.dest, s32[8]{0:T(128)S(1)} %reshape.100.segments, s32[24]{0:T(128)S(1)} %reshape.101.lives, bf16[8,512,768]{2,1,0:T(8,128)(2,1)} %source.5, bf16[4,128,768]{2,1,0:T(8,128)(2,1)} %copy-done.2, ...), custom_call_target="tpu_custom_call" | custom-call | flops 2415919104 | bytes 6291456 | tf_op jit(solution)/shard_map/scores/pallas_call | solution.py:162
  44.1 4.4 %collective-permute-done.6.refs_0_ = bf16[4,128,768]{2,1,0:T(8,128)(2,1)S(1)} collective-permute-done((bf16[4,128,768]{2,1,0:T(8,128)(2,1)S(1)}, bf16[4,128,768]{2,1,0:T(8,128)(2,1)S(1)}, u32[]{:S(2)}, u32[]{:S(2)}) %collective-permute-start.6) | collective-permute-done | bytes 786464 | tf_op jit(solution)/shard_map/ppermute | solution.py:31
  48.5 2.0 %collective-permute-done.8.refs_2_ = bf16[4,128,768]{2,1,0:T(8,128)(2,1)S(1)} collective-permute-done((bf16[4,128,768]{2,1,0:T(8,128)(2,1)S(1)}, bf16[4,128,768]{2,1,0:T(8,128)(2,1)S(1)}, u32[]{:S(2)}, u32[]{:S(2)}) %collective-permute-start.8) | collective-permute-done | bytes 786464 | tf_op jit(solution)/shard_map/ppermute | solution.py:31
  56.7 2.6 %collective-permute-start.15 = (bf16[2,128,768]{2,1,0:T(8,128)(2,1)S(1)}, bf16[2,128,768]{2,1,0:T(8,128)(2,1)S(1)}, u32[]{:S(2)}, u32[]{:S(2)}) collective-permute-start(bf16[2,128,768]{2,1,0:T(8,128)(2,1)S(1)} %slice.52), channel_id=1, source_target_pairs={{0,24},{4,28},{8,0},{12,4},{16,8},{20,12},{24,16},{28,20},{32,56},... | collective-permute-start | bytes 1179656 | tf_op jit(solution)/shard_map/ppermute | solution.py:31
  60.2 10.1 %scores.4 = (f32[8,12,128,512]{3,2,1,0:T(8,128)S(1)}, f32[8,16,512]{2,1,0:T(8,128)S(1)}, f32[8,16,512]{2,1,0:T(8,128)S(1)}) custom-call(s32[32]{0:T(128)S(1)} %split.10.dest, s32[8]{0:T(128)S(1)} %reshape.100.segments, s32[24]{0:T(128)S(1)} %reshape.101.lives, ...), custom_call_target="tpu_custom_call", output_to_operand_aliasing={{0}: (12, {}), {1}: (13, {}), {2}: (14, {})} | custom-call | flops 4831838208 | bytes 12582912 | tf_op jit(solution)/shard_map/scores/pallas_call | solution.py:162
  70.4 2.0 %collective-permute-start.20 = (bf16[2,128,768]{2,1,0:T(8,128)(2,1)S(1)}, bf16[2,128,768]{2,1,0:T(8,128)(2,1)S(1)}, u32[]{:S(2)}, u32[]{:S(2)}) collective-permute-start(bf16[2,128,768]{2,1,0:T(8,128)(2,1)S(1)} %collective-permute-done.12.refs_0_), channel_id=1, source_target_pairs={{0,4},{4,0},{8,12},{12,8},{16,20},{20,16},{24,28},{28,24},{32,36},... | collective-permute-start | bytes 1179656 | tf_op jit(solution)/shard_map/ppermute | solution.py:31
  76.2 8.9 %scores.5 = (f32[8,12,128,512]{3,2,1,0:T(8,128)S(1)}, f32[8,16,512]{2,1,0:T(8,128)S(1)}, f32[8,16,512]{2,1,0:T(8,128)S(1)}, f32[8,512]{1,0:T(8,128)S(1)}, f32[8,512]{1,0:T(8,128)S(1)}) custom-call(s32[16]{0:T(128)S(1)} %get-tuple-element.35.dest, s32[8]{0:T(128)S(1)} %reshape.100.segments, ...), custom_call_target="tpu_custom_call", output_to_operand_aliasing={{0}: (12, {}), {1}: (13, {}), {2}: (14, {})} | custom-call | flops 2415919104 | bytes 6291456 | tf_op jit(solution)/shard_map/scores/pallas_call | solution.py:162
  86.4 2.5 %collective-permute-start.25 = (f32[2,8,512]{2,1,0:T(8,128)S(1)}, f32[2,8,512]{2,1,0:T(8,128)S(1)}, u32[]{:S(2)}, u32[]{:S(2)}) collective-permute-start(f32[2,8,512]{2,1,0:T(8,128)S(1)} %pad_maximum_fusion.2), channel_id=1, source_target_pairs={{0,2},{1,3},{2,0},{3,1},{4,6},{5,7},{6,4},{7,5},{8,10},{9,11},{10,... | collective-permute-start | bytes 98312 | tf_op jit(solution)/shard_map/ppermute | solution.py:296
  91.9 4.9 %columns.3 = f32[64,128]{1,0:T(8,128)S(1)} custom-call(s32[8]{0:T(128)S(1)} %copy-done, s32[24]{0:T(128)S(1)} %reshape.99.slots, s32[192]{0:T(256)S(1)} %pad_add_fusion.order, f32[8,512]{1,0:T(8,128)S(1)} %get-tuple-element.65.level, f32[8,512]{1,0:T(8,128)S(1)} %get-tuple-element.70.part, f32[8,512]{1,0:T(8,128)S(1)} %get-tuple-element.69.near, ...), custom_call_target="tpu_custom_call" | custom-call | tf_op jit(solution)/shard_map/columns/pallas_call | solution.py:231
  96.8 2.1 %collective-permute-start.27 = (f32[64,128]{1,0:T(8,128)S(1)}, f32[64,128]{1,0:T(8,128)S(1)}, u32[]{:S(2)}, u32[]{:S(2)}) collective-permute-start(f32[64,128]{1,0:T(8,128)S(1)} %columns.3), channel_id=1, source_target_pairs={{0,4},{4,0},{8,12},{12,8},{16,20},{20,16},{24,28},{28,24},{32,36},... | collective-permute-start | bytes 98312 | tf_op jit(solution)/shard_map/ppermute | solution.py:31
  106.2 2.3 %collective-permute-start.32 = (f32[64,128]{1,0:T(8,128)S(1)}, f32[64,128]{1,0:T(8,128)S(1)}, u32[]{:S(2)}, u32[]{:S(2)}) collective-permute-start(f32[64,128]{1,0:T(8,128)S(1)} %add_add_fusion.3), channel_id=1, source_target_pairs={{0,64},{4,68},{8,72},{12,76},{16,80},{20,84},{24,88},{28,92},{32,9... | collective-permute-start | bytes 98312 | tf_op jit(solution)/shard_map/ppermute | solution.py:31
  111.3 2.6 %rows.2.part = f32[8,512]{1,0:T(8,128)S(1)} custom-call(s32[8]{0:T(128)S(1)} %copy-done, s32[24]{0:T(128)S(1)} %reshape.99.slots, s32[192]{0:T(256)S(1)} %pad_add_fusion.order, f32[8,512]{1,0:T(8,128)S(1)} %get-tuple-element.65.level, f32[64,128]{1,0:T(8,128)S(1)} %add_add_fusion.2.sums, f32[8,12,128,512]{3,2,1,0:T(8,128)S(1)} %get-tuple-element.60.matrix, ...), custom_call_target="tpu_custom_call" | custom-call | tf_op jit(solution)/shard_map/rows/pallas_call | solution.py:280
  114.0 3.5 %collective-permute-start.35 = (f32[8,512]{1,0:T(8,128)S(1)}, f32[8,512]{1,0:T(8,128)S(1)}, u32[]{:S(2)}, u32[]{:S(2)}) collective-permute-start(f32[8,512]{1,0:T(8,128)S(1)} %rows.2.part), channel_id=1, source_target_pairs={{0,2},{1,3},{2,0},{3,1},{4,6},{5,7},{6,4},{7,5},{8,10},{9,11},{10,... | collective-permute-start | bytes 49160 | tf_op jit(solution)/shard_map/ppermute | solution.py:296
  120.1 4.9 %columns.4 = f32[64,128]{1,0:T(8,128)S(1)} custom-call(s32[8]{0:T(128)S(1)} %copy-done, s32[24]{0:T(128)S(1)} %reshape.99.slots, s32[192]{0:T(256)S(1)} %pad_add_fusion.order, f32[8,512]{1,0:T(8,128)S(1)} %get-tuple-element.65.level, f32[8,512]{1,0:T(8,128)S(1)} %rows.2.part, f32[8,512]{1,0:T(8,128)S(1)} %collective-permute-done.34.near, ...), custom_call_target="tpu_custom_call" | custom-call | tf_op jit(solution)/shard_map/columns/pallas_call | solution.py:231
  125.0 5.9 %collective-permute-start.37 = (f32[64,128]{1,0:T(8,128)S(1)}, f32[64,128]{1,0:T(8,128)S(1)}, u32[]{:S(2)}, u32[]{:S(2)}) collective-permute-start(f32[64,128]{1,0:T(8,128)S(1)} %columns.4), channel_id=1, source_target_pairs={{0,4},{4,0},{8,12},{12,8},{16,20},{20,16},{24,28},{28,24},{32,36},... | collective-permute-start | bytes 98312 | tf_op jit(solution)/shard_map/ppermute | solution.py:31
  144.0 2.6 %rows.3.part = f32[8,512]{1,0:T(8,128)S(1)} custom-call(s32[8]{0:T(128)S(1)} %copy-done, s32[24]{0:T(128)S(1)} %reshape.99.slots, s32[192]{0:T(256)S(1)} %pad_add_fusion.order, f32[8,512]{1,0:T(8,128)S(1)} %get-tuple-element.65.level, f32[64,128]{1,0:T(8,128)S(1)} %add_add_fusion.sums, f32[8,12,128,512]{3,2,1,0:T(8,128)S(1)} %get-tuple-element.60.matrix, ...), custom_call_target="tpu_custom_call" | custom-call | tf_op jit(solution)/shard_map/rows/pallas_call | solution.py:280
  146.7 2.2 %collective-permute-start.45 = (f32[8,512]{1,0:T(8,128)S(1)}, f32[8,512]{1,0:T(8,128)S(1)}, u32[]{:S(2)}, u32[]{:S(2)}) collective-permute-start(f32[8,512]{1,0:T(8,128)S(1)} %rows.3.part), channel_id=1, source_target_pairs={{0,2},{1,3},{2,0},{3,1},{4,6},{5,7},{6,4},{7,5},{8,10},{9,11},{10,... | collective-permute-start | bytes 49160 | tf_op jit(solution)/shard_map/ppermute | solution.py:296
  151.4 5.4 %columns.5 = (f32[64,128]{1,0:T(8,128)S(1)}, f32[8,512]{1,0:T(8,128)}) custom-call(s32[8]{0:T(128)S(1)} %copy-done, s32[24]{0:T(128)S(1)} %reshape.99.slots, s32[192]{0:T(256)S(1)} %pad_add_fusion.order, f32[8,512]{1,0:T(8,128)S(1)} %get-tuple-element.65.level, f32[8,512]{1,0:T(8,128)S(1)} %rows.3.part, f32[8,512]{1,0:T(8,128)S(1)} %collective-permute-done.44.near, ...), custom_call_target="tpu_custom_call" | custom-call | tf_op jit(solution)/shard_map/columns/pallas_call | solution.py:231
  156.8 18.3 %all_to_all.5 = f32[32,2,128]{2,1,0:T(2,128)S(1)} all-to-all(f32[32,2,128]{2,1,0:T(2,128)S(1)} %bitcast.43), channel_id=1, replica_groups=mesh['row'=32,'col'=4] {'row'}, dimensions={0} | all-to-all | bytes 65536 | tf_op jit(solution)/shard_map/all_to_all | solution.py:394
  (182 shorter events, 63.5 us)
Async XLA Ops:
  1.7 17.4 %collective-permute-start.3 = (bf16[1,128,768]{2,1,0:T(8,128)(2,1)S(1)}, bf16[1,128,768]{2,1,0:T(8,128)(2,1)S(1)}, u32[]{:S(2)}, u32[]{:S(2)}) collective-permute-start(bf16[1,128,768]{2,1,0:T(8,128)(2,1)S(1)} %get-tuple-element.66), channel_id=1, source_target_pairs={{0,32},{4,36},{8,40},{12,44},{16,48},{20,52},{24,56},{28,60},{32,6... | collective-permute-start | bytes 589832 | tf_op jit(solution)/shard_map/ppermute | solution.py:31
  4.2 16.6 %collective-permute-start.4 = (bf16[1,128,768]{2,1,0:T(8,128)(2,1)S(1)}, bf16[1,128,768]{2,1,0:T(8,128)(2,1)S(1)}, u32[]{:S(2)}, u32[]{:S(2)}) collective-permute-start(bf16[1,128,768]{2,1,0:T(8,128)(2,1)S(1)} %get-tuple-element.66), channel_id=1, source_target_pairs={{0,96},{4,100},{8,104},{12,108},{16,112},{20,116},{24,120},{28,124... | collective-permute-start | bytes 589832 | tf_op jit(solution)/shard_map/ppermute | solution.py:31
  6.4 14.4 %collective-permute-start.5 = (bf16[1,128,768]{2,1,0:T(8,128)(2,1)S(1)}, bf16[1,128,768]{2,1,0:T(8,128)(2,1)S(1)}, u32[]{:S(2)}, u32[]{:S(2)}) collective-permute-start(bf16[1,128,768]{2,1,0:T(8,128)(2,1)S(1)} %get-tuple-element.66), channel_id=1, source_target_pairs={{0,64},{4,68},{8,72},{12,76},{16,80},{20,84},{24,88},{28,92},{32,9... | collective-permute-start | bytes 589832 | tf_op jit(solution)/shard_map/ppermute | solution.py:31
  7.6 13.3 %collective-permute-start = (bf16[1,128,768]{2,1,0:T(8,128)(2,1)S(1)}, bf16[1,128,768]{2,1,0:T(8,128)(2,1)S(1)}, u32[]{:S(2)}, u32[]{:S(2)}) collective-permute-start(bf16[1,128,768]{2,1,0:T(8,128)(2,1)S(1)} %get-tuple-element.67), channel_id=1, source_target_pairs={{0,8},{4,12},{8,16},{12,20},{16,24},{20,28},{24,0},{28,4},{32,40},... | collective-permute-start | bytes 589832 | tf_op jit(solution)/shard_map/ppermute | solution.py:31
  8.9 12.0 %collective-permute-start.1 = (bf16[1,128,768]{2,1,0:T(8,128)(2,1)S(1)}, bf16[1,128,768]{2,1,0:T(8,128)(2,1)S(1)}, u32[]{:S(2)}, u32[]{:S(2)}) collective-permute-start(bf16[1,128,768]{2,1,0:T(8,128)(2,1)S(1)} %get-tuple-element.67), channel_id=1, source_target_pairs={{0,24},{4,28},{8,0},{12,4},{16,8},{20,12},{24,16},{28,20},{32,56},... | collective-permute-start | bytes 589832 | tf_op jit(solution)/shard_map/ppermute | solution.py:31
  19.1 6.0 %collective-permute-start.2 = (bf16[1,128,768]{2,1,0:T(8,128)(2,1)S(1)}, bf16[1,128,768]{2,1,0:T(8,128)(2,1)S(1)}, u32[]{:S(2)}, u32[]{:S(2)}) collective-permute-start(bf16[1,128,768]{2,1,0:T(8,128)(2,1)S(1)} %get-tuple-element.67), channel_id=1, source_target_pairs={{0,16},{4,20},{8,24},{12,28},{16,0},{20,4},{24,8},{28,12},{32,48},... | collective-permute-start | bytes 589832 | tf_op jit(solution)/shard_map/ppermute | solution.py:31
  25.3 6.1 %collective-permute-start.10 = (bf16[4,128,768]{2,1,0:T(8,128)(2,1)S(1)}, bf16[4,128,768]{2,1,0:T(8,128)(2,1)S(1)}, u32[]{:S(2)}, u32[]{:S(2)}) collective-permute-start(bf16[4,128,768]{2,1,0:T(8,128)(2,1)S(1)} %pad_maximum_fusion.refs_0_), channel_id=1, source_target_pairs={{0,4},{4,0},{8,12},{12,8},{16,20},{20,16},{24,28},{28,24},{32,36},... | collective-permute-start | bytes 2359304 | tf_op jit(solution)/shard_map/ppermute | solution.py:31
  28.5 5.5 %collective-permute-start.11 = (bf16[4,128,768]{2,1,0:T(8,128)(2,1)S(1)}, bf16[4,128,768]{2,1,0:T(8,128)(2,1)S(1)}, u32[]{:S(2)}, u32[]{:S(2)}) collective-permute-start(bf16[4,128,768]{2,1,0:T(8,128)(2,1)S(1)} %pad_maximum_fusion.1.refs_1_), channel_id=1, source_target_pairs={{0,4},{4,0},{8,12},{12,8},{16,20},{20,16},{24,28},{28,24},{32,36},... | collective-permute-start | bytes 2359304 | tf_op jit(solution)/shard_map/ppermute | solution.py:31
  28.6 19.9 %collective-permute-start.6 = (bf16[4,128,768]{2,1,0:T(8,128)(2,1)S(1)}, bf16[4,128,768]{2,1,0:T(8,128)(2,1)S(1)}, u32[]{:S(2)}, u32[]{:S(2)}) collective-permute-start(bf16[4,128,768]{2,1,0:T(8,128)(2,1)S(1)} %pad_maximum_fusion.refs_0_), channel_id=1, source_target_pairs={{0,32},{4,36},{8,40},{12,44},{16,48},{20,52},{24,56},{28,60},{32,6... | collective-permute-start | bytes 2359304 | tf_op jit(solution)/shard_map/ppermute | solution.py:31
  29.3 19.2 %collective-permute-start.7 = (bf16[4,128,768]{2,1,0:T(8,128)(2,1)S(1)}, bf16[4,128,768]{2,1,0:T(8,128)(2,1)S(1)}, u32[]{:S(2)}, u32[]{:S(2)}) collective-permute-start(bf16[4,128,768]{2,1,0:T(8,128)(2,1)S(1)} %pad_maximum_fusion.refs_0_), channel_id=1, source_target_pairs={{0,96},{4,100},{8,104},{12,108},{16,112},{20,116},{24,120},{28,124... | collective-permute-start | bytes 2359304 | tf_op jit(solution)/shard_map/ppermute | solution.py:31
  31.3 19.3 %collective-permute-start.8 = (bf16[4,128,768]{2,1,0:T(8,128)(2,1)S(1)}, bf16[4,128,768]{2,1,0:T(8,128)(2,1)S(1)}, u32[]{:S(2)}, u32[]{:S(2)}) collective-permute-start(bf16[4,128,768]{2,1,0:T(8,128)(2,1)S(1)} %pad_maximum_fusion.1.refs_1_), channel_id=1, source_target_pairs={{0,8},{4,12},{8,16},{12,20},{16,24},{20,28},{24,0},{28,4},{32,40},... | collective-permute-start | bytes 2359304 | tf_op jit(solution)/shard_map/ppermute | solution.py:31
  31.4 19.2 %collective-permute-start.9 = (bf16[4,128,768]{2,1,0:T(8,128)(2,1)S(1)}, bf16[4,128,768]{2,1,0:T(8,128)(2,1)S(1)}, u32[]{:S(2)}, u32[]{:S(2)}) collective-permute-start(bf16[4,128,768]{2,1,0:T(8,128)(2,1)S(1)} %pad_maximum_fusion.1.refs_1_), channel_id=1, source_target_pairs={{0,24},{4,28},{8,0},{12,4},{16,8},{20,12},{24,16},{28,20},{32,56},... | collective-permute-start | bytes 2359304 | tf_op jit(solution)/shard_map/ppermute | solution.py:31
  53.0 6.3 %collective-permute-start.19 = (bf16[4,128,768]{2,1,0:T(8,128)(2,1)S(1)}, bf16[4,128,768]{2,1,0:T(8,128)(2,1)S(1)}, u32[]{:S(2)}, u32[]{:S(2)}) collective-permute-start(bf16[4,128,768]{2,1,0:T(8,128)(2,1)S(1)} %collective-permute-done.9.refs_3_), channel_id=1, source_target_pairs={{0,4},{4,0},{8,12},{12,8},{16,20},{20,16},{24,28},{28,24},{32,36},... | collective-permute-start | bytes 2359304 | tf_op jit(solution)/shard_map/ppermute | solution.py:31
  53.3 17.0 %collective-permute-start.12 = (bf16[2,128,768]{2,1,0:T(8,128)(2,1)S(1)}, bf16[2,128,768]{2,1,0:T(8,128)(2,1)S(1)}, u32[]{:S(2)}, u32[]{:S(2)}) collective-permute-start(bf16[2,128,768]{2,1,0:T(8,128)(2,1)S(1)} %slice.49), channel_id=1, source_target_pairs={{0,32},{4,36},{8,40},{12,44},{16,48},{20,52},{24,56},{28,60},{32,6... | collective-permute-start | bytes 1179656 | tf_op jit(solution)/shard_map/ppermute | solution.py:31
  54.5 15.9 %collective-permute-start.13 = (bf16[2,128,768]{2,1,0:T(8,128)(2,1)S(1)}, bf16[2,128,768]{2,1,0:T(8,128)(2,1)S(1)}, u32[]{:S(2)}, u32[]{:S(2)}) collective-permute-start(bf16[2,128,768]{2,1,0:T(8,128)(2,1)S(1)} %slice.50), channel_id=1, source_target_pairs={{0,96},{4,100},{8,104},{12,108},{16,112},{20,116},{24,120},{28,124... | collective-permute-start | bytes 1179656 | tf_op jit(solution)/shard_map/ppermute | solution.py:31
  56.0 14.3 %collective-permute-start.14 = (bf16[2,128,768]{2,1,0:T(8,128)(2,1)S(1)}, bf16[2,128,768]{2,1,0:T(8,128)(2,1)S(1)}, u32[]{:S(2)}, u32[]{:S(2)}) collective-permute-start(bf16[2,128,768]{2,1,0:T(8,128)(2,1)S(1)} %slice.51), channel_id=1, source_target_pairs={{0,8},{4,12},{8,16},{12,20},{16,24},{20,28},{24,0},{28,4},{32,40},... | collective-permute-start | bytes 1179656 | tf_op jit(solution)/shard_map/ppermute | solution.py:31
  56.7 13.6 %collective-permute-start.15 = (bf16[2,128,768]{2,1,0:T(8,128)(2,1)S(1)}, bf16[2,128,768]{2,1,0:T(8,128)(2,1)S(1)}, u32[]{:S(2)}, u32[]{:S(2)}) collective-permute-start(bf16[2,128,768]{2,1,0:T(8,128)(2,1)S(1)} %slice.52), channel_id=1, source_target_pairs={{0,24},{4,28},{8,0},{12,4},{16,8},{20,12},{24,16},{28,20},{32,56},... | collective-permute-start | bytes 1179656 | tf_op jit(solution)/shard_map/ppermute | solution.py:31
  85.1 4.9 %collective-permute-start.24 = (f32[2,8,512]{2,1,0:T(8,128)S(1)}, f32[2,8,512]{2,1,0:T(8,128)S(1)}, u32[]{:S(2)}, u32[]{:S(2)}) collective-permute-start(f32[2,8,512]{2,1,0:T(8,128)S(1)} %pad_maximum_fusion.2), channel_id=1, source_target_pairs={{0,1},{1,2},{2,3},{3,0},{4,5},{5,6},{6,7},{7,4},{8,9},{9,10},{10,1... | collective-permute-start | bytes 98312 | tf_op jit(solution)/shard_map/ppermute | solution.py:296
  86.4 4.5 %collective-permute-start.25 = (f32[2,8,512]{2,1,0:T(8,128)S(1)}, f32[2,8,512]{2,1,0:T(8,128)S(1)}, u32[]{:S(2)}, u32[]{:S(2)}) collective-permute-start(f32[2,8,512]{2,1,0:T(8,128)S(1)} %pad_maximum_fusion.2), channel_id=1, source_target_pairs={{0,2},{1,3},{2,0},{3,1},{4,6},{5,7},{6,4},{7,5},{8,10},{9,11},{10,... | collective-permute-start | bytes 98312 | tf_op jit(solution)/shard_map/ppermute | solution.py:296
  99.8 4.7 %collective-permute-start.28 = (f32[64,128]{1,0:T(8,128)S(1)}, f32[64,128]{1,0:T(8,128)S(1)}, u32[]{:S(2)}, u32[]{:S(2)}) collective-permute-start(f32[64,128]{1,0:T(8,128)S(1)} %add.132), channel_id=1, source_target_pairs={{0,8},{4,12},{8,16},{12,20},{16,24},{20,28},{24,0},{28,4},{32,40},... | collective-permute-start | bytes 98312 | tf_op jit(solution)/shard_map/ppermute | solution.py:31
  106.2 4.3 %collective-permute-start.32 = (f32[64,128]{1,0:T(8,128)S(1)}, f32[64,128]{1,0:T(8,128)S(1)}, u32[]{:S(2)}, u32[]{:S(2)}) collective-permute-start(f32[64,128]{1,0:T(8,128)S(1)} %add_add_fusion.3), channel_id=1, source_target_pairs={{0,64},{4,68},{8,72},{12,76},{16,80},{20,84},{24,88},{28,92},{32,9... | collective-permute-start | bytes 98312 | tf_op jit(solution)/shard_map/ppermute | solution.py:31
  114.0 4.8 %collective-permute-start.35 = (f32[8,512]{1,0:T(8,128)S(1)}, f32[8,512]{1,0:T(8,128)S(1)}, u32[]{:S(2)}, u32[]{:S(2)}) collective-permute-start(f32[8,512]{1,0:T(8,128)S(1)} %rows.2.part), channel_id=1, source_target_pairs={{0,2},{1,3},{2,0},{3,1},{4,6},{5,7},{6,4},{7,5},{8,10},{9,11},{10,... | collective-permute-start | bytes 49160 | tf_op jit(solution)/shard_map/ppermute | solution.py:296
  125.0 6.8 %collective-permute-start.37 = (f32[64,128]{1,0:T(8,128)S(1)}, f32[64,128]{1,0:T(8,128)S(1)}, u32[]{:S(2)}, u32[]{:S(2)}) collective-permute-start(f32[64,128]{1,0:T(8,128)S(1)} %columns.4), channel_id=1, source_target_pairs={{0,4},{4,0},{8,12},{12,8},{16,20},{20,16},{24,28},{28,24},{32,36},... | collective-permute-start | bytes 98312 | tf_op jit(solution)/shard_map/ppermute | solution.py:31
  133.5 4.3 %collective-permute-start.39 = (f32[64,128]{1,0:T(8,128)S(1)}, f32[64,128]{1,0:T(8,128)S(1)}, u32[]{:S(2)}, u32[]{:S(2)}) collective-permute-start(f32[64,128]{1,0:T(8,128)S(1)} %add.139), channel_id=1, source_target_pairs={{0,16},{4,20},{8,24},{12,28},{16,0},{20,4},{24,8},{28,12},{32,48},... | collective-permute-start | bytes 98312 | tf_op jit(solution)/shard_map/ppermute | solution.py:31
  (44 other events, 199.9 us)

commit v4 on v3

--- a/solution.py
+++ b/solution.py
@@ -39,9 +39,8 @@
     return lax.optimization_barrier(arrays)
 
 
-def ring_gather(own, dz, dy):
-    parts = [own, send(own, dz, dy, 0), send(own, -dz, -dy, 0), send(own, 2 * dz, 2 * dy, 0)]
-    return jnp.concatenate(parts, axis=0)
+def ring_sends(own, dz, dy):
+    return [send(own, dz, dy, 0), send(own, -dz, -dy, 0), send(own, 2 * dz, 2 * dy, 0)]
 
 
 def piece_layout():
@@ -84,7 +83,8 @@
             pieces[piece].at[index], held.at[pl.ds(entry * rows, rows)], fetch_sems.at[entry]
         )
 
-    for position, (piece, index, *_) in enumerate(layout):
+    offset = sum(len(entries) for entries in piece_layout()[:stage])
+    for position, (piece, index, *_) in enumerate(layout, offset):
 
         @pl.when(dest[position] >= 0)
         def _():
@@ -193,31 +193,38 @@
     for s in range(blocks):
         weights[s] = jnp.exp2(peaks[s] - level[s : s + 1, :]) * inverse[s : s + 1, :]
     sums_out[...] = jnp.zeros_like(sums_out)
+    lanes = block_rows // 128
+
     for g in range(blocks // SHARE):
 
         def one_entry(k, carry):
-            columns[...] = jnp.zeros_like(columns)
-            for m in range(SHARE):
-                s = g * SHARE + m
-
-                @pl.when(order[(blocks + s) * listed + k] > 0)
-                def _():
-                    w = weights[s, pl.ds(k, 1), :]
-                    spread = [
-                        jnp.broadcast_to(w[:, 128 * l : 128 * l + 128], (8, 128))
-                        for l in range(block_rows // 128)
-                    ]
-                    for j in range(0, rows, 8):
-                        piece = columns[j : j + 8, :]
-                        for l, ws in enumerate(spread):
-                            piece = piece + matrix[s, k, j : j + 8, 128 * l : 128 * l + 128] * ws
-                        columns[j : j + 8, :] = piece
-
-            row = jnp.sum(columns[...].T, axis=0, keepdims=True)
-            sums_out[pl.ds(slots[g * listed + k], 1), :] = row
+            def one_source(s, acc):
+                w = weights[s, pl.ds(k, 1), :]
+                spread = [jnp.broadcast_to(w[:, 128 * l : 128 * l + 128], (8, 128)) for l in range(lanes)]
+                return tuple(
+                    sum((matrix[s, k, 8 * j : 8 * j + 8, 128 * l : 128 * l + 128] * spread[l] for l in range(lanes)), a)
+                    for j, a in enumerate(acc)
+                )
+
+            acc = tuple(jnp.zeros((8, 128), jnp.float32) for _ in range(rows // 8))
+            for s in range(g * SHARE, (g + 1) * SHARE):
+                live = order[(blocks + s) * listed + k] > 0
+                acc = lax.cond(live, functools.partial(one_source, s), lambda acc: acc, acc)
+            for j, a in enumerate(acc):
+                columns[g * listed + k, 8 * j : 8 * j + 8, :] = a
             return carry
 
         lax.fori_loop(0, listed, one_entry, 0)
+
+    lane = lax.broadcasted_iota(jnp.int32, (8, 128), 1)
+    merged = [jnp.zeros((8, 128), jnp.float32)] * (rows // 8)
+    for e in range(2 * listed):
+        for j in range(rows // 8):
+            one = jnp.sum(columns[e, 8 * j : 8 * j + 8, :], axis=1, keepdims=True)
+            merged[j] = jnp.where(lane == e, one, merged[j])
+    by_entry = jnp.concatenate(merged, axis=0).T
+    for e in range(2 * listed):
+        sums_out[pl.ds(slots[e], 1), :] = by_entry[e : e + 1, :]
 
 
 def column_pass(final, counts, slots, order, targets, level, parts, matrix, peaks):
@@ -235,7 +242,7 @@
         out_shape=out_shape,
         scratch_shapes=[
             pltpu.VMEM(peaks.shape, jnp.float32),
-            pltpu.VMEM((rows, 128), jnp.float32),
+            pltpu.VMEM((2 * matrix.shape[1], rows, 128), jnp.float32),
         ],
         compiler_params=pltpu.CompilerParams(vmem_limit_bytes=8 * MIB),
         name="columns",
@@ -302,42 +309,70 @@
     return x + send(x, 1, 0, 0) + send(x, 2, 0, 0) + send(x, 3, 0, 0)
 
 
+def tables_kernel(target_blocks, me, pairs, counts, owners, slots, dest, segments, lives, order, listing):
+    blocks, listed = pairs.shape
+    starts = np.cumsum([0] + [len(stage) for stage in piece_layout()])
+    z, y, core = me[0] // 8, (me[0] // 2) % 4, me[0] % 2
+    for n in range(int(starts[-1])):
+        dest[n] = -1
+    for g in range(blocks // SHARE):
+        found = []
+        for k in range(listed):
+            slot = owners[pairs[g * SHARE, k]]
+            owner, which = slot // target_blocks, slot % target_blocks
+            dz = (owner // 8 - z + 4) % 4
+            dy = ((owner // 2) % 4 - y + 4) % 4
+            other = jnp.where(owner % 2 == core, 0, 1)
+            across = jnp.where(which == 0, dz, dy)
+            along = jnp.where(which == 0, dy, dz)
+            stage = jnp.where(across == 0, 0, jnp.where(across == 2, 2, 1))
+            index = jnp.where(along == 0, 0, jnp.where(along == 3, 1, along + 1))
+            set_at = other * 2 + which
+            near = 2 * set_at + jnp.where(across == 3, 0, 1)
+            position = index + 4 * jnp.where(stage == 1, near, set_at)
+            base = jnp.where(stage == 0, int(starts[0]), jnp.where(stage == 1, int(starts[1]), int(starts[2])))
+            found.append((slot, stage, base + position))
+        following = []
+        begin = jnp.int32(0)
+        for stage in range(STAGES):
+            segments[g * (STAGES + 1) + stage] = begin
+            following.append(begin)
+            begin = begin + sum(jnp.where(f[1] == stage, 1, 0) for f in found)
+        segments[g * (STAGES + 1) + STAGES] = begin
+        for k, (slot, stage, position) in enumerate(found):
+            place = jnp.where(stage == 0, following[0], jnp.where(stage == 1, following[1], following[2]))
+            following = [f + jnp.where(stage == n, 1, 0) for n, f in enumerate(following)]
+            slots[g * listed + place] = slot
+            dest[position] = g * listed + place
+            listing[place] = k
+        for s in range(g * SHARE, (g + 1) * SHARE):
+            count = counts[s]
+            for stage in range(STAGES):
+                lives[s * STAGES + stage] = sum(
+                    jnp.where((f[1] == stage) & (k < count), 1, 0) for k, f in enumerate(found)
+                )
+            turn = jnp.int32(0)
+            for place in range(listed):
+                live = jnp.where(listing[place] < count, 1, 0)
+                order[s * listed + turn] = place
+                order[(blocks + s) * listed + place] = live
+                turn = turn + live
+
+
 def tables(pair_list, counts, owner_map, target_blocks):
     blocks, listed = pair_list.shape
-    groups = blocks // SHARE
-    targets = owner_map.shape[0]
-    lead = pair_list.reshape(groups, SHARE, listed)[:, 0, :]
-    lookup = lead[:, :, None] == jnp.arange(targets, dtype=jnp.int32)
-    stored = jnp.sum(jnp.where(lookup, owner_map, 0), axis=2)
-    me = lax.axis_index("row")
-    z, y, core = me // 8, (me // 2) % 4, me % 2
-    stages = piece_layout()
-    layout = np.array([entry for stage in stages for entry in stage], np.int32)
-    stage_at = np.array([n for n, stage in enumerate(stages) for _ in stage], np.int32)
-    owner = (((z + layout[:, 2]) % 4) * 4 + (y + layout[:, 3]) % 4) * 2 + (core ^ layout[:, 4])
-    held_slot = owner * target_blocks + layout[:, 5]
-    match = held_slot[:, None, None] == stored[None]
-    stage_of = jnp.sum(jnp.where(match, stage_at[:, None, None], 0), axis=0)
-    ids = jnp.arange(listed, dtype=jnp.int32)
-    rank = stage_of * listed + ids
-    place = jnp.sum((rank[:, None, :] < rank[:, :, None]).astype(jnp.int32), axis=2)
-    offset = jnp.arange(groups, dtype=jnp.int32)[:, None] * listed
-    dest = jnp.sum(jnp.where(match, offset + place + 1, 0), axis=(1, 2)) - 1
-    bounds = jnp.arange(STAGES + 1, dtype=jnp.int32)
-    segments = jnp.sum((stage_of[:, None, :] < bounds[:, None]).astype(jnp.int32), axis=2)
-    alive = ids[None, :] < counts[:, None]
-    stage_rows = jnp.repeat(stage_of, SHARE, axis=0)
-    lives = jnp.sum((alive[:, None, :] & (stage_rows[:, None, :] == bounds[:STAGES, None])).astype(jnp.int32), axis=2)
-    at_place = place[:, None, :] == ids[None, :, None]
-    slots = jnp.sum(jnp.where(at_place, stored[:, None, :], 0), axis=2)
-    alive_at = jnp.any(jnp.repeat(at_place, SHARE, axis=0) & alive[:, None, :], axis=2)
-    turn = jnp.sum((alive_at[:, None, :] & (ids[None, :] < ids[:, None])[None]).astype(jnp.int32), axis=2)
-    order = jnp.sum(
-        jnp.where(alive_at[:, None, :] & (turn[:, None, :] == ids[None, :, None]), ids[None, None, :], 0), axis=2
-    )
-    order = jnp.concatenate([order.reshape(-1), alive_at.astype(jnp.int32).reshape(-1)])
-    cuts = np.cumsum([len(stage) for stage in stages])[:-1]
-    return slots.reshape(-1), jnp.split(dest, cuts), segments.reshape(-1), lives.reshape(-1), order
+    entries = blocks // SHARE * listed
+    me = jnp.reshape(lax.axis_index("row"), (1,)).astype(jnp.int32)
+    smem = pl.BlockSpec(memory_space=pltpu.SMEM)
+    sizes = (entries, owner_map.shape[0], blocks // SHARE * (STAGES + 1), blocks * STAGES, 2 * blocks * listed)
+    return pl.pallas_call(
+        functools.partial(tables_kernel, target_blocks),
+        in_specs=[smem] * 4,
+        out_specs=[smem] * 5,
+        out_shape=[jax.ShapeDtypeStruct((size,), jnp.int32) for size in sizes],
+        scratch_shapes=[pltpu.SMEM((listed,), jnp.int32)],
+        name="tables",
+    )(me, pair_list, counts, owner_map)
 
 
 def shards(source_vectors, target_vectors, pair_list, counts, owner_map):
@@ -353,12 +388,13 @@
 
     def stage(number, pieces, earlier):
         return score_stage(
-            number, listed, dest[number], segments, lives, source_vectors, across(pieces), earlier
+            number, listed, dest, segments, lives, source_vectors, across(pieces), earlier
         )
 
-    first = [ring_gather(target_vectors[:1], 0, 1), ring_gather(target_vectors[1:], 1, 0)]
-    *first, slots, segments, lives, order, early, later, latest = tie(*first, slots, segments, lives, order, *dest)
-    dest = [early, later, latest]
+    along_y, along_z = target_vectors[:1], target_vectors[1:]
+    arrived = ring_sends(along_y, 0, 1) + ring_sends(along_z, 1, 0)
+    *arrived, slots, dest, segments, lives, order = tie(*arrived, slots, dest, segments, lives, order)
+    first = [jnp.concatenate([along_y] + arrived[:3], axis=0), jnp.concatenate([along_z] + arrived[3:], axis=0)]
     second = [
         send(first[0], 1, 0, 0),
         send(first[0], -1, 0, 0),

time: 176 us -> 167 us (0.949)
  other arithmetic: 6.75 us -> 0.91 us
  starting transfers between devices: 63.7 us -> 59.6 us
  Pallas kernels: 48.5 us -> 50.5 us
  blocking collectives: 18.3 us -> 16.3 us
    pallas_call x3, Pallas kernels: 15.1 us -> 10.5 us  [column_pass(): pl.pallas_call(functools.partial(column_kernel, final), in_specs=[smem] *...]
    ppermute x38, starting transfers between devices: 51.8 us -> 47.7 us  [send(): return lax.ppermute(x, 'row', row_perm(dz, dy, dc))]
    reduce_sum x9 -> x0, other arithmetic: 3.69 us -> none  [the longest x1 1 us: tables(): stage_of = jnp.sum(jnp.where(match, stage_at[:, None, None], 0), axis=0)]
    unnamed x42 -> x58, local copies, waits for them, and re-layouts: 2.53 us -> 5.65 us
    pallas_call x0 -> x1, Pallas kernels: none -> 3.02 us  [tables(): pl.pallas_call(functools.partial(tables_kernel, target_blocks), in_specs=...]
    pallas_call x3, Pallas kernels: 28.2 us -> 30.6 us  [score_stage(): pl.pallas_call(functools.partial(score_kernel, stage, listed), in_specs=[...]
    all_to_all x1, blocking collectives: 18.3 us -> 16.3 us  [shards(): lax.all_to_all(sums.reshape(row_count, target_blocks, quarter), 'row', sp...]
  transfers between devices with their start and end apart: 47 -> 47, of which waited for: 29 -> 30; matrix products, arithmetic and copies ran while one was open for 5% -> 0% of each run, Pallas kernels for 11% -> 13%
where the time goes in v4:
time: 167 us; the launch traced here: 166 us
  starting transfers between devices  59.6 us (36%)
  Pallas kernels  50.5 us (30%)
  waiting for transfers between devices  30.9 us (19%)
  blocking collectives  16.3 us (10%)
  local copies, waits for them, and re-layouts  6.81 us (4%)
    ppermute x38, starting transfers between devices, send(): return lax.ppermute(x, 'row', row_perm(dz, dy, dc))  47.7 us
    pallas_call x3, Pallas kernels, score_stage(): pl.pallas_call(functools.partial(score_kernel, stage, listed), in_specs=[...  30.6 us
    ppermute x38, waiting for transfers between devices, send(): return lax.ppermute(x, 'row', row_perm(dz, dy, dc))  25 us
    all_to_all x1, blocking collectives, shards(): lax.all_to_all(sums.reshape(row_count, target_blocks, quarter), 'row', sp...  16.3 us
    ppermute x9, starting transfers between devices, from_columns(): lax.ppermute(x, 'col', [(i, (i + d) % 4) for i in range(4)])  11.9 us
    pallas_call x3, Pallas kernels, column_pass(): pl.pallas_call(functools.partial(column_kernel, final), in_specs=[smem] *...  10.5 us
    pallas_call x2, Pallas kernels, row_pass(): pl.pallas_call(row_kernel, in_specs=[smem] * 3 + [vmem] * 4, out_specs=vm...  6.45 us
    ppermute x9, waiting for transfers between devices, from_columns(): lax.ppermute(x, 'col', [(i, (i + d) % 4) for i in range(4)])  5.9 us
  transfers between devices with their start and end apart: 47, of which 30 were waited for; matrix products, arithmetic and copies ran while one was open for 0% of the time, Pallas kernels for 13%

profile of v4, /device:TPU:1, one launch (start us, length us, event | category | flops | bytes accessed | tf_op | source)
XLA Modules:
  0.0 166.1 jit_solution(8715586611325708760)
XLA Ops:
  10.7 2.6 %collective-permute-start.5 = (bf16[1,128,768]{2,1,0:T(8,128)(2,1)S(1)}, bf16[1,128,768]{2,1,0:T(8,128)(2,1)S(1)}, u32[]{:S(2)}, u32[]{:S(2)}) collective-permute-start(bf16[1,128,768]{2,1,0:T(8,128)(2,1)S(1)} %get-tuple-element.80), channel_id=1, source_target_pairs={{0,64},{4,68},{8,72},{12,76},{16,80},{20,84},{24,88},{28,92},{32,9... | collective-permute-start | bytes 589832 | tf_op jit(solution)/shard_map/ppermute | solution.py:31
  13.3 3.0 %tables.1 = (s32[24]{0:T(128)}, s32[64]{0:T(128)}, s32[8]{0:T(128)}, s32[24]{0:T(128)}, s32[192]{0:T(256)}) custom-call(s32[1]{0:T(128)} %bitcast.me, s32[8,12]{1,0:T(8,128)} %pairs.1, s32[8]{0:T(128)} %counts.11, s32[64]{0:T(128)} %owners.1), custom_call_target="tpu_custom_call" | custom-call | tf_op jit(solution)/shard_map/tables/pallas_call | solution.py:368
  16.4 3.2 %collective-permute-done.5 = bf16[1,128,768]{2,1,0:T(8,128)(2,1)S(1)} collective-permute-done((bf16[1,128,768]{2,1,0:T(8,128)(2,1)S(1)}, bf16[1,128,768]{2,1,0:T(8,128)(2,1)S(1)}, u32[]{:S(2)}, u32[]{:S(2)}) %collective-permute-start.5) | collective-permute-done | bytes 196640 | tf_op jit(solution)/shard_map/ppermute | solution.py:31
  19.6 2.5 %collective-permute-start.11 = (bf16[4,128,768]{2,1,0:T(8,128)(2,1)S(1)}, bf16[4,128,768]{2,1,0:T(8,128)(2,1)S(1)}, u32[]{:S(2)}, u32[]{:S(2)}) collective-permute-start(bf16[4,128,768]{2,1,0:T(8,128)(2,1)S(1)} %pad_maximum_fusion.1.refs_1_), channel_id=1, source_target_pairs={{0,4},{4,0},{8,12},{12,8},{16,20},{20,16},{24,28},{28,24},{32,36},... | collective-permute-start | bytes 2359304 | tf_op jit(solution)/shard_map/ppermute | solution.py:31
  22.8 2.3 %collective-permute-start.9 = (bf16[4,128,768]{2,1,0:T(8,128)(2,1)S(1)}, bf16[4,128,768]{2,1,0:T(8,128)(2,1)S(1)}, u32[]{:S(2)}, u32[]{:S(2)}) collective-permute-start(bf16[4,128,768]{2,1,0:T(8,128)(2,1)S(1)} %pad_maximum_fusion.1.refs_1_), channel_id=1, source_target_pairs={{0,24},{4,28},{8,0},{12,4},{16,8},{20,12},{24,16},{28,20},{32,56},... | collective-permute-start | bytes 2359304 | tf_op jit(solution)/shard_map/ppermute | solution.py:31
  30.6 7.6 %scores.3 = (f32[8,12,128,512]{3,2,1,0:T(8,128)S(1)}, f32[8,16,512]{2,1,0:T(8,128)S(1)}, f32[8,16,512]{2,1,0:T(8,128)S(1)}) custom-call(s32[64]{0:T(128)S(1)} %copy-done.3, s32[8]{0:T(128)S(1)} %copy-done.5, s32[24]{0:T(128)S(1)} %copy-done.7, bf16[8,512,768]{2,1,0:T(8,128)(2,1)} %source.5, bf16[4,128,768]{2,1,0:T(8,128)(2,1)} %copy-done.10, ...), custom_call_target="tpu_custom_call" | custom-call | flops 2415919104 | bytes 6291456 | tf_op jit(solution)/shard_map/scores/pallas_call | solution.py:162
  38.2 4.1 %collective-permute-done.8.refs_2_ = bf16[4,128,768]{2,1,0:T(8,128)(2,1)S(1)} collective-permute-done((bf16[4,128,768]{2,1,0:T(8,128)(2,1)S(1)}, bf16[4,128,768]{2,1,0:T(8,128)(2,1)S(1)}, u32[]{:S(2)}, u32[]{:S(2)}) %collective-permute-start.8) | collective-permute-done | bytes 786464 | tf_op jit(solution)/shard_map/ppermute | solution.py:31
  48.3 2.6 %collective-permute-start.13 = (bf16[2,128,768]{2,1,0:T(8,128)(2,1)S(1)}, bf16[2,128,768]{2,1,0:T(8,128)(2,1)S(1)}, u32[]{:S(2)}, u32[]{:S(2)}) collective-permute-start(bf16[2,128,768]{2,1,0:T(8,128)(2,1)S(1)} %slice.42), channel_id=1, source_target_pairs={{0,96},{4,100},{8,104},{12,108},{16,112},{20,116},{24,120},{28,124... | collective-permute-start | bytes 1179656 | tf_op jit(solution)/shard_map/ppermute | solution.py:31
  51.3 2.3 %collective-permute-start.15 = (bf16[2,128,768]{2,1,0:T(8,128)(2,1)S(1)}, bf16[2,128,768]{2,1,0:T(8,128)(2,1)S(1)}, u32[]{:S(2)}, u32[]{:S(2)}) collective-permute-start(bf16[2,128,768]{2,1,0:T(8,128)(2,1)S(1)} %slice.44), channel_id=1, source_target_pairs={{0,24},{4,28},{8,0},{12,4},{16,8},{20,12},{24,16},{28,20},{32,56},... | collective-permute-start | bytes 1179656 | tf_op jit(solution)/shard_map/ppermute | solution.py:31
  55.7 11.7 %scores.4 = (f32[8,12,128,512]{3,2,1,0:T(8,128)S(1)}, f32[8,16,512]{2,1,0:T(8,128)S(1)}, f32[8,16,512]{2,1,0:T(8,128)S(1)}) custom-call(s32[64]{0:T(128)S(1)} %copy-done.4, s32[8]{0:T(128)S(1)} %copy-done.6, s32[24]{0:T(128)S(1)} %copy-done.7, bf16[8,512,768]{2,1,0:T(8,128)(2,1)} %source.5, ...), custom_call_target="tpu_custom_call", output_to_operand_aliasing={{0}: (12, {}), {1}: (13, {}), {2}: (14, {})} | custom-call | flops 4831838208 | bytes 12582912 | tf_op jit(solution)/shard_map/scores/pallas_call | solution.py:162
  72.6 11.2 %scores.5 = (f32[8,12,128,512]{3,2,1,0:T(8,128)S(1)}, f32[8,16,512]{2,1,0:T(8,128)S(1)}, f32[8,16,512]{2,1,0:T(8,128)S(1)}, f32[8,512]{1,0:T(8,128)S(1)}, f32[8,512]{1,0:T(8,128)S(1)}) custom-call(s32[64]{0:T(128)S(1)} %copy-done.4, s32[8]{0:T(128)S(1)} %copy-done.6, s32[24]{0:T(128)S(1)} %copy-done.8, ...), custom_call_target="tpu_custom_call", output_to_operand_aliasing={{0}: (12, {}), {1}: (13, {}), {2}: (14, {})} | custom-call | flops 2415919104 | bytes 6291456 | tf_op jit(solution)/shard_map/scores/pallas_call | solution.py:162
  85.2 2.5 %collective-permute-start.25 = (f32[2,8,512]{2,1,0:T(8,128)S(1)}, f32[2,8,512]{2,1,0:T(8,128)S(1)}, u32[]{:S(2)}, u32[]{:S(2)}) collective-permute-start(f32[2,8,512]{2,1,0:T(8,128)S(1)} %pad_maximum_fusion.2), channel_id=1, source_target_pairs={{0,2},{1,3},{2,0},{3,1},{4,6},{5,7},{6,4},{7,5},{8,10},{9,11},{10,... | collective-permute-start | bytes 98312 | tf_op jit(solution)/shard_map/ppermute | solution.py:303
  90.5 3.5 %columns.3 = f32[64,128]{1,0:T(8,128)S(1)} custom-call(s32[8]{0:T(128)S(1)} %copy-done.1, s32[24]{0:T(128)S(1)} %copy-done.2, s32[192]{0:T(256)S(1)} %copy-done, f32[8,512]{1,0:T(8,128)S(1)} %get-tuple-element.79.level, f32[8,512]{1,0:T(8,128)S(1)} %get-tuple-element.84.part, f32[8,512]{1,0:T(8,128)S(1)} %get-tuple-element.83.near, ...), custom_call_target="tpu_custom_call" | custom-call | tf_op jit(solution)/shard_map/columns/pallas_call | solution.py:238
  95.4 2.5 %collective-permute-start.30 = (f32[64,128]{1,0:T(8,128)S(1)}, f32[64,128]{1,0:T(8,128)S(1)}, u32[]{:S(2)}, u32[]{:S(2)}) collective-permute-start(f32[64,128]{1,0:T(8,128)S(1)} %add.48), channel_id=1, source_target_pairs={{0,24},{4,28},{8,0},{12,4},{16,8},{20,12},{24,16},{28,20},{32,56},... | collective-permute-start | bytes 98312 | tf_op jit(solution)/shard_map/ppermute | solution.py:31
  105.5 3.2 %rows.2.part = f32[8,512]{1,0:T(8,128)S(1)} custom-call(s32[8]{0:T(128)S(1)} %copy-done.1, s32[24]{0:T(128)S(1)} %copy-done.2, s32[192]{0:T(256)S(1)} %copy-done, f32[8,512]{1,0:T(8,128)S(1)} %get-tuple-element.79.level, f32[64,128]{1,0:T(8,128)S(1)} %add_add_fusion.2.sums, f32[8,12,128,512]{3,2,1,0:T(8,128)S(1)} %get-tuple-element.74.matrix, ...), custom_call_target="tpu_custom_call" | custom-call | tf_op jit(solution)/shard_map/rows/pallas_call | solution.py:287
  109.1 3.3 %collective-permute-start.35 = (f32[8,512]{1,0:T(8,128)S(1)}, f32[8,512]{1,0:T(8,128)S(1)}, u32[]{:S(2)}, u32[]{:S(2)}) collective-permute-start(f32[8,512]{1,0:T(8,128)S(1)} %rows.2.part), channel_id=1, source_target_pairs={{0,2},{1,3},{2,0},{3,1},{4,6},{5,7},{6,4},{7,5},{8,10},{9,11},{10,... | collective-permute-start | bytes 49160 | tf_op jit(solution)/shard_map/ppermute | solution.py:303
  114.9 3.5 %columns.4 = f32[64,128]{1,0:T(8,128)S(1)} custom-call(s32[8]{0:T(128)S(1)} %copy-done.1, s32[24]{0:T(128)S(1)} %copy-done.2, s32[192]{0:T(256)S(1)} %copy-done, f32[8,512]{1,0:T(8,128)S(1)} %get-tuple-element.79.level, f32[8,512]{1,0:T(8,128)S(1)} %rows.2.part, f32[8,512]{1,0:T(8,128)S(1)} %collective-permute-done.34.near, ...), custom_call_target="tpu_custom_call" | custom-call | tf_op jit(solution)/shard_map/columns/pallas_call | solution.py:238
  118.4 4.5 %collective-permute-start.37 = (f32[64,128]{1,0:T(8,128)S(1)}, f32[64,128]{1,0:T(8,128)S(1)}, u32[]{:S(2)}, u32[]{:S(2)}) collective-permute-start(f32[64,128]{1,0:T(8,128)S(1)} %columns.4), channel_id=1, source_target_pairs={{0,4},{4,0},{8,12},{12,8},{16,20},{20,16},{24,28},{28,24},{32,36},... | collective-permute-start | bytes 98312 | tf_op jit(solution)/shard_map/ppermute | solution.py:31
  124.6 2.7 %collective-permute-start.39 = (f32[64,128]{1,0:T(8,128)S(1)}, f32[64,128]{1,0:T(8,128)S(1)}, u32[]{:S(2)}, u32[]{:S(2)}) collective-permute-start(f32[64,128]{1,0:T(8,128)S(1)} %add.55), channel_id=1, source_target_pairs={{0,16},{4,20},{8,24},{12,28},{16,0},{20,4},{24,8},{28,12},{32,48},... | collective-permute-start | bytes 98312 | tf_op jit(solution)/shard_map/ppermute | solution.py:31
  131.4 3.1 %collective-permute-start.42 = (f32[64,128]{1,0:T(8,128)S(1)}, f32[64,128]{1,0:T(8,128)S(1)}, u32[]{:S(2)}, u32[]{:S(2)}) collective-permute-start(f32[64,128]{1,0:T(8,128)S(1)} %add_add_fusion.1), channel_id=1, source_target_pairs={{0,64},{4,68},{8,72},{12,76},{16,80},{20,84},{24,88},{28,92},{32,9... | collective-permute-start | bytes 98312 | tf_op jit(solution)/shard_map/ppermute | solution.py:31
  137.3 3.2 %rows.3.part = f32[8,512]{1,0:T(8,128)S(1)} custom-call(s32[8]{0:T(128)S(1)} %copy-done.1, s32[24]{0:T(128)S(1)} %copy-done.2, s32[192]{0:T(256)S(1)} %copy-done, f32[8,512]{1,0:T(8,128)S(1)} %get-tuple-element.79.level, f32[64,128]{1,0:T(8,128)S(1)} %add_add_fusion.sums, f32[8,12,128,512]{3,2,1,0:T(8,128)S(1)} %get-tuple-element.74.matrix, ...), custom_call_target="tpu_custom_call" | custom-call | tf_op jit(solution)/shard_map/rows/pallas_call | solution.py:287
  140.6 2.4 %collective-permute-start.45 = (f32[8,512]{1,0:T(8,128)S(1)}, f32[8,512]{1,0:T(8,128)S(1)}, u32[]{:S(2)}, u32[]{:S(2)}) collective-permute-start(f32[8,512]{1,0:T(8,128)S(1)} %rows.3.part), channel_id=1, source_target_pairs={{0,2},{1,3},{2,0},{3,1},{4,6},{5,7},{6,4},{7,5},{8,10},{9,11},{10,... | collective-permute-start | bytes 49160 | tf_op jit(solution)/shard_map/ppermute | solution.py:303
  145.6 3.5 %columns.5 = (f32[64,128]{1,0:T(8,128)S(1)}, f32[8,512]{1,0:T(8,128)}) custom-call(s32[8]{0:T(128)S(1)} %copy-done.1, s32[24]{0:T(128)S(1)} %copy-done.2, s32[192]{0:T(256)S(1)} %copy-done, f32[8,512]{1,0:T(8,128)S(1)} %get-tuple-element.79.level, f32[8,512]{1,0:T(8,128)S(1)} %rows.3.part, f32[8,512]{1,0:T(8,128)S(1)} %collective-permute-done.44.near, ...), custom_call_target="tpu_custom_call" | custom-call | tf_op jit(solution)/shard_map/columns/pallas_call | solution.py:238
  149.1 16.3 %all_to_all.5 = f32[32,2,128]{2,1,0:T(2,128)S(1)} all-to-all(f32[32,2,128]{2,1,0:T(2,128)S(1)} %bitcast.39), channel_id=1, replica_groups=mesh['row'=32,'col'=4] {'row'}, dimensions={0} | all-to-all | bytes 65536 | tf_op jit(solution)/shard_map/all_to_all | solution.py:430
  (156 shorter events, 57.6 us)
Async XLA Ops:
  1.7 9.0 %collective-permute-start = (bf16[1,128,768]{2,1,0:T(8,128)(2,1)S(1)}, bf16[1,128,768]{2,1,0:T(8,128)(2,1)S(1)}, u32[]{:S(2)}, u32[]{:S(2)}) collective-permute-start(bf16[1,128,768]{2,1,0:T(8,128)(2,1)S(1)} %get-tuple-element.81), channel_id=1, source_target_pairs={{0,8},{4,12},{8,16},{12,20},{16,24},{20,28},{24,0},{28,4},{32,40},... | collective-permute-start | bytes 589832 | tf_op jit(solution)/shard_map/ppermute | solution.py:31
  3.9 12.4 %collective-permute-start.1 = (bf16[1,128,768]{2,1,0:T(8,128)(2,1)S(1)}, bf16[1,128,768]{2,1,0:T(8,128)(2,1)S(1)}, u32[]{:S(2)}, u32[]{:S(2)}) collective-permute-start(bf16[1,128,768]{2,1,0:T(8,128)(2,1)S(1)} %get-tuple-element.81), channel_id=1, source_target_pairs={{0,24},{4,28},{8,0},{12,4},{16,8},{20,12},{24,16},{28,20},{32,56},... | collective-permute-start | bytes 589832 | tf_op jit(solution)/shard_map/ppermute | solution.py:31
  5.4 10.9 %collective-permute-start.2 = (bf16[1,128,768]{2,1,0:T(8,128)(2,1)S(1)}, bf16[1,128,768]{2,1,0:T(8,128)(2,1)S(1)}, u32[]{:S(2)}, u32[]{:S(2)}) collective-permute-start(bf16[1,128,768]{2,1,0:T(8,128)(2,1)S(1)} %get-tuple-element.81), channel_id=1, source_target_pairs={{0,16},{4,20},{8,24},{12,28},{16,0},{20,4},{24,8},{28,12},{32,48},... | collective-permute-start | bytes 589832 | tf_op jit(solution)/shard_map/ppermute | solution.py:31
  7.0 9.4 %collective-permute-start.3 = (bf16[1,128,768]{2,1,0:T(8,128)(2,1)S(1)}, bf16[1,128,768]{2,1,0:T(8,128)(2,1)S(1)}, u32[]{:S(2)}, u32[]{:S(2)}) collective-permute-start(bf16[1,128,768]{2,1,0:T(8,128)(2,1)S(1)} %get-tuple-element.80), channel_id=1, source_target_pairs={{0,32},{4,36},{8,40},{12,44},{16,48},{20,52},{24,56},{28,60},{32,6... | collective-permute-start | bytes 589832 | tf_op jit(solution)/shard_map/ppermute | solution.py:31
  8.6 7.8 %collective-permute-start.4 = (bf16[1,128,768]{2,1,0:T(8,128)(2,1)S(1)}, bf16[1,128,768]{2,1,0:T(8,128)(2,1)S(1)}, u32[]{:S(2)}, u32[]{:S(2)}) collective-permute-start(bf16[1,128,768]{2,1,0:T(8,128)(2,1)S(1)} %get-tuple-element.80), channel_id=1, source_target_pairs={{0,96},{4,100},{8,104},{12,108},{16,112},{20,116},{24,120},{28,124... | collective-permute-start | bytes 589832 | tf_op jit(solution)/shard_map/ppermute | solution.py:31
  10.7 8.8 %collective-permute-start.5 = (bf16[1,128,768]{2,1,0:T(8,128)(2,1)S(1)}, bf16[1,128,768]{2,1,0:T(8,128)(2,1)S(1)}, u32[]{:S(2)}, u32[]{:S(2)}) collective-permute-start(bf16[1,128,768]{2,1,0:T(8,128)(2,1)S(1)} %get-tuple-element.80), channel_id=1, source_target_pairs={{0,64},{4,68},{8,72},{12,76},{16,80},{20,84},{24,88},{28,92},{32,9... | collective-permute-start | bytes 589832 | tf_op jit(solution)/shard_map/ppermute | solution.py:31
  19.6 6.3 %collective-permute-start.11 = (bf16[4,128,768]{2,1,0:T(8,128)(2,1)S(1)}, bf16[4,128,768]{2,1,0:T(8,128)(2,1)S(1)}, u32[]{:S(2)}, u32[]{:S(2)}) collective-permute-start(bf16[4,128,768]{2,1,0:T(8,128)(2,1)S(1)} %pad_maximum_fusion.1.refs_1_), channel_id=1, source_target_pairs={{0,4},{4,0},{8,12},{12,8},{16,20},{20,16},{24,28},{28,24},{32,36},... | collective-permute-start | bytes 2359304 | tf_op jit(solution)/shard_map/ppermute | solution.py:31
  22.3 5.5 %collective-permute-start.10 = (bf16[4,128,768]{2,1,0:T(8,128)(2,1)S(1)}, bf16[4,128,768]{2,1,0:T(8,128)(2,1)S(1)}, u32[]{:S(2)}, u32[]{:S(2)}) collective-permute-start(bf16[4,128,768]{2,1,0:T(8,128)(2,1)S(1)} %pad_maximum_fusion.refs_0_), channel_id=1, source_target_pairs={{0,4},{4,0},{8,12},{12,8},{16,20},{20,16},{24,28},{28,24},{32,36},... | collective-permute-start | bytes 2359304 | tf_op jit(solution)/shard_map/ppermute | solution.py:31
  22.4 20.0 %collective-permute-start.8 = (bf16[4,128,768]{2,1,0:T(8,128)(2,1)S(1)}, bf16[4,128,768]{2,1,0:T(8,128)(2,1)S(1)}, u32[]{:S(2)}, u32[]{:S(2)}) collective-permute-start(bf16[4,128,768]{2,1,0:T(8,128)(2,1)S(1)} %pad_maximum_fusion.1.refs_1_), channel_id=1, source_target_pairs={{0,8},{4,12},{8,16},{12,20},{16,24},{20,28},{24,0},{28,4},{32,40},... | collective-permute-start | bytes 2359304 | tf_op jit(solution)/shard_map/ppermute | solution.py:31
  22.8 19.5 %collective-permute-start.9 = (bf16[4,128,768]{2,1,0:T(8,128)(2,1)S(1)}, bf16[4,128,768]{2,1,0:T(8,128)(2,1)S(1)}, u32[]{:S(2)}, u32[]{:S(2)}) collective-permute-start(bf16[4,128,768]{2,1,0:T(8,128)(2,1)S(1)} %pad_maximum_fusion.1.refs_1_), channel_id=1, source_target_pairs={{0,24},{4,28},{8,0},{12,4},{16,8},{20,12},{24,16},{28,20},{32,56},... | collective-permute-start | bytes 2359304 | tf_op jit(solution)/shard_map/ppermute | solution.py:31
  25.1 19.3 %collective-permute-start.6 = (bf16[4,128,768]{2,1,0:T(8,128)(2,1)S(1)}, bf16[4,128,768]{2,1,0:T(8,128)(2,1)S(1)}, u32[]{:S(2)}, u32[]{:S(2)}) collective-permute-start(bf16[4,128,768]{2,1,0:T(8,128)(2,1)S(1)} %pad_maximum_fusion.refs_0_), channel_id=1, source_target_pairs={{0,32},{4,36},{8,40},{12,44},{16,48},{20,52},{24,56},{28,60},{32,6... | collective-permute-start | bytes 2359304 | tf_op jit(solution)/shard_map/ppermute | solution.py:31
  26.0 18.4 %collective-permute-start.7 = (bf16[4,128,768]{2,1,0:T(8,128)(2,1)S(1)}, bf16[4,128,768]{2,1,0:T(8,128)(2,1)S(1)}, u32[]{:S(2)}, u32[]{:S(2)}) collective-permute-start(bf16[4,128,768]{2,1,0:T(8,128)(2,1)S(1)} %pad_maximum_fusion.refs_0_), channel_id=1, source_target_pairs={{0,96},{4,100},{8,104},{12,108},{16,112},{20,116},{24,120},{28,124... | collective-permute-start | bytes 2359304 | tf_op jit(solution)/shard_map/ppermute | solution.py:31
  46.4 4.5 %collective-permute-start.17 = (bf16[4,128,768]{2,1,0:T(8,128)(2,1)S(1)}, bf16[4,128,768]{2,1,0:T(8,128)(2,1)S(1)}, u32[]{:S(2)}, u32[]{:S(2)}) collective-permute-start(bf16[4,128,768]{2,1,0:T(8,128)(2,1)S(1)} %collective-permute-done.7.refs_1_), channel_id=1, source_target_pairs={{0,4},{4,0},{8,12},{12,8},{16,20},{20,16},{24,28},{28,24},{32,36},... | collective-permute-start | bytes 2359304 | tf_op jit(solution)/shard_map/ppermute | solution.py:31
  46.5 4.8 %collective-permute-start.18 = (bf16[4,128,768]{2,1,0:T(8,128)(2,1)S(1)}, bf16[4,128,768]{2,1,0:T(8,128)(2,1)S(1)}, u32[]{:S(2)}, u32[]{:S(2)}) collective-permute-start(bf16[4,128,768]{2,1,0:T(8,128)(2,1)S(1)} %collective-permute-done.8.refs_2_), channel_id=1, source_target_pairs={{0,4},{4,0},{8,12},{12,8},{16,20},{20,16},{24,28},{28,24},{32,36},... | collective-permute-start | bytes 2359304 | tf_op jit(solution)/shard_map/ppermute | solution.py:31
  46.9 6.7 %collective-permute-start.19 = (bf16[4,128,768]{2,1,0:T(8,128)(2,1)S(1)}, bf16[4,128,768]{2,1,0:T(8,128)(2,1)S(1)}, u32[]{:S(2)}, u32[]{:S(2)}) collective-permute-start(bf16[4,128,768]{2,1,0:T(8,128)(2,1)S(1)} %collective-permute-done.9.refs_3_), channel_id=1, source_target_pairs={{0,4},{4,0},{8,12},{12,8},{16,20},{20,16},{24,28},{28,24},{32,36},... | collective-permute-start | bytes 2359304 | tf_op jit(solution)/shard_map/ppermute | solution.py:31
  47.1 20.4 %collective-permute-start.12 = (bf16[2,128,768]{2,1,0:T(8,128)(2,1)S(1)}, bf16[2,128,768]{2,1,0:T(8,128)(2,1)S(1)}, u32[]{:S(2)}, u32[]{:S(2)}) collective-permute-start(bf16[2,128,768]{2,1,0:T(8,128)(2,1)S(1)} %slice.41), channel_id=1, source_target_pairs={{0,32},{4,36},{8,40},{12,44},{16,48},{20,52},{24,56},{28,60},{32,6... | collective-permute-start | bytes 1179656 | tf_op jit(solution)/shard_map/ppermute | solution.py:31
  48.3 19.2 %collective-permute-start.13 = (bf16[2,128,768]{2,1,0:T(8,128)(2,1)S(1)}, bf16[2,128,768]{2,1,0:T(8,128)(2,1)S(1)}, u32[]{:S(2)}, u32[]{:S(2)}) collective-permute-start(bf16[2,128,768]{2,1,0:T(8,128)(2,1)S(1)} %slice.42), channel_id=1, source_target_pairs={{0,96},{4,100},{8,104},{12,108},{16,112},{20,116},{24,120},{28,124... | collective-permute-start | bytes 1179656 | tf_op jit(solution)/shard_map/ppermute | solution.py:31
  50.9 16.6 %collective-permute-start.14 = (bf16[2,128,768]{2,1,0:T(8,128)(2,1)S(1)}, bf16[2,128,768]{2,1,0:T(8,128)(2,1)S(1)}, u32[]{:S(2)}, u32[]{:S(2)}) collective-permute-start(bf16[2,128,768]{2,1,0:T(8,128)(2,1)S(1)} %slice.43), channel_id=1, source_target_pairs={{0,8},{4,12},{8,16},{12,20},{16,24},{20,28},{24,0},{28,4},{32,40},... | collective-permute-start | bytes 1179656 | tf_op jit(solution)/shard_map/ppermute | solution.py:31
  51.3 16.2 %collective-permute-start.15 = (bf16[2,128,768]{2,1,0:T(8,128)(2,1)S(1)}, bf16[2,128,768]{2,1,0:T(8,128)(2,1)S(1)}, u32[]{:S(2)}, u32[]{:S(2)}) collective-permute-start(bf16[2,128,768]{2,1,0:T(8,128)(2,1)S(1)} %slice.44), channel_id=1, source_target_pairs={{0,24},{4,28},{8,0},{12,4},{16,8},{20,12},{24,16},{28,20},{32,56},... | collective-permute-start | bytes 1179656 | tf_op jit(solution)/shard_map/ppermute | solution.py:31
  83.9 4.9 %collective-permute-start.24 = (f32[2,8,512]{2,1,0:T(8,128)S(1)}, f32[2,8,512]{2,1,0:T(8,128)S(1)}, u32[]{:S(2)}, u32[]{:S(2)}) collective-permute-start(f32[2,8,512]{2,1,0:T(8,128)S(1)} %pad_maximum_fusion.2), channel_id=1, source_target_pairs={{0,1},{1,2},{2,3},{3,0},{4,5},{5,6},{6,7},{7,4},{8,9},{9,10},{10,1... | collective-permute-start | bytes 98312 | tf_op jit(solution)/shard_map/ppermute | solution.py:303
  95.4 5.1 %collective-permute-start.30 = (f32[64,128]{1,0:T(8,128)S(1)}, f32[64,128]{1,0:T(8,128)S(1)}, u32[]{:S(2)}, u32[]{:S(2)}) collective-permute-start(f32[64,128]{1,0:T(8,128)S(1)} %add.48), channel_id=1, source_target_pairs={{0,24},{4,28},{8,0},{12,4},{16,8},{20,12},{24,16},{28,20},{32,56},... | collective-permute-start | bytes 98312 | tf_op jit(solution)/shard_map/ppermute | solution.py:31
  109.1 4.6 %collective-permute-start.35 = (f32[8,512]{1,0:T(8,128)S(1)}, f32[8,512]{1,0:T(8,128)S(1)}, u32[]{:S(2)}, u32[]{:S(2)}) collective-permute-start(f32[8,512]{1,0:T(8,128)S(1)} %rows.2.part), channel_id=1, source_target_pairs={{0,2},{1,3},{2,0},{3,1},{4,6},{5,7},{6,4},{7,5},{8,10},{9,11},{10,... | collective-permute-start | bytes 49160 | tf_op jit(solution)/shard_map/ppermute | solution.py:303
  118.4 5.4 %collective-permute-start.37 = (f32[64,128]{1,0:T(8,128)S(1)}, f32[64,128]{1,0:T(8,128)S(1)}, u32[]{:S(2)}, u32[]{:S(2)}) collective-permute-start(f32[64,128]{1,0:T(8,128)S(1)} %columns.4), channel_id=1, source_target_pairs={{0,4},{4,0},{8,12},{12,8},{16,20},{20,16},{24,28},{28,24},{32,36},... | collective-permute-start | bytes 98312 | tf_op jit(solution)/shard_map/ppermute | solution.py:31
  131.4 4.8 %collective-permute-start.42 = (f32[64,128]{1,0:T(8,128)S(1)}, f32[64,128]{1,0:T(8,128)S(1)}, u32[]{:S(2)}, u32[]{:S(2)}) collective-permute-start(f32[64,128]{1,0:T(8,128)S(1)} %add_add_fusion.1), channel_id=1, source_target_pairs={{0,64},{4,68},{8,72},{12,76},{16,80},{20,84},{24,88},{28,92},{32,9... | collective-permute-start | bytes 98312 | tf_op jit(solution)/shard_map/ppermute | solution.py:31
  (52 other events, 289.8 us)

commit v5 on v4

--- a/solution.py
+++ b/solution.py
@@ -60,7 +60,10 @@
     return stages
 
 
-def score_kernel(stage, listed, dest, segments, lives, source, *refs):
+SLOTS, DEST, SEGMENTS, LIVES, ORDER, ALIVE, COUNTS, TABLE = 0, 24, 88, 96, 120, 216, 312, 320
+
+
+def score_kernel(stage, listed, table, source, *refs):
     layout = piece_layout()[stage]
     number = max(entry[0] for entry in layout) + 1
     pieces, refs = refs[:number], refs[number:]
@@ -69,26 +72,25 @@
     matrix, peak_out, sum_out = refs[:3]
     if stage == STAGES - 1:
         high_out, total_out = refs[3:5]
-    held, streamed, fetch_sems, stream_sems = refs[-4:]
+    held, fetch_sems = refs[-2:]
     blocks = source.shape[0]
     rows = matrix.shape[2]
 
     def stream(s):
         return pltpu.make_async_copy(source.at[s], streamed.at[lax.rem(s, 2)], stream_sems.at[lax.rem(s, 2)])
 
-    stream(0).start()
 
     def fetch(piece, index, entry):
         return pltpu.make_async_copy(
             pieces[piece].at[index], held.at[pl.ds(entry * rows, rows)], fetch_sems.at[entry]
         )
 
-    offset = sum(len(entries) for entries in piece_layout()[:stage])
+    offset = DEST + sum(len(entries) for entries in piece_layout()[:stage])
     for position, (piece, index, *_) in enumerate(layout, offset):
 
-        @pl.when(dest[position] >= 0)
+        @pl.when(table[position] >= 0)
         def _():
-            fetch(piece, index, dest[position]).start()
+            fetch(piece, index, table[position]).start()
 
     if stage == 0:
         peak_out[...] = jnp.full(peak_out.shape, NEGATIVE, jnp.float32)
@@ -96,8 +98,8 @@
 
     def one_block(s, carry):
         group = s // SHARE
-        begin = segments[group * (STAGES + 1) + stage]
-        live = lives[s * STAGES + stage]
+        begin = table[SEGMENTS + group * (STAGES + 1) + stage]
+        live = table[LIVES + s * STAGES + stage]
 
         @pl.when(lax.rem(s, SHARE) == 0)
         def _():
@@ -105,19 +107,13 @@
                 fetch(0, 0, group * listed + entry).wait()
                 return carry
 
-            lax.fori_loop(begin, segments[group * (STAGES + 1) + stage + 1], arrive, 0)
-
-        @pl.when(s + 1 < blocks)
-        def _():
-            stream(s + 1).start()
-
-        stream(s).wait()
+            lax.fori_loop(begin, table[SEGMENTS + group * (STAGES + 1) + stage + 1], arrive, 0)
 
         def batch(first, size):
             base = pl.multiple_of((group * listed + begin + first) * rows, rows)
             scores = lax.dot_general(
                 held[pl.ds(base, size * rows), :],
-                streamed[lax.rem(s, 2)],
+                source[s],
                 (((1,), (1,)), ((), ())),
                 preferred_element_type=jnp.float32,
             )
@@ -146,7 +142,7 @@
             total_out[s : s + 1, :] = jnp.sum(sum_out[s] * jnp.exp2(peak_out[s] - high), axis=0, keepdims=True)
 
 
-def score_stage(stage, listed, dest, segments, lives, source_vectors, pieces, earlier):
+def score_stage(stage, listed, table, source_vectors, pieces, earlier):
     blocks, block_rows, width = source_vectors.shape
     rows = pieces[0].shape[1]
     padded = 16
@@ -161,27 +157,25 @@
         earlier = [pltpu.with_memory_space_constraint(earlier[0], pltpu.VMEM)] + earlier[1:]
     return pl.pallas_call(
         functools.partial(score_kernel, stage, listed),
-        in_specs=[smem] * 3 + [hbm] * (1 + len(pieces)) + [vmem] * len(earlier),
+        in_specs=[smem, vmem] + [hbm] * len(pieces) + [vmem] * len(earlier),
         out_specs=[vmem] * (3 + 2 * last),
         out_shape=[pltpu.VMEM((blocks, listed, rows, block_rows), jnp.float32), small, small] + [whole] * 2 * last,
         scratch_shapes=[
             pltpu.VMEM((2 * listed * rows, width), jnp.bfloat16),
-            pltpu.VMEM((2, block_rows, width), jnp.bfloat16),
             pltpu.SemaphoreType.DMA((2 * listed,)),
-            pltpu.SemaphoreType.DMA((2,)),
         ],
-        input_output_aliases={4 + len(pieces) + n: n for n in range(len(earlier))},
-        compiler_params=pltpu.CompilerParams(vmem_limit_bytes=12 * MIB),
+        input_output_aliases={2 + len(pieces) + n: n for n in range(len(earlier))},
+        compiler_params=pltpu.CompilerParams(vmem_limit_bytes=8 * MIB),
         cost_estimate=pl.CostEstimate(
             flops=int(2 * blocks * listed * rows * block_rows * width * share),
             bytes_accessed=int(4 * blocks * listed * rows * block_rows * share),
             transcendentals=0,
         ),
         name="scores",
-    )(dest, segments, lives, source_vectors, *pieces, *earlier)
-
-
-def column_kernel(final, counts, slots, order, level, part, near, far, back, matrix, peaks, *refs):
+    )(table, source_vectors, *pieces, *earlier)
+
+
+def column_kernel(final, table, level, part, near, far, back, matrix, peaks, *refs):
     sums_out = refs[0]
     weights, columns = refs[-2:]
     blocks, block_rows = part.shape
@@ -208,7 +202,7 @@
 
             acc = tuple(jnp.zeros((8, 128), jnp.float32) for _ in range(rows // 8))
             for s in range(g * SHARE, (g + 1) * SHARE):
-                live = order[(blocks + s) * listed + k] > 0
+                live = table[ALIVE + s * listed + k] > 0
                 acc = lax.cond(live, functools.partial(one_source, s), lambda acc: acc, acc)
             for j, a in enumerate(acc):
                 columns[g * listed + k, 8 * j : 8 * j + 8, :] = a
@@ -224,10 +218,10 @@
             merged[j] = jnp.where(lane == e, one, merged[j])
     by_entry = jnp.concatenate(merged, axis=0).T
     for e in range(2 * listed):
-        sums_out[pl.ds(slots[e], 1), :] = by_entry[e : e + 1, :]
-
-
-def column_pass(final, counts, slots, order, targets, level, parts, matrix, peaks):
+        sums_out[pl.ds(table[SLOTS + e], 1), :] = by_entry[e : e + 1, :]
+
+
+def column_pass(final, table, targets, level, parts, matrix, peaks):
     blocks, block_rows = level.shape
     rows = matrix.shape[2]
     vmem = pl.BlockSpec(memory_space=pltpu.VMEM)
@@ -237,7 +231,7 @@
         out_shape.append(jax.ShapeDtypeStruct((blocks, block_rows), jnp.float32))
     return pl.pallas_call(
         functools.partial(column_kernel, final),
-        in_specs=[smem] * 3 + [vmem] * 7,
+        in_specs=[smem] + [vmem] * 7,
         out_specs=[vmem] * len(out_shape),
         out_shape=out_shape,
         scratch_shapes=[
@@ -246,14 +240,14 @@
         ],
         compiler_params=pltpu.CompilerParams(vmem_limit_bytes=8 * MIB),
         name="columns",
-    )(counts, slots, order, level, *parts, matrix, peaks)
-
-
-def row_kernel(counts, slots, order, level, sums, matrix, peaks, out, weights, gathered, spread):
+    )(table, level, *parts, matrix, peaks)
+
+
+def row_kernel(table, level, sums, matrix, peaks, out, weights, gathered, spread):
     blocks, block_rows = out.shape
     listed, rows = matrix.shape[1:3]
     for e in range(2 * listed):
-        gathered[e : e + 1, :] = sums[pl.ds(slots[e], 1), :]
+        gathered[e : e + 1, :] = sums[pl.ds(table[SLOTS + e], 1), :]
     factors = (1.0 / (1.0 + gathered[...])).T
     for e in range(2 * listed):
         spread[e] = jnp.broadcast_to(factors[:, e : e + 1], (rows, 128))
@@ -264,7 +258,7 @@
         g = s // SHARE
 
         def one_entry(t, total):
-            k = order[s * listed + t]
+            k = table[ORDER + s * listed + t]
             acc = [jnp.zeros((8, 128), jnp.float32) for _ in range(lanes)]
             for j in range(0, rows, 8):
                 v = spread[g * listed + k, j : j + 8, :]
@@ -274,19 +268,19 @@
             return tuple(t + a * w[:, 128 * l : 128 * l + 128] for l, (t, a) in enumerate(zip(total, acc)))
 
         total = lax.fori_loop(
-            0, counts[s], one_entry, tuple(jnp.zeros((8, 128), jnp.float32) for _ in range(lanes))
+            0, table[COUNTS + s], one_entry, tuple(jnp.zeros((8, 128), jnp.float32) for _ in range(lanes))
         )
         out[s : s + 1, :] = jnp.concatenate([jnp.sum(t, axis=0, keepdims=True) for t in total], axis=1)
 
 
-def row_pass(counts, slots, order, level, sums, matrix, peaks):
+def row_pass(table, level, sums, matrix, peaks):
     blocks, block_rows = level.shape
     listed, rows = matrix.shape[1:3]
     vmem = pl.BlockSpec(memory_space=pltpu.VMEM)
     smem = pl.BlockSpec(memory_space=pltpu.SMEM)
     return pl.pallas_call(
         row_kernel,
-        in_specs=[smem] * 3 + [vmem] * 4,
+        in_specs=[smem] + [vmem] * 4,
         out_specs=vmem,
         out_shape=jax.ShapeDtypeStruct((blocks, block_rows), jnp.float32),
         scratch_shapes=[
@@ -296,7 +290,7 @@
         ],
         compiler_params=pltpu.CompilerParams(vmem_limit_bytes=8 * MIB),
         name="rows",
-    )(counts, slots, order, level, sums, matrix, peaks)
+    )(table, level, sums, matrix, peaks)
 
 
 def from_columns(x):
@@ -309,12 +303,15 @@
     return x + send(x, 1, 0, 0) + send(x, 2, 0, 0) + send(x, 3, 0, 0)
 
 
-def tables_kernel(target_blocks, me, pairs, counts, owners, slots, dest, segments, lives, order, listing):
+def tables_kernel(target_blocks, me, pairs, counts, owners, source, table, loaded, listing, sems):
     blocks, listed = pairs.shape
+    copies = [pltpu.make_async_copy(source.at[s], loaded.at[s], sems.at[s]) for s in range(blocks)]
+    for copy in copies:
+        copy.start()
     starts = np.cumsum([0] + [len(stage) for stage in piece_layout()])
     z, y, core = me[0] // 8, (me[0] // 2) % 4, me[0] % 2
     for n in range(int(starts[-1])):
-        dest[n] = -1
+        table[DEST + n] = -1
     for g in range(blocks // SHARE):
         found = []
         for k in range(listed):
@@ -335,44 +332,49 @@
         following = []
         begin = jnp.int32(0)
         for stage in range(STAGES):
-            segments[g * (STAGES + 1) + stage] = begin
+            table[SEGMENTS + g * (STAGES + 1) + stage] = begin
             following.append(begin)
             begin = begin + sum(jnp.where(f[1] == stage, 1, 0) for f in found)
-        segments[g * (STAGES + 1) + STAGES] = begin
+        table[SEGMENTS + g * (STAGES + 1) + STAGES] = begin
         for k, (slot, stage, position) in enumerate(found):
             place = jnp.where(stage == 0, following[0], jnp.where(stage == 1, following[1], following[2]))
             following = [f + jnp.where(stage == n, 1, 0) for n, f in enumerate(following)]
-            slots[g * listed + place] = slot
-            dest[position] = g * listed + place
+            table[SLOTS + g * listed + place] = slot
+            table[DEST + position] = g * listed + place
             listing[place] = k
         for s in range(g * SHARE, (g + 1) * SHARE):
             count = counts[s]
+            table[COUNTS + s] = count
             for stage in range(STAGES):
-                lives[s * STAGES + stage] = sum(
+                table[LIVES + s * STAGES + stage] = sum(
                     jnp.where((f[1] == stage) & (k < count), 1, 0) for k, f in enumerate(found)
                 )
             turn = jnp.int32(0)
             for place in range(listed):
                 live = jnp.where(listing[place] < count, 1, 0)
-                order[s * listed + turn] = place
-                order[(blocks + s) * listed + place] = live
+                table[ORDER + s * listed + turn] = place
+                table[ALIVE + s * listed + place] = live
                 turn = turn + live
-
-
-def tables(pair_list, counts, owner_map, target_blocks):
-    blocks, listed = pair_list.shape
-    entries = blocks // SHARE * listed
+    for copy in copies:
+        copy.wait()
+
+
+def tables(pair_list, counts, owner_map, source_vectors, target_blocks):
+    listed = pair_list.shape[1]
     me = jnp.reshape(lax.axis_index("row"), (1,)).astype(jnp.int32)
     smem = pl.BlockSpec(memory_space=pltpu.SMEM)
-    sizes = (entries, owner_map.shape[0], blocks // SHARE * (STAGES + 1), blocks * STAGES, 2 * blocks * listed)
     return pl.pallas_call(
         functools.partial(tables_kernel, target_blocks),
-        in_specs=[smem] * 4,
-        out_specs=[smem] * 5,
-        out_shape=[jax.ShapeDtypeStruct((size,), jnp.int32) for size in sizes],
-        scratch_shapes=[pltpu.SMEM((listed,), jnp.int32)],
+        in_specs=[smem] * 4 + [pl.BlockSpec(memory_space=pltpu.HBM)],
+        out_specs=[smem, pl.BlockSpec(memory_space=pltpu.VMEM)],
+        out_shape=[
+            jax.ShapeDtypeStruct((TABLE,), jnp.int32),
+            pltpu.VMEM(source_vectors.shape, source_vectors.dtype),
+        ],
+        scratch_shapes=[pltpu.SMEM((listed,), jnp.int32), pltpu.SemaphoreType.DMA(source_vectors.shape[:1])],
+        compiler_params=pltpu.CompilerParams(vmem_limit_bytes=4 * MIB),
         name="tables",
-    )(me, pair_list, counts, owner_map)
+    )(me, pair_list, counts, owner_map, source_vectors)
 
 
 def shards(source_vectors, target_vectors, pair_list, counts, owner_map):
@@ -380,20 +382,17 @@
     listed = pair_list.shape[1]
     targets = owner_map.shape[0]
     source_vectors = pltpu.with_memory_space_constraint(source_vectors, pltpu.HBM)
-    slots, dest, segments, lives, order = tables(pair_list, counts, owner_map, target_blocks)
-
-    def across(pieces):
+    table, loaded = tables(pair_list, counts, owner_map, source_vectors, target_blocks)
+
+    def stage(number, pieces, earlier):
         pieces = pieces + [send(piece, 0, 0, 1) for piece in pieces]
-        return [pltpu.with_memory_space_constraint(piece, pltpu.HBM) for piece in pieces]
-
-    def stage(number, pieces, earlier):
-        return score_stage(
-            number, listed, dest, segments, lives, source_vectors, across(pieces), earlier
-        )
+        pieces = [pltpu.with_memory_space_constraint(piece, pltpu.HBM) for piece in pieces]
+        return score_stage(number, listed, table, loaded, pieces, earlier)
 
     along_y, along_z = target_vectors[:1], target_vectors[1:]
     arrived = ring_sends(along_y, 0, 1) + ring_sends(along_z, 1, 0)
-    *arrived, slots, dest, segments, lives, order = tie(*arrived, slots, dest, segments, lives, order)
+    *arrived, table, loaded = tie(*arrived, table, loaded)
+    loaded = pltpu.with_memory_space_constraint(loaded, pltpu.VMEM)
     first = [jnp.concatenate([along_y] + arrived[:3], axis=0), jnp.concatenate([along_z] + arrived[3:], axis=0)]
     second = [
         send(first[0], 1, 0, 0),
@@ -420,11 +419,11 @@
 
     for sweep_index in range(SWEEPS):
         final = sweep_index == SWEEPS - 1
-        sums = column_pass(final, counts, slots, order, targets, level, parts, matrix, peaks)
+        sums = column_pass(final, table, targets, level, parts, matrix, peaks)
         if final:
             break
         sums = sum_over_rows(sums[0])
-        parts = from_columns(row_pass(counts, slots, order, level, sums, matrix, peaks))
+        parts = from_columns(row_pass(table, level, sums, matrix, peaks))
     sums, source_dual = sums
     row_count = targets // target_blocks
     back = lax.all_to_all(

time: 167 us -> 163 us (0.976)
  Pallas kernels: 50.5 us -> 39.7 us
  starting transfers between devices: 59.6 us -> 69.6 us
    ppermute x38, starting transfers between devices: 47.7 us -> 57.8 us  [send(): return lax.ppermute(x, 'row', row_perm(dz, dy, dc))]
    pallas_call x3, Pallas kernels: 30.6 us -> 20.7 us  [score_stage(): pl.pallas_call(functools.partial(score_kernel, stage, listed), in_specs=[...]
    pallas_call x5, Pallas kernels: 16.9 us -> 15 us  [the longest x3 9.46 us: column_pass(): pl.pallas_call(functools.partial(column_kernel, final), in_specs=[smem] +...]
    unnamed x58 -> x46, local copies, waits for them, and re-layouts: 5.65 us -> 4.5 us
  transfers between devices with their start and end apart: 47 -> 47, of which waited for: 30 -> 31; matrix products, arithmetic and copies ran while one was open for 0% -> 0% of each run, Pallas kernels for 13% -> 11%
where the time goes in v5:
time: 163 us
  starting transfers between devices  69.6 us (43%)
  Pallas kernels  39.7 us (24%)
  waiting for transfers between devices  29.5 us (18%)
  blocking collectives  17 us (10%)
  local copies, waits for them, and re-layouts  5.66 us (3%)
    ppermute x38, starting transfers between devices, send(): return lax.ppermute(x, 'row', row_perm(dz, dy, dc))  57.8 us
    ppermute x38, waiting for transfers between devices, send(): return lax.ppermute(x, 'row', row_perm(dz, dy, dc))  23.6 us
    pallas_call x3, Pallas kernels, score_stage(): pl.pallas_call(functools.partial(score_kernel, stage, listed), in_specs=[...  20.7 us
    all_to_all x1, blocking collectives, shards(): lax.all_to_all(sums.reshape(row_count, target_blocks, quarter), 'row', sp...  17 us
    ppermute x9, starting transfers between devices, from_columns(): lax.ppermute(x, 'col', [(i, (i + d) % 4) for i in range(4)])  11.9 us
    pallas_call x3, Pallas kernels, column_pass(): pl.pallas_call(functools.partial(column_kernel, final), in_specs=[smem] +...  9.46 us
    ppermute x9, waiting for transfers between devices, from_columns(): lax.ppermute(x, 'col', [(i, (i + d) % 4) for i in range(4)])  5.92 us
    pallas_call x2, Pallas kernels, row_pass(): pl.pallas_call(row_kernel, in_specs=[smem] + [vmem] * 4, out_specs=vmem,...  5.5 us
  transfers between devices with their start and end apart: 47, of which 31 were waited for; matrix products, arithmetic and copies ran while one was open for 0% of the time, Pallas kernels for 11%

profile of v5, /device:TPU:1, one launch (start us, length us, event | category | flops | bytes accessed | tf_op | source)
XLA Modules:
  0.0 163.4 jit_solution(15343946466009762014)
XLA Ops:
  1.7 2.2 %collective-permute-start = (bf16[1,128,768]{2,1,0:T(8,128)(2,1)S(1)}, bf16[1,128,768]{2,1,0:T(8,128)(2,1)S(1)}, u32[]{:S(2)}, u32[]{:S(2)}) collective-permute-start(bf16[1,128,768]{2,1,0:T(8,128)(2,1)S(1)} %get-tuple-element.69), channel_id=1, source_target_pairs={{0,8},{4,12},{8,16},{12,20},{16,24},{20,28},{24,0},{28,4},{32,40},... | collective-permute-start | bytes 589832 | tf_op jit(solution)/shard_map/ppermute | solution.py:31
  10.7 2.6 %collective-permute-start.5 = (bf16[1,128,768]{2,1,0:T(8,128)(2,1)S(1)}, bf16[1,128,768]{2,1,0:T(8,128)(2,1)S(1)}, u32[]{:S(2)}, u32[]{:S(2)}) collective-permute-start(bf16[1,128,768]{2,1,0:T(8,128)(2,1)S(1)} %get-tuple-element.68), channel_id=1, source_target_pairs={{0,64},{4,68},{8,72},{12,76},{16,80},{20,84},{24,88},{28,92},{32,9... | collective-permute-start | bytes 589832 | tf_op jit(solution)/shard_map/ppermute | solution.py:31
  15.3 4.1 %tables.1 = (s32[320]{0:T(512)S(1)}, bf16[8,512,768]{2,1,0:T(8,128)(2,1)S(1)}) custom-call(s32[1]{0:T(128)} %bitcast.me, s32[8,12]{1,0:T(8,128)S(1)} %copy-done, s32[8]{0:T(128)S(1)} %copy-done.1, s32[64]{0:T(128)S(1)} %copy-done.2, bf16[8,512,768]{2,1,0:T(8,128)(2,1)} %source.1), custom_call_target="tpu_custom_call" | custom-call | tf_op jit(solution)/shard_map/tables/pallas_call | solution.py:366
  19.6 2.5 %collective-permute-start.11 = (bf16[4,128,768]{2,1,0:T(8,128)(2,1)S(1)}, bf16[4,128,768]{2,1,0:T(8,128)(2,1)S(1)}, u32[]{:S(2)}, u32[]{:S(2)}) collective-permute-start(bf16[4,128,768]{2,1,0:T(8,128)(2,1)S(1)} %pad_maximum_fusion.1.refs_1_), channel_id=1, source_target_pairs={{0,4},{4,0},{8,12},{12,8},{16,20},{20,16},{24,28},{28,24},{32,36},... | collective-permute-start | bytes 2359304 | tf_op jit(solution)/shard_map/ppermute | solution.py:31
  22.8 2.3 %collective-permute-start.9 = (bf16[4,128,768]{2,1,0:T(8,128)(2,1)S(1)}, bf16[4,128,768]{2,1,0:T(8,128)(2,1)S(1)}, u32[]{:S(2)}, u32[]{:S(2)}) collective-permute-start(bf16[4,128,768]{2,1,0:T(8,128)(2,1)S(1)} %pad_maximum_fusion.1.refs_1_), channel_id=1, source_target_pairs={{0,24},{4,28},{8,0},{12,4},{16,8},{20,12},{24,16},{28,20},{32,56},... | collective-permute-start | bytes 2359304 | tf_op jit(solution)/shard_map/ppermute | solution.py:31
  28.7 6.4 %scores.3 = (f32[8,12,128,512]{3,2,1,0:T(8,128)S(1)}, f32[8,16,512]{2,1,0:T(8,128)S(1)}, f32[8,16,512]{2,1,0:T(8,128)S(1)}) custom-call(s32[320]{0:T(512)S(1)} %get-tuple-element.36.table, bf16[8,512,768]{2,1,0:T(8,128)(2,1)S(1)} %get-tuple-element.37.source, bf16[4,128,768]{2,1,0:T(8,128)(2,1)} %copy-done.4, bf16[4,128,768]{2,1,0:T(8,128)(2,1)} %copy-done.3, ...), custom_call_target="tpu_custom_call" | custom-call | flops 2415919104 | bytes 6291456 | tf_op jit(solution)/shard_map/scores/pallas_call | solution.py:158
  35.1 7.2 %collective-permute-done.8.refs_2_ = bf16[4,128,768]{2,1,0:T(8,128)(2,1)S(1)} collective-permute-done((bf16[4,128,768]{2,1,0:T(8,128)(2,1)S(1)}, bf16[4,128,768]{2,1,0:T(8,128)(2,1)S(1)}, u32[]{:S(2)}, u32[]{:S(2)}) %collective-permute-start.8) | collective-permute-done | bytes 786464 | tf_op jit(solution)/shard_map/ppermute | solution.py:31
  48.3 2.6 %collective-permute-start.13 = (bf16[2,128,768]{2,1,0:T(8,128)(2,1)S(1)}, bf16[2,128,768]{2,1,0:T(8,128)(2,1)S(1)}, u32[]{:S(2)}, u32[]{:S(2)}) collective-permute-start(bf16[2,128,768]{2,1,0:T(8,128)(2,1)S(1)} %slice.42), channel_id=1, source_target_pairs={{0,96},{4,100},{8,104},{12,108},{16,112},{20,116},{24,120},{28,124... | collective-permute-start | bytes 1179656 | tf_op jit(solution)/shard_map/ppermute | solution.py:31
  54.8 7.1 %scores.4 = (f32[8,12,128,512]{3,2,1,0:T(8,128)S(1)}, f32[8,16,512]{2,1,0:T(8,128)S(1)}, f32[8,16,512]{2,1,0:T(8,128)S(1)}) custom-call(s32[320]{0:T(512)S(1)} %get-tuple-element.36.table, bf16[8,512,768]{2,1,0:T(8,128)(2,1)S(1)} %get-tuple-element.37.source, ...), custom_call_target="tpu_custom_call", output_to_operand_aliasing={{0}: (10, {}), {1}: (11, {}), {2}: (12, {})} | custom-call | flops 4831838208 | bytes 12582912 | tf_op jit(solution)/shard_map/scores/pallas_call | solution.py:158
  62.7 2.2 %collective-permute-start.20 = (bf16[2,128,768]{2,1,0:T(8,128)(2,1)S(1)}, bf16[2,128,768]{2,1,0:T(8,128)(2,1)S(1)}, u32[]{:S(2)}, u32[]{:S(2)}) collective-permute-start(bf16[2,128,768]{2,1,0:T(8,128)(2,1)S(1)} %collective-permute-done.12.refs_0_), channel_id=1, source_target_pairs={{0,4},{4,0},{8,12},{12,8},{16,20},{20,16},{24,28},{28,24},{32,36},... | collective-permute-start | bytes 1179656 | tf_op jit(solution)/shard_map/ppermute | solution.py:31
  68.7 7.2 %scores.5 = (f32[8,12,128,512]{3,2,1,0:T(8,128)S(1)}, f32[8,16,512]{2,1,0:T(8,128)S(1)}, f32[8,16,512]{2,1,0:T(8,128)S(1)}, f32[8,512]{1,0:T(8,128)S(1)}, f32[8,512]{1,0:T(8,128)S(1)}) custom-call(s32[320]{0:T(512)S(1)} %get-tuple-element.36.table, ...), custom_call_target="tpu_custom_call", output_to_operand_aliasing={{0}: (10, {}), {1}: (11, {}), {2}: (12, {})} | custom-call | flops 2415919104 | bytes 6291456 | tf_op jit(solution)/shard_map/scores/pallas_call | solution.py:158
  77.2 2.5 %collective-permute-start.25 = (f32[2,8,512]{2,1,0:T(8,128)S(1)}, f32[2,8,512]{2,1,0:T(8,128)S(1)}, u32[]{:S(2)}, u32[]{:S(2)}) collective-permute-start(f32[2,8,512]{2,1,0:T(8,128)S(1)} %pad_maximum_fusion.2), channel_id=1, source_target_pairs={{0,2},{1,3},{2,0},{3,1},{4,6},{5,7},{6,4},{7,5},{8,10},{9,11},{10,... | collective-permute-start | bytes 98312 | tf_op jit(solution)/shard_map/ppermute | solution.py:297
  82.8 3.1 %columns.3 = f32[64,128]{1,0:T(8,128)S(1)} custom-call(s32[320]{0:T(512)S(1)} %get-tuple-element.36.table, f32[8,512]{1,0:T(8,128)S(1)} %get-tuple-element.67.level, f32[8,512]{1,0:T(8,128)S(1)} %get-tuple-element.72.part, f32[8,512]{1,0:T(8,128)S(1)} %get-tuple-element.71.near, f32[8,512]{1,0:T(8,128)S(1)} %get-tuple-element.70.far, ...), custom_call_target="tpu_custom_call" | custom-call | tf_op jit(solution)/shard_map/columns/pallas_call | solution.py:232
  85.9 2.2 %collective-permute-start.27 = (f32[64,128]{1,0:T(8,128)S(1)}, f32[64,128]{1,0:T(8,128)S(1)}, u32[]{:S(2)}, u32[]{:S(2)}) collective-permute-start(f32[64,128]{1,0:T(8,128)S(1)} %columns.3), channel_id=1, source_target_pairs={{0,4},{4,0},{8,12},{12,8},{16,20},{20,16},{24,28},{28,24},{32,36},... | collective-permute-start | bytes 98312 | tf_op jit(solution)/shard_map/ppermute | solution.py:31
  88.9 4.0 %collective-permute-start.28 = (f32[64,128]{1,0:T(8,128)S(1)}, f32[64,128]{1,0:T(8,128)S(1)}, u32[]{:S(2)}, u32[]{:S(2)}) collective-permute-start(f32[64,128]{1,0:T(8,128)S(1)} %add.48), channel_id=1, source_target_pairs={{0,8},{4,12},{8,16},{12,20},{16,24},{20,28},{24,0},{28,4},{32,40},... | collective-permute-start | bytes 98312 | tf_op jit(solution)/shard_map/ppermute | solution.py:31
  103.2 2.8 %rows.2.part = f32[8,512]{1,0:T(8,128)S(1)} custom-call(s32[320]{0:T(512)S(1)} %get-tuple-element.36.table, f32[8,512]{1,0:T(8,128)S(1)} %get-tuple-element.67.level, f32[64,128]{1,0:T(8,128)S(1)} %add_add_fusion.2.sums, f32[8,12,128,512]{3,2,1,0:T(8,128)S(1)} %get-tuple-element.62.matrix, f32[8,16,512]{2,1,0:T(8,128)S(1)} %get-tuple-element.63.peaks), custom_call_target="tpu_custom_call" | custom-call | tf_op jit(solution)/shard_map/rows/pallas_call | solution.py:281
  106.0 3.5 %collective-permute-start.35 = (f32[8,512]{1,0:T(8,128)S(1)}, f32[8,512]{1,0:T(8,128)S(1)}, u32[]{:S(2)}, u32[]{:S(2)}) collective-permute-start(f32[8,512]{1,0:T(8,128)S(1)} %rows.2.part), channel_id=1, source_target_pairs={{0,2},{1,3},{2,0},{3,1},{4,6},{5,7},{6,4},{7,5},{8,10},{9,11},{10,... | collective-permute-start | bytes 49160 | tf_op jit(solution)/shard_map/ppermute | solution.py:297
  112.1 3.1 %columns.4 = f32[64,128]{1,0:T(8,128)S(1)} custom-call(s32[320]{0:T(512)S(1)} %get-tuple-element.36.table, f32[8,512]{1,0:T(8,128)S(1)} %get-tuple-element.67.level, f32[8,512]{1,0:T(8,128)S(1)} %rows.2.part, f32[8,512]{1,0:T(8,128)S(1)} %collective-permute-done.34.near, f32[8,512]{1,0:T(8,128)S(1)} %collective-permute-done.35.far, ...), custom_call_target="tpu_custom_call" | custom-call | tf_op jit(solution)/shard_map/columns/pallas_call | solution.py:232
  115.3 5.6 %collective-permute-start.37 = (f32[64,128]{1,0:T(8,128)S(1)}, f32[64,128]{1,0:T(8,128)S(1)}, u32[]{:S(2)}, u32[]{:S(2)}) collective-permute-start(f32[64,128]{1,0:T(8,128)S(1)} %columns.4), channel_id=1, source_target_pairs={{0,4},{4,0},{8,12},{12,8},{16,20},{20,16},{24,28},{28,24},{32,36},... | collective-permute-start | bytes 98312 | tf_op jit(solution)/shard_map/ppermute | solution.py:31
  122.6 3.8 %collective-permute-start.39 = (f32[64,128]{1,0:T(8,128)S(1)}, f32[64,128]{1,0:T(8,128)S(1)}, u32[]{:S(2)}, u32[]{:S(2)}) collective-permute-start(f32[64,128]{1,0:T(8,128)S(1)} %add.55), channel_id=1, source_target_pairs={{0,16},{4,20},{8,24},{12,28},{16,0},{20,4},{24,8},{28,12},{32,48},... | collective-permute-start | bytes 98312 | tf_op jit(solution)/shard_map/ppermute | solution.py:31
  130.1 2.2 %collective-permute-start.42 = (f32[64,128]{1,0:T(8,128)S(1)}, f32[64,128]{1,0:T(8,128)S(1)}, u32[]{:S(2)}, u32[]{:S(2)}) collective-permute-start(f32[64,128]{1,0:T(8,128)S(1)} %add_add_fusion.1), channel_id=1, source_target_pairs={{0,64},{4,68},{8,72},{12,76},{16,80},{20,84},{24,88},{28,92},{32,9... | collective-permute-start | bytes 98312 | tf_op jit(solution)/shard_map/ppermute | solution.py:31
  135.1 2.8 %rows.3.part = f32[8,512]{1,0:T(8,128)S(1)} custom-call(s32[320]{0:T(512)S(1)} %get-tuple-element.36.table, f32[8,512]{1,0:T(8,128)S(1)} %get-tuple-element.67.level, f32[64,128]{1,0:T(8,128)S(1)} %add_add_fusion.sums, f32[8,12,128,512]{3,2,1,0:T(8,128)S(1)} %get-tuple-element.62.matrix, f32[8,16,512]{2,1,0:T(8,128)S(1)} %get-tuple-element.63.peaks), custom_call_target="tpu_custom_call" | custom-call | tf_op jit(solution)/shard_map/rows/pallas_call | solution.py:281
  142.6 3.2 %columns.5 = (f32[64,128]{1,0:T(8,128)S(1)}, f32[8,512]{1,0:T(8,128)}) custom-call(s32[320]{0:T(512)S(1)} %get-tuple-element.36.table, f32[8,512]{1,0:T(8,128)S(1)} %get-tuple-element.67.level, f32[8,512]{1,0:T(8,128)S(1)} %rows.3.part, f32[8,512]{1,0:T(8,128)S(1)} %collective-permute-done.44.near, f32[8,512]{1,0:T(8,128)S(1)} %collective-permute-done.45.far, ...), custom_call_target="tpu_custom_call" | custom-call | tf_op jit(solution)/shard_map/columns/pallas_call | solution.py:232
  145.8 17.0 %all_to_all.5 = f32[32,2,128]{2,1,0:T(2,128)S(1)} all-to-all(f32[32,2,128]{2,1,0:T(2,128)S(1)} %bitcast.39), channel_id=1, replica_groups=mesh['row'=32,'col'=4] {'row'}, dimensions={0} | all-to-all | bytes 65536 | tf_op jit(solution)/shard_map/all_to_all | solution.py:429
  (144 shorter events, 60.3 us)
Async XLA Ops:
  1.7 9.0 %collective-permute-start = (bf16[1,128,768]{2,1,0:T(8,128)(2,1)S(1)}, bf16[1,128,768]{2,1,0:T(8,128)(2,1)S(1)}, u32[]{:S(2)}, u32[]{:S(2)}) collective-permute-start(bf16[1,128,768]{2,1,0:T(8,128)(2,1)S(1)} %get-tuple-element.69), channel_id=1, source_target_pairs={{0,8},{4,12},{8,16},{12,20},{16,24},{20,28},{24,0},{28,4},{32,40},... | collective-permute-start | bytes 589832 | tf_op jit(solution)/shard_map/ppermute | solution.py:31
  3.9 15.5 %collective-permute-start.1 = (bf16[1,128,768]{2,1,0:T(8,128)(2,1)S(1)}, bf16[1,128,768]{2,1,0:T(8,128)(2,1)S(1)}, u32[]{:S(2)}, u32[]{:S(2)}) collective-permute-start(bf16[1,128,768]{2,1,0:T(8,128)(2,1)S(1)} %get-tuple-element.69), channel_id=1, source_target_pairs={{0,24},{4,28},{8,0},{12,4},{16,8},{20,12},{24,16},{28,20},{32,56},... | collective-permute-start | bytes 589832 | tf_op jit(solution)/shard_map/ppermute | solution.py:31
  5.4 14.0 %collective-permute-start.2 = (bf16[1,128,768]{2,1,0:T(8,128)(2,1)S(1)}, bf16[1,128,768]{2,1,0:T(8,128)(2,1)S(1)}, u32[]{:S(2)}, u32[]{:S(2)}) collective-permute-start(bf16[1,128,768]{2,1,0:T(8,128)(2,1)S(1)} %get-tuple-element.69), channel_id=1, source_target_pairs={{0,16},{4,20},{8,24},{12,28},{16,0},{20,4},{24,8},{28,12},{32,48},... | collective-permute-start | bytes 589832 | tf_op jit(solution)/shard_map/ppermute | solution.py:31
  7.0 12.4 %collective-permute-start.3 = (bf16[1,128,768]{2,1,0:T(8,128)(2,1)S(1)}, bf16[1,128,768]{2,1,0:T(8,128)(2,1)S(1)}, u32[]{:S(2)}, u32[]{:S(2)}) collective-permute-start(bf16[1,128,768]{2,1,0:T(8,128)(2,1)S(1)} %get-tuple-element.68), channel_id=1, source_target_pairs={{0,32},{4,36},{8,40},{12,44},{16,48},{20,52},{24,56},{28,60},{32,6... | collective-permute-start | bytes 589832 | tf_op jit(solution)/shard_map/ppermute | solution.py:31
  8.6 10.8 %collective-permute-start.4 = (bf16[1,128,768]{2,1,0:T(8,128)(2,1)S(1)}, bf16[1,128,768]{2,1,0:T(8,128)(2,1)S(1)}, u32[]{:S(2)}, u32[]{:S(2)}) collective-permute-start(bf16[1,128,768]{2,1,0:T(8,128)(2,1)S(1)} %get-tuple-element.68), channel_id=1, source_target_pairs={{0,96},{4,100},{8,104},{12,108},{16,112},{20,116},{24,120},{28,124... | collective-permute-start | bytes 589832 | tf_op jit(solution)/shard_map/ppermute | solution.py:31
  10.7 8.8 %collective-permute-start.5 = (bf16[1,128,768]{2,1,0:T(8,128)(2,1)S(1)}, bf16[1,128,768]{2,1,0:T(8,128)(2,1)S(1)}, u32[]{:S(2)}, u32[]{:S(2)}) collective-permute-start(bf16[1,128,768]{2,1,0:T(8,128)(2,1)S(1)} %get-tuple-element.68), channel_id=1, source_target_pairs={{0,64},{4,68},{8,72},{12,76},{16,80},{20,84},{24,88},{28,92},{32,9... | collective-permute-start | bytes 589832 | tf_op jit(solution)/shard_map/ppermute | solution.py:31
  19.6 6.3 %collective-permute-start.11 = (bf16[4,128,768]{2,1,0:T(8,128)(2,1)S(1)}, bf16[4,128,768]{2,1,0:T(8,128)(2,1)S(1)}, u32[]{:S(2)}, u32[]{:S(2)}) collective-permute-start(bf16[4,128,768]{2,1,0:T(8,128)(2,1)S(1)} %pad_maximum_fusion.1.refs_1_), channel_id=1, source_target_pairs={{0,4},{4,0},{8,12},{12,8},{16,20},{20,16},{24,28},{28,24},{32,36},... | collective-permute-start | bytes 2359304 | tf_op jit(solution)/shard_map/ppermute | solution.py:31
  22.3 5.5 %collective-permute-start.10 = (bf16[4,128,768]{2,1,0:T(8,128)(2,1)S(1)}, bf16[4,128,768]{2,1,0:T(8,128)(2,1)S(1)}, u32[]{:S(2)}, u32[]{:S(2)}) collective-permute-start(bf16[4,128,768]{2,1,0:T(8,128)(2,1)S(1)} %pad_maximum_fusion.refs_0_), channel_id=1, source_target_pairs={{0,4},{4,0},{8,12},{12,8},{16,20},{20,16},{24,28},{28,24},{32,36},... | collective-permute-start | bytes 2359304 | tf_op jit(solution)/shard_map/ppermute | solution.py:31
  22.4 20.0 %collective-permute-start.8 = (bf16[4,128,768]{2,1,0:T(8,128)(2,1)S(1)}, bf16[4,128,768]{2,1,0:T(8,128)(2,1)S(1)}, u32[]{:S(2)}, u32[]{:S(2)}) collective-permute-start(bf16[4,128,768]{2,1,0:T(8,128)(2,1)S(1)} %pad_maximum_fusion.1.refs_1_), channel_id=1, source_target_pairs={{0,8},{4,12},{8,16},{12,20},{16,24},{20,28},{24,0},{28,4},{32,40},... | collective-permute-start | bytes 2359304 | tf_op jit(solution)/shard_map/ppermute | solution.py:31
  22.8 21.6 %collective-permute-start.9 = (bf16[4,128,768]{2,1,0:T(8,128)(2,1)S(1)}, bf16[4,128,768]{2,1,0:T(8,128)(2,1)S(1)}, u32[]{:S(2)}, u32[]{:S(2)}) collective-permute-start(bf16[4,128,768]{2,1,0:T(8,128)(2,1)S(1)} %pad_maximum_fusion.1.refs_1_), channel_id=1, source_target_pairs={{0,24},{4,28},{8,0},{12,4},{16,8},{20,12},{24,16},{28,20},{32,56},... | collective-permute-start | bytes 2359304 | tf_op jit(solution)/shard_map/ppermute | solution.py:31
  25.1 19.3 %collective-permute-start.6 = (bf16[4,128,768]{2,1,0:T(8,128)(2,1)S(1)}, bf16[4,128,768]{2,1,0:T(8,128)(2,1)S(1)}, u32[]{:S(2)}, u32[]{:S(2)}) collective-permute-start(bf16[4,128,768]{2,1,0:T(8,128)(2,1)S(1)} %pad_maximum_fusion.refs_0_), channel_id=1, source_target_pairs={{0,32},{4,36},{8,40},{12,44},{16,48},{20,52},{24,56},{28,60},{32,6... | collective-permute-start | bytes 2359304 | tf_op jit(solution)/shard_map/ppermute | solution.py:31
  26.0 18.4 %collective-permute-start.7 = (bf16[4,128,768]{2,1,0:T(8,128)(2,1)S(1)}, bf16[4,128,768]{2,1,0:T(8,128)(2,1)S(1)}, u32[]{:S(2)}, u32[]{:S(2)}) collective-permute-start(bf16[4,128,768]{2,1,0:T(8,128)(2,1)S(1)} %pad_maximum_fusion.refs_0_), channel_id=1, source_target_pairs={{0,96},{4,100},{8,104},{12,108},{16,112},{20,116},{24,120},{28,124... | collective-permute-start | bytes 2359304 | tf_op jit(solution)/shard_map/ppermute | solution.py:31
  46.5 6.5 %collective-permute-start.18 = (bf16[4,128,768]{2,1,0:T(8,128)(2,1)S(1)}, bf16[4,128,768]{2,1,0:T(8,128)(2,1)S(1)}, u32[]{:S(2)}, u32[]{:S(2)}) collective-permute-start(bf16[4,128,768]{2,1,0:T(8,128)(2,1)S(1)} %collective-permute-done.8.refs_2_), channel_id=1, source_target_pairs={{0,4},{4,0},{8,12},{12,8},{16,20},{20,16},{24,28},{28,24},{32,36},... | collective-permute-start | bytes 2359304 | tf_op jit(solution)/shard_map/ppermute | solution.py:31
  46.9 7.1 %collective-permute-start.19 = (bf16[4,128,768]{2,1,0:T(8,128)(2,1)S(1)}, bf16[4,128,768]{2,1,0:T(8,128)(2,1)S(1)}, u32[]{:S(2)}, u32[]{:S(2)}) collective-permute-start(bf16[4,128,768]{2,1,0:T(8,128)(2,1)S(1)} %collective-permute-done.9.refs_3_), channel_id=1, source_target_pairs={{0,4},{4,0},{8,12},{12,8},{16,20},{20,16},{24,28},{28,24},{32,36},... | collective-permute-start | bytes 2359304 | tf_op jit(solution)/shard_map/ppermute | solution.py:31
  47.1 14.8 %collective-permute-start.12 = (bf16[2,128,768]{2,1,0:T(8,128)(2,1)S(1)}, bf16[2,128,768]{2,1,0:T(8,128)(2,1)S(1)}, u32[]{:S(2)}, u32[]{:S(2)}) collective-permute-start(bf16[2,128,768]{2,1,0:T(8,128)(2,1)S(1)} %slice.41), channel_id=1, source_target_pairs={{0,32},{4,36},{8,40},{12,44},{16,48},{20,52},{24,56},{28,60},{32,6... | collective-permute-start | bytes 1179656 | tf_op jit(solution)/shard_map/ppermute | solution.py:31
  48.3 13.7 %collective-permute-start.13 = (bf16[2,128,768]{2,1,0:T(8,128)(2,1)S(1)}, bf16[2,128,768]{2,1,0:T(8,128)(2,1)S(1)}, u32[]{:S(2)}, u32[]{:S(2)}) collective-permute-start(bf16[2,128,768]{2,1,0:T(8,128)(2,1)S(1)} %slice.42), channel_id=1, source_target_pairs={{0,96},{4,100},{8,104},{12,108},{16,112},{20,116},{24,120},{28,124... | collective-permute-start | bytes 1179656 | tf_op jit(solution)/shard_map/ppermute | solution.py:31
  50.9 11.4 %collective-permute-start.14 = (bf16[2,128,768]{2,1,0:T(8,128)(2,1)S(1)}, bf16[2,128,768]{2,1,0:T(8,128)(2,1)S(1)}, u32[]{:S(2)}, u32[]{:S(2)}) collective-permute-start(bf16[2,128,768]{2,1,0:T(8,128)(2,1)S(1)} %slice.43), channel_id=1, source_target_pairs={{0,8},{4,12},{8,16},{12,20},{16,24},{20,28},{24,0},{28,4},{32,40},... | collective-permute-start | bytes 1179656 | tf_op jit(solution)/shard_map/ppermute | solution.py:31
  53.0 9.7 %collective-permute-start.15 = (bf16[2,128,768]{2,1,0:T(8,128)(2,1)S(1)}, bf16[2,128,768]{2,1,0:T(8,128)(2,1)S(1)}, u32[]{:S(2)}, u32[]{:S(2)}) collective-permute-start(bf16[2,128,768]{2,1,0:T(8,128)(2,1)S(1)} %slice.44), channel_id=1, source_target_pairs={{0,24},{4,28},{8,0},{12,4},{16,8},{20,12},{24,16},{28,20},{32,56},... | collective-permute-start | bytes 1179656 | tf_op jit(solution)/shard_map/ppermute | solution.py:31
  75.9 4.9 %collective-permute-start.24 = (f32[2,8,512]{2,1,0:T(8,128)S(1)}, f32[2,8,512]{2,1,0:T(8,128)S(1)}, u32[]{:S(2)}, u32[]{:S(2)}) collective-permute-start(f32[2,8,512]{2,1,0:T(8,128)S(1)} %pad_maximum_fusion.2), channel_id=1, source_target_pairs={{0,1},{1,2},{2,3},{3,0},{4,5},{5,6},{6,7},{7,4},{8,9},{9,10},{10,1... | collective-permute-start | bytes 98312 | tf_op jit(solution)/shard_map/ppermute | solution.py:297
  88.9 8.2 %collective-permute-start.28 = (f32[64,128]{1,0:T(8,128)S(1)}, f32[64,128]{1,0:T(8,128)S(1)}, u32[]{:S(2)}, u32[]{:S(2)}) collective-permute-start(f32[64,128]{1,0:T(8,128)S(1)} %add.48), channel_id=1, source_target_pairs={{0,8},{4,12},{8,16},{12,20},{16,24},{20,28},{24,0},{28,4},{32,40},... | collective-permute-start | bytes 98312 | tf_op jit(solution)/shard_map/ppermute | solution.py:31
  106.0 4.8 %collective-permute-start.35 = (f32[8,512]{1,0:T(8,128)S(1)}, f32[8,512]{1,0:T(8,128)S(1)}, u32[]{:S(2)}, u32[]{:S(2)}) collective-permute-start(f32[8,512]{1,0:T(8,128)S(1)} %rows.2.part), channel_id=1, source_target_pairs={{0,2},{1,3},{2,0},{3,1},{4,6},{5,7},{6,4},{7,5},{8,10},{9,11},{10,... | collective-permute-start | bytes 49160 | tf_op jit(solution)/shard_map/ppermute | solution.py:297
  115.3 6.4 %collective-permute-start.37 = (f32[64,128]{1,0:T(8,128)S(1)}, f32[64,128]{1,0:T(8,128)S(1)}, u32[]{:S(2)}, u32[]{:S(2)}) collective-permute-start(f32[64,128]{1,0:T(8,128)S(1)} %columns.4), channel_id=1, source_target_pairs={{0,4},{4,0},{8,12},{12,8},{16,20},{20,16},{24,28},{28,24},{32,36},... | collective-permute-start | bytes 98312 | tf_op jit(solution)/shard_map/ppermute | solution.py:31
  121.7 4.8 %collective-permute-start.38 = (f32[64,128]{1,0:T(8,128)S(1)}, f32[64,128]{1,0:T(8,128)S(1)}, u32[]{:S(2)}, u32[]{:S(2)}) collective-permute-start(f32[64,128]{1,0:T(8,128)S(1)} %add.55), channel_id=1, source_target_pairs={{0,8},{4,12},{8,16},{12,20},{16,24},{20,28},{24,0},{28,4},{32,40},... | collective-permute-start | bytes 98312 | tf_op jit(solution)/shard_map/ppermute | solution.py:31
  122.6 5.5 %collective-permute-start.39 = (f32[64,128]{1,0:T(8,128)S(1)}, f32[64,128]{1,0:T(8,128)S(1)}, u32[]{:S(2)}, u32[]{:S(2)}) collective-permute-start(f32[64,128]{1,0:T(8,128)S(1)} %add.55), channel_id=1, source_target_pairs={{0,16},{4,20},{8,24},{12,28},{16,0},{20,4},{24,8},{28,12},{32,48},... | collective-permute-start | bytes 98312 | tf_op jit(solution)/shard_map/ppermute | solution.py:31
  (46 other events, 176.3 us)

commit v6 on v5

--- a/solution.py
+++ b/solution.py
@@ -33,6 +33,7 @@
 
 RING = (0, -1, 1, 2)
 STAGES = 3
+TOGETHER = (1, 2, 4)
 
 
 def tie(*arrays):
@@ -96,12 +97,16 @@
         peak_out[...] = jnp.full(peak_out.shape, NEGATIVE, jnp.float32)
         sum_out[...] = jnp.zeros(sum_out.shape, jnp.float32)
 
-    def one_block(s, carry):
-        group = s // SHARE
+    together = TOGETHER[stage]
+    largest = 8 // together if together > 1 else 4
+
+    def some_blocks(turn, carry):
+        group = turn * together // SHARE
         begin = table[SEGMENTS + group * (STAGES + 1) + stage]
-        live = table[LIVES + s * STAGES + stage]
-
-        @pl.when(lax.rem(s, SHARE) == 0)
+        alive = [table[LIVES + (turn * together + m) * STAGES + stage] for m in range(together)]
+        live = functools.reduce(jnp.maximum, alive)
+
+        @pl.when(lax.rem(turn * together, SHARE) == 0)
         def _():
             def arrive(entry, carry):
                 fetch(0, 0, group * listed + entry).wait()
@@ -111,30 +116,40 @@
 
         def batch(first, size):
             base = pl.multiple_of((group * listed + begin + first) * rows, rows)
-            scores = lax.dot_general(
-                held[pl.ds(base, size * rows), :],
-                source[s],
-                (((1,), (1,)), ((), ())),
-                preferred_element_type=jnp.float32,
-            )
-            for p in range(size):
-                one = scores[p * rows : (p + 1) * rows] * SCALE
-                peak = jnp.max(one, axis=0, keepdims=True)
-                lifted = jnp.exp2(one - peak)
-                matrix[s, begin + first + p] = lifted
-                peak_out[s, pl.ds(begin + first + p, 1), :] = peak
-                sum_out[s, pl.ds(begin + first + p, 1), :] = jnp.sum(lifted, axis=0, keepdims=True)
-
-        def four(q, carry):
-            batch(4 * q, 4)
+            vectors = held[pl.ds(base, size * rows), :]
+            scores = [
+                lax.dot_general(
+                    vectors,
+                    source[turn * together + m],
+                    (((1,), (1,)), ((), ())),
+                    preferred_element_type=jnp.float32,
+                )
+                for m in range(together)
+            ]
+            for m in range(together):
+                s = turn * together + m
+                for p in range(size):
+                    one = scores[m][p * rows : (p + 1) * rows] * SCALE
+                    peak = jnp.max(one, axis=0, keepdims=True)
+                    lifted = jnp.exp2(one - peak)
+                    matrix[s, begin + first + p] = lifted
+                    total = jnp.sum(lifted, axis=0, keepdims=True)
+                    if together > 1:
+                        used = first + p < alive[m]
+                        peak, total = jnp.where(used, peak, NEGATIVE), jnp.where(used, total, 0.0)
+                    peak_out[s, pl.ds(begin + first + p, 1), :] = peak
+                    sum_out[s, pl.ds(begin + first + p, 1), :] = total
+
+        def whole(q, carry):
+            batch(largest * q, largest)
             return carry
 
-        lax.fori_loop(0, live // 4, four, 0)
-        for size in (1, 2, 3):
-            pl.when(lax.rem(live, 4) == size)(functools.partial(batch, live - size, size))
+        lax.fori_loop(0, live // largest, whole, 0)
+        for size in range(1, largest):
+            pl.when(lax.rem(live, largest) == size)(functools.partial(batch, live - size, size))
         return carry
 
-    lax.fori_loop(0, blocks, one_block, 0)
+    lax.fori_loop(0, blocks // together, some_blocks, 0)
     if stage == STAGES - 1:
         for s in range(blocks):
             high = jnp.max(peak_out[s], axis=0, keepdims=True)

time: 163 us -> 161 us (0.988)
  starting transfers between devices: 69.6 us -> 66.2 us
    ppermute x38, starting transfers between devices: 57.8 us -> 54.4 us  [send(): return lax.ppermute(x, 'row', row_perm(dz, dy, dc))]
  transfers between devices with their start and end apart: 47 -> 47, of which waited for: 31 -> 30; matrix products, arithmetic and copies ran while one was open for 0% -> 0% of each run, Pallas kernels for 11% -> 13%
where the time goes in v6:
time: 161 us
  starting transfers between devices  66.2 us (41%)
  Pallas kernels  41.2 us (26%)
  waiting for transfers between devices  28.6 us (18%)
  blocking collectives  17.1 us (11%)
  local copies, waits for them, and re-layouts  5.66 us (4%)
    ppermute x38, starting transfers between devices, send(): return lax.ppermute(x, 'row', row_perm(dz, dy, dc))  54.4 us
    ppermute x38, waiting for transfers between devices, send(): return lax.ppermute(x, 'row', row_perm(dz, dy, dc))  22.7 us
    pallas_call x3, Pallas kernels, score_stage(): pl.pallas_call(functools.partial(score_kernel, stage, listed), in_specs=[...  21.3 us
    all_to_all x1, blocking collectives, shards(): lax.all_to_all(sums.reshape(row_count, target_blocks, quarter), 'row', sp...  17.1 us
    ppermute x9, starting transfers between devices, from_columns(): lax.ppermute(x, 'col', [(i, (i + d) % 4) for i in range(4)])  11.9 us
    pallas_call x3, Pallas kernels, column_pass(): pl.pallas_call(functools.partial(column_kernel, final), in_specs=[smem] +...  9.87 us
    pallas_call x2, Pallas kernels, row_pass(): pl.pallas_call(row_kernel, in_specs=[smem] + [vmem] * 4, out_specs=vmem,...  5.93 us
    ppermute x9, waiting for transfers between devices, from_columns(): lax.ppermute(x, 'col', [(i, (i + d) % 4) for i in range(4)])  5.9 us
  transfers between devices with their start and end apart: 47, of which 30 were waited for; matrix products, arithmetic and copies ran while one was open for 0% of the time, Pallas kernels for 13%

profile of v6, /device:TPU:1, one launch (start us, length us, event | category | flops | bytes accessed | tf_op | source)
XLA Modules:
  0.0 160.8 jit_solution(5693897785654615500)
XLA Ops:
  1.7 2.2 %collective-permute-start = (bf16[1,128,768]{2,1,0:T(8,128)(2,1)S(1)}, bf16[1,128,768]{2,1,0:T(8,128)(2,1)S(1)}, u32[]{:S(2)}, u32[]{:S(2)}) collective-permute-start(bf16[1,128,768]{2,1,0:T(8,128)(2,1)S(1)} %get-tuple-element.69), channel_id=1, source_target_pairs={{0,8},{4,12},{8,16},{12,20},{16,24},{20,28},{24,0},{28,4},{32,40},... | collective-permute-start | bytes 589832 | tf_op jit(solution)/shard_map/ppermute | solution.py:31
  8.6 2.1 %collective-permute-start.4 = (bf16[1,128,768]{2,1,0:T(8,128)(2,1)S(1)}, bf16[1,128,768]{2,1,0:T(8,128)(2,1)S(1)}, u32[]{:S(2)}, u32[]{:S(2)}) collective-permute-start(bf16[1,128,768]{2,1,0:T(8,128)(2,1)S(1)} %get-tuple-element.68), channel_id=1, source_target_pairs={{0,96},{4,100},{8,104},{12,108},{16,112},{20,116},{24,120},{28,124... | collective-permute-start | bytes 589832 | tf_op jit(solution)/shard_map/ppermute | solution.py:31
  10.7 2.6 %collective-permute-start.5 = (bf16[1,128,768]{2,1,0:T(8,128)(2,1)S(1)}, bf16[1,128,768]{2,1,0:T(8,128)(2,1)S(1)}, u32[]{:S(2)}, u32[]{:S(2)}) collective-permute-start(bf16[1,128,768]{2,1,0:T(8,128)(2,1)S(1)} %get-tuple-element.68), channel_id=1, source_target_pairs={{0,64},{4,68},{8,72},{12,76},{16,80},{20,84},{24,88},{28,92},{32,9... | collective-permute-start | bytes 589832 | tf_op jit(solution)/shard_map/ppermute | solution.py:31
  15.3 4.1 %tables.1 = (s32[320]{0:T(512)S(1)}, bf16[8,512,768]{2,1,0:T(8,128)(2,1)S(1)}) custom-call(s32[1]{0:T(128)} %bitcast.me, s32[8,12]{1,0:T(8,128)S(1)} %copy-done, s32[8]{0:T(128)S(1)} %copy-done.1, s32[64]{0:T(128)S(1)} %copy-done.2, bf16[8,512,768]{2,1,0:T(8,128)(2,1)} %source.1), custom_call_target="tpu_custom_call" | custom-call | tf_op jit(solution)/shard_map/tables/pallas_call | solution.py:381
  19.6 2.5 %collective-permute-start.11 = (bf16[4,128,768]{2,1,0:T(8,128)(2,1)S(1)}, bf16[4,128,768]{2,1,0:T(8,128)(2,1)S(1)}, u32[]{:S(2)}, u32[]{:S(2)}) collective-permute-start(bf16[4,128,768]{2,1,0:T(8,128)(2,1)S(1)} %pad_maximum_fusion.1.refs_1_), channel_id=1, source_target_pairs={{0,4},{4,0},{8,12},{12,8},{16,20},{20,16},{24,28},{28,24},{32,36},... | collective-permute-start | bytes 2359304 | tf_op jit(solution)/shard_map/ppermute | solution.py:31
  22.8 2.3 %collective-permute-start.9 = (bf16[4,128,768]{2,1,0:T(8,128)(2,1)S(1)}, bf16[4,128,768]{2,1,0:T(8,128)(2,1)S(1)}, u32[]{:S(2)}, u32[]{:S(2)}) collective-permute-start(bf16[4,128,768]{2,1,0:T(8,128)(2,1)S(1)} %pad_maximum_fusion.1.refs_1_), channel_id=1, source_target_pairs={{0,24},{4,28},{8,0},{12,4},{16,8},{20,12},{24,16},{28,20},{32,56},... | collective-permute-start | bytes 2359304 | tf_op jit(solution)/shard_map/ppermute | solution.py:31
  28.7 7.8 %scores.3 = (f32[8,12,128,512]{3,2,1,0:T(8,128)S(1)}, f32[8,16,512]{2,1,0:T(8,128)S(1)}, f32[8,16,512]{2,1,0:T(8,128)S(1)}) custom-call(s32[320]{0:T(512)S(1)} %get-tuple-element.36.table, bf16[8,512,768]{2,1,0:T(8,128)(2,1)S(1)} %get-tuple-element.37.source, bf16[4,128,768]{2,1,0:T(8,128)(2,1)} %copy-done.4, bf16[4,128,768]{2,1,0:T(8,128)(2,1)} %copy-done.3, ...), custom_call_target="tpu_custom_call" | custom-call | flops 2415919104 | bytes 6291456 | tf_op jit(solution)/shard_map/scores/pallas_call | solution.py:173
  36.6 5.8 %collective-permute-done.8.refs_2_ = bf16[4,128,768]{2,1,0:T(8,128)(2,1)S(1)} collective-permute-done((bf16[4,128,768]{2,1,0:T(8,128)(2,1)S(1)}, bf16[4,128,768]{2,1,0:T(8,128)(2,1)S(1)}, u32[]{:S(2)}, u32[]{:S(2)}) %collective-permute-start.8) | collective-permute-done | bytes 786464 | tf_op jit(solution)/shard_map/ppermute | solution.py:31
  48.3 2.6 %collective-permute-start.13 = (bf16[2,128,768]{2,1,0:T(8,128)(2,1)S(1)}, bf16[2,128,768]{2,1,0:T(8,128)(2,1)S(1)}, u32[]{:S(2)}, u32[]{:S(2)}) collective-permute-start(bf16[2,128,768]{2,1,0:T(8,128)(2,1)S(1)} %slice.42), channel_id=1, source_target_pairs={{0,96},{4,100},{8,104},{12,108},{16,112},{20,116},{24,120},{28,124... | collective-permute-start | bytes 1179656 | tf_op jit(solution)/shard_map/ppermute | solution.py:31
  54.8 8.9 %scores.4 = (f32[8,12,128,512]{3,2,1,0:T(8,128)S(1)}, f32[8,16,512]{2,1,0:T(8,128)S(1)}, f32[8,16,512]{2,1,0:T(8,128)S(1)}) custom-call(s32[320]{0:T(512)S(1)} %get-tuple-element.36.table, bf16[8,512,768]{2,1,0:T(8,128)(2,1)S(1)} %get-tuple-element.37.source, ...), custom_call_target="tpu_custom_call", output_to_operand_aliasing={{0}: (10, {}), {1}: (11, {}), {2}: (12, {})} | custom-call | flops 4831838208 | bytes 12582912 | tf_op jit(solution)/shard_map/scores/pallas_call | solution.py:173
  69.0 4.6 %scores.5 = (f32[8,12,128,512]{3,2,1,0:T(8,128)S(1)}, f32[8,16,512]{2,1,0:T(8,128)S(1)}, f32[8,16,512]{2,1,0:T(8,128)S(1)}, f32[8,512]{1,0:T(8,128)S(1)}, f32[8,512]{1,0:T(8,128)S(1)}) custom-call(s32[320]{0:T(512)S(1)} %get-tuple-element.36.table, ...), custom_call_target="tpu_custom_call", output_to_operand_aliasing={{0}: (10, {}), {1}: (11, {}), {2}: (12, {})} | custom-call | flops 2415919104 | bytes 6291456 | tf_op jit(solution)/shard_map/scores/pallas_call | solution.py:173
  74.8 2.5 %collective-permute-start.25 = (f32[2,8,512]{2,1,0:T(8,128)S(1)}, f32[2,8,512]{2,1,0:T(8,128)S(1)}, u32[]{:S(2)}, u32[]{:S(2)}) collective-permute-start(f32[2,8,512]{2,1,0:T(8,128)S(1)} %pad_maximum_fusion.2), channel_id=1, source_target_pairs={{0,2},{1,3},{2,0},{3,1},{4,6},{5,7},{6,4},{7,5},{8,10},{9,11},{10,... | collective-permute-start | bytes 98312 | tf_op jit(solution)/shard_map/ppermute | solution.py:312
  80.1 3.3 %columns.3 = f32[64,128]{1,0:T(8,128)S(1)} custom-call(s32[320]{0:T(512)S(1)} %get-tuple-element.36.table, f32[8,512]{1,0:T(8,128)S(1)} %get-tuple-element.67.level, f32[8,512]{1,0:T(8,128)S(1)} %get-tuple-element.72.part, f32[8,512]{1,0:T(8,128)S(1)} %get-tuple-element.71.near, f32[8,512]{1,0:T(8,128)S(1)} %get-tuple-element.70.far, ...), custom_call_target="tpu_custom_call" | custom-call | tf_op jit(solution)/shard_map/columns/pallas_call | solution.py:247
  83.4 6.2 %collective-permute-start.27 = (f32[64,128]{1,0:T(8,128)S(1)}, f32[64,128]{1,0:T(8,128)S(1)}, u32[]{:S(2)}, u32[]{:S(2)}) collective-permute-start(f32[64,128]{1,0:T(8,128)S(1)} %columns.3), channel_id=1, source_target_pairs={{0,4},{4,0},{8,12},{12,8},{16,20},{20,16},{24,28},{28,24},{32,36},... | collective-permute-start | bytes 98312 | tf_op jit(solution)/shard_map/ppermute | solution.py:31
  95.8 2.1 %collective-permute-start.32 = (f32[64,128]{1,0:T(8,128)S(1)}, f32[64,128]{1,0:T(8,128)S(1)}, u32[]{:S(2)}, u32[]{:S(2)}) collective-permute-start(f32[64,128]{1,0:T(8,128)S(1)} %add_add_fusion.3), channel_id=1, source_target_pairs={{0,64},{4,68},{8,72},{12,76},{16,80},{20,84},{24,88},{28,92},{32,9... | collective-permute-start | bytes 98312 | tf_op jit(solution)/shard_map/ppermute | solution.py:31
  100.7 3.0 %rows.2.part = f32[8,512]{1,0:T(8,128)S(1)} custom-call(s32[320]{0:T(512)S(1)} %get-tuple-element.36.table, f32[8,512]{1,0:T(8,128)S(1)} %get-tuple-element.67.level, f32[64,128]{1,0:T(8,128)S(1)} %add_add_fusion.2.sums, f32[8,12,128,512]{3,2,1,0:T(8,128)S(1)} %get-tuple-element.62.matrix, f32[8,16,512]{2,1,0:T(8,128)S(1)} %get-tuple-element.63.peaks), custom_call_target="tpu_custom_call" | custom-call | tf_op jit(solution)/shard_map/rows/pallas_call | solution.py:296
  104.0 3.3 %collective-permute-start.35 = (f32[8,512]{1,0:T(8,128)S(1)}, f32[8,512]{1,0:T(8,128)S(1)}, u32[]{:S(2)}, u32[]{:S(2)}) collective-permute-start(f32[8,512]{1,0:T(8,128)S(1)} %rows.2.part), channel_id=1, source_target_pairs={{0,2},{1,3},{2,0},{3,1},{4,6},{5,7},{6,4},{7,5},{8,10},{9,11},{10,... | collective-permute-start | bytes 49160 | tf_op jit(solution)/shard_map/ppermute | solution.py:312
  109.8 3.3 %columns.4 = f32[64,128]{1,0:T(8,128)S(1)} custom-call(s32[320]{0:T(512)S(1)} %get-tuple-element.36.table, f32[8,512]{1,0:T(8,128)S(1)} %get-tuple-element.67.level, f32[8,512]{1,0:T(8,128)S(1)} %rows.2.part, f32[8,512]{1,0:T(8,128)S(1)} %collective-permute-done.34.near, f32[8,512]{1,0:T(8,128)S(1)} %collective-permute-done.35.far, ...), custom_call_target="tpu_custom_call" | custom-call | tf_op jit(solution)/shard_map/columns/pallas_call | solution.py:247
  113.1 5.1 %collective-permute-start.37 = (f32[64,128]{1,0:T(8,128)S(1)}, f32[64,128]{1,0:T(8,128)S(1)}, u32[]{:S(2)}, u32[]{:S(2)}) collective-permute-start(f32[64,128]{1,0:T(8,128)S(1)} %columns.4), channel_id=1, source_target_pairs={{0,4},{4,0},{8,12},{12,8},{16,20},{20,16},{24,28},{28,24},{32,36},... | collective-permute-start | bytes 98312 | tf_op jit(solution)/shard_map/ppermute | solution.py:31
  120.4 2.8 %collective-permute-start.39 = (f32[64,128]{1,0:T(8,128)S(1)}, f32[64,128]{1,0:T(8,128)S(1)}, u32[]{:S(2)}, u32[]{:S(2)}) collective-permute-start(f32[64,128]{1,0:T(8,128)S(1)} %add.55), channel_id=1, source_target_pairs={{0,16},{4,20},{8,24},{12,28},{16,0},{20,4},{24,8},{28,12},{32,48},... | collective-permute-start | bytes 98312 | tf_op jit(solution)/shard_map/ppermute | solution.py:31
  131.7 3.0 %rows.3.part = f32[8,512]{1,0:T(8,128)S(1)} custom-call(s32[320]{0:T(512)S(1)} %get-tuple-element.36.table, f32[8,512]{1,0:T(8,128)S(1)} %get-tuple-element.67.level, f32[64,128]{1,0:T(8,128)S(1)} %add_add_fusion.sums, f32[8,12,128,512]{3,2,1,0:T(8,128)S(1)} %get-tuple-element.62.matrix, f32[8,16,512]{2,1,0:T(8,128)S(1)} %get-tuple-element.63.peaks), custom_call_target="tpu_custom_call" | custom-call | tf_op jit(solution)/shard_map/rows/pallas_call | solution.py:296
  134.7 2.4 %collective-permute-start.45 = (f32[8,512]{1,0:T(8,128)S(1)}, f32[8,512]{1,0:T(8,128)S(1)}, u32[]{:S(2)}, u32[]{:S(2)}) collective-permute-start(f32[8,512]{1,0:T(8,128)S(1)} %rows.3.part), channel_id=1, source_target_pairs={{0,2},{1,3},{2,0},{3,1},{4,6},{5,7},{6,4},{7,5},{8,10},{9,11},{10,... | collective-permute-start | bytes 49160 | tf_op jit(solution)/shard_map/ppermute | solution.py:312
  139.7 3.3 %columns.5 = (f32[64,128]{1,0:T(8,128)S(1)}, f32[8,512]{1,0:T(8,128)}) custom-call(s32[320]{0:T(512)S(1)} %get-tuple-element.36.table, f32[8,512]{1,0:T(8,128)S(1)} %get-tuple-element.67.level, f32[8,512]{1,0:T(8,128)S(1)} %rows.3.part, f32[8,512]{1,0:T(8,128)S(1)} %collective-permute-done.44.near, f32[8,512]{1,0:T(8,128)S(1)} %collective-permute-done.45.far, ...), custom_call_target="tpu_custom_call" | custom-call | tf_op jit(solution)/shard_map/columns/pallas_call | solution.py:247
  143.1 17.1 %all_to_all.5 = f32[32,2,128]{2,1,0:T(2,128)S(1)} all-to-all(f32[32,2,128]{2,1,0:T(2,128)S(1)} %bitcast.39), channel_id=1, replica_groups=mesh['row'=32,'col'=4] {'row'}, dimensions={0} | all-to-all | bytes 65536 | tf_op jit(solution)/shard_map/all_to_all | solution.py:444
  (144 shorter events, 57.0 us)
Async XLA Ops:
  1.7 9.0 %collective-permute-start = (bf16[1,128,768]{2,1,0:T(8,128)(2,1)S(1)}, bf16[1,128,768]{2,1,0:T(8,128)(2,1)S(1)}, u32[]{:S(2)}, u32[]{:S(2)}) collective-permute-start(bf16[1,128,768]{2,1,0:T(8,128)(2,1)S(1)} %get-tuple-element.69), channel_id=1, source_target_pairs={{0,8},{4,12},{8,16},{12,20},{16,24},{20,28},{24,0},{28,4},{32,40},... | collective-permute-start | bytes 589832 | tf_op jit(solution)/shard_map/ppermute | solution.py:31
  3.9 15.5 %collective-permute-start.1 = (bf16[1,128,768]{2,1,0:T(8,128)(2,1)S(1)}, bf16[1,128,768]{2,1,0:T(8,128)(2,1)S(1)}, u32[]{:S(2)}, u32[]{:S(2)}) collective-permute-start(bf16[1,128,768]{2,1,0:T(8,128)(2,1)S(1)} %get-tuple-element.69), channel_id=1, source_target_pairs={{0,24},{4,28},{8,0},{12,4},{16,8},{20,12},{24,16},{28,20},{32,56},... | collective-permute-start | bytes 589832 | tf_op jit(solution)/shard_map/ppermute | solution.py:31
  5.4 14.0 %collective-permute-start.2 = (bf16[1,128,768]{2,1,0:T(8,128)(2,1)S(1)}, bf16[1,128,768]{2,1,0:T(8,128)(2,1)S(1)}, u32[]{:S(2)}, u32[]{:S(2)}) collective-permute-start(bf16[1,128,768]{2,1,0:T(8,128)(2,1)S(1)} %get-tuple-element.69), channel_id=1, source_target_pairs={{0,16},{4,20},{8,24},{12,28},{16,0},{20,4},{24,8},{28,12},{32,48},... | collective-permute-start | bytes 589832 | tf_op jit(solution)/shard_map/ppermute | solution.py:31
  7.0 12.4 %collective-permute-start.3 = (bf16[1,128,768]{2,1,0:T(8,128)(2,1)S(1)}, bf16[1,128,768]{2,1,0:T(8,128)(2,1)S(1)}, u32[]{:S(2)}, u32[]{:S(2)}) collective-permute-start(bf16[1,128,768]{2,1,0:T(8,128)(2,1)S(1)} %get-tuple-element.68), channel_id=1, source_target_pairs={{0,32},{4,36},{8,40},{12,44},{16,48},{20,52},{24,56},{28,60},{32,6... | collective-permute-start | bytes 589832 | tf_op jit(solution)/shard_map/ppermute | solution.py:31
  8.6 10.8 %collective-permute-start.4 = (bf16[1,128,768]{2,1,0:T(8,128)(2,1)S(1)}, bf16[1,128,768]{2,1,0:T(8,128)(2,1)S(1)}, u32[]{:S(2)}, u32[]{:S(2)}) collective-permute-start(bf16[1,128,768]{2,1,0:T(8,128)(2,1)S(1)} %get-tuple-element.68), channel_id=1, source_target_pairs={{0,96},{4,100},{8,104},{12,108},{16,112},{20,116},{24,120},{28,124... | collective-permute-start | bytes 589832 | tf_op jit(solution)/shard_map/ppermute | solution.py:31
  10.7 8.8 %collective-permute-start.5 = (bf16[1,128,768]{2,1,0:T(8,128)(2,1)S(1)}, bf16[1,128,768]{2,1,0:T(8,128)(2,1)S(1)}, u32[]{:S(2)}, u32[]{:S(2)}) collective-permute-start(bf16[1,128,768]{2,1,0:T(8,128)(2,1)S(1)} %get-tuple-element.68), channel_id=1, source_target_pairs={{0,64},{4,68},{8,72},{12,76},{16,80},{20,84},{24,88},{28,92},{32,9... | collective-permute-start | bytes 589832 | tf_op jit(solution)/shard_map/ppermute | solution.py:31
  19.6 6.3 %collective-permute-start.11 = (bf16[4,128,768]{2,1,0:T(8,128)(2,1)S(1)}, bf16[4,128,768]{2,1,0:T(8,128)(2,1)S(1)}, u32[]{:S(2)}, u32[]{:S(2)}) collective-permute-start(bf16[4,128,768]{2,1,0:T(8,128)(2,1)S(1)} %pad_maximum_fusion.1.refs_1_), channel_id=1, source_target_pairs={{0,4},{4,0},{8,12},{12,8},{16,20},{20,16},{24,28},{28,24},{32,36},... | collective-permute-start | bytes 2359304 | tf_op jit(solution)/shard_map/ppermute | solution.py:31
  22.3 5.5 %collective-permute-start.10 = (bf16[4,128,768]{2,1,0:T(8,128)(2,1)S(1)}, bf16[4,128,768]{2,1,0:T(8,128)(2,1)S(1)}, u32[]{:S(2)}, u32[]{:S(2)}) collective-permute-start(bf16[4,128,768]{2,1,0:T(8,128)(2,1)S(1)} %pad_maximum_fusion.refs_0_), channel_id=1, source_target_pairs={{0,4},{4,0},{8,12},{12,8},{16,20},{20,16},{24,28},{28,24},{32,36},... | collective-permute-start | bytes 2359304 | tf_op jit(solution)/shard_map/ppermute | solution.py:31
  22.4 20.0 %collective-permute-start.8 = (bf16[4,128,768]{2,1,0:T(8,128)(2,1)S(1)}, bf16[4,128,768]{2,1,0:T(8,128)(2,1)S(1)}, u32[]{:S(2)}, u32[]{:S(2)}) collective-permute-start(bf16[4,128,768]{2,1,0:T(8,128)(2,1)S(1)} %pad_maximum_fusion.1.refs_1_), channel_id=1, source_target_pairs={{0,8},{4,12},{8,16},{12,20},{16,24},{20,28},{24,0},{28,4},{32,40},... | collective-permute-start | bytes 2359304 | tf_op jit(solution)/shard_map/ppermute | solution.py:31
  22.8 21.6 %collective-permute-start.9 = (bf16[4,128,768]{2,1,0:T(8,128)(2,1)S(1)}, bf16[4,128,768]{2,1,0:T(8,128)(2,1)S(1)}, u32[]{:S(2)}, u32[]{:S(2)}) collective-permute-start(bf16[4,128,768]{2,1,0:T(8,128)(2,1)S(1)} %pad_maximum_fusion.1.refs_1_), channel_id=1, source_target_pairs={{0,24},{4,28},{8,0},{12,4},{16,8},{20,12},{24,16},{28,20},{32,56},... | collective-permute-start | bytes 2359304 | tf_op jit(solution)/shard_map/ppermute | solution.py:31
  25.1 19.3 %collective-permute-start.6 = (bf16[4,128,768]{2,1,0:T(8,128)(2,1)S(1)}, bf16[4,128,768]{2,1,0:T(8,128)(2,1)S(1)}, u32[]{:S(2)}, u32[]{:S(2)}) collective-permute-start(bf16[4,128,768]{2,1,0:T(8,128)(2,1)S(1)} %pad_maximum_fusion.refs_0_), channel_id=1, source_target_pairs={{0,32},{4,36},{8,40},{12,44},{16,48},{20,52},{24,56},{28,60},{32,6... | collective-permute-start | bytes 2359304 | tf_op jit(solution)/shard_map/ppermute | solution.py:31
  26.0 18.4 %collective-permute-start.7 = (bf16[4,128,768]{2,1,0:T(8,128)(2,1)S(1)}, bf16[4,128,768]{2,1,0:T(8,128)(2,1)S(1)}, u32[]{:S(2)}, u32[]{:S(2)}) collective-permute-start(bf16[4,128,768]{2,1,0:T(8,128)(2,1)S(1)} %pad_maximum_fusion.refs_0_), channel_id=1, source_target_pairs={{0,96},{4,100},{8,104},{12,108},{16,112},{20,116},{24,120},{28,124... | collective-permute-start | bytes 2359304 | tf_op jit(solution)/shard_map/ppermute | solution.py:31
  46.4 4.5 %collective-permute-start.17 = (bf16[4,128,768]{2,1,0:T(8,128)(2,1)S(1)}, bf16[4,128,768]{2,1,0:T(8,128)(2,1)S(1)}, u32[]{:S(2)}, u32[]{:S(2)}) collective-permute-start(bf16[4,128,768]{2,1,0:T(8,128)(2,1)S(1)} %collective-permute-done.7.refs_1_), channel_id=1, source_target_pairs={{0,4},{4,0},{8,12},{12,8},{16,20},{20,16},{24,28},{28,24},{32,36},... | collective-permute-start | bytes 2359304 | tf_op jit(solution)/shard_map/ppermute | solution.py:31
  46.5 6.5 %collective-permute-start.18 = (bf16[4,128,768]{2,1,0:T(8,128)(2,1)S(1)}, bf16[4,128,768]{2,1,0:T(8,128)(2,1)S(1)}, u32[]{:S(2)}, u32[]{:S(2)}) collective-permute-start(bf16[4,128,768]{2,1,0:T(8,128)(2,1)S(1)} %collective-permute-done.8.refs_2_), channel_id=1, source_target_pairs={{0,4},{4,0},{8,12},{12,8},{16,20},{20,16},{24,28},{28,24},{32,36},... | collective-permute-start | bytes 2359304 | tf_op jit(solution)/shard_map/ppermute | solution.py:31
  46.9 7.1 %collective-permute-start.19 = (bf16[4,128,768]{2,1,0:T(8,128)(2,1)S(1)}, bf16[4,128,768]{2,1,0:T(8,128)(2,1)S(1)}, u32[]{:S(2)}, u32[]{:S(2)}) collective-permute-start(bf16[4,128,768]{2,1,0:T(8,128)(2,1)S(1)} %collective-permute-done.9.refs_3_), channel_id=1, source_target_pairs={{0,4},{4,0},{8,12},{12,8},{16,20},{20,16},{24,28},{28,24},{32,36},... | collective-permute-start | bytes 2359304 | tf_op jit(solution)/shard_map/ppermute | solution.py:31
  47.1 16.6 %collective-permute-start.12 = (bf16[2,128,768]{2,1,0:T(8,128)(2,1)S(1)}, bf16[2,128,768]{2,1,0:T(8,128)(2,1)S(1)}, u32[]{:S(2)}, u32[]{:S(2)}) collective-permute-start(bf16[2,128,768]{2,1,0:T(8,128)(2,1)S(1)} %slice.41), channel_id=1, source_target_pairs={{0,32},{4,36},{8,40},{12,44},{16,48},{20,52},{24,56},{28,60},{32,6... | collective-permute-start | bytes 1179656 | tf_op jit(solution)/shard_map/ppermute | solution.py:31
  48.3 15.5 %collective-permute-start.13 = (bf16[2,128,768]{2,1,0:T(8,128)(2,1)S(1)}, bf16[2,128,768]{2,1,0:T(8,128)(2,1)S(1)}, u32[]{:S(2)}, u32[]{:S(2)}) collective-permute-start(bf16[2,128,768]{2,1,0:T(8,128)(2,1)S(1)} %slice.42), channel_id=1, source_target_pairs={{0,96},{4,100},{8,104},{12,108},{16,112},{20,116},{24,120},{28,124... | collective-permute-start | bytes 1179656 | tf_op jit(solution)/shard_map/ppermute | solution.py:31
  50.9 12.9 %collective-permute-start.14 = (bf16[2,128,768]{2,1,0:T(8,128)(2,1)S(1)}, bf16[2,128,768]{2,1,0:T(8,128)(2,1)S(1)}, u32[]{:S(2)}, u32[]{:S(2)}) collective-permute-start(bf16[2,128,768]{2,1,0:T(8,128)(2,1)S(1)} %slice.43), channel_id=1, source_target_pairs={{0,8},{4,12},{8,16},{12,20},{16,24},{20,28},{24,0},{28,4},{32,40},... | collective-permute-start | bytes 1179656 | tf_op jit(solution)/shard_map/ppermute | solution.py:31
  53.0 10.8 %collective-permute-start.15 = (bf16[2,128,768]{2,1,0:T(8,128)(2,1)S(1)}, bf16[2,128,768]{2,1,0:T(8,128)(2,1)S(1)}, u32[]{:S(2)}, u32[]{:S(2)}) collective-permute-start(bf16[2,128,768]{2,1,0:T(8,128)(2,1)S(1)} %slice.44), channel_id=1, source_target_pairs={{0,24},{4,28},{8,0},{12,4},{16,8},{20,12},{24,16},{28,20},{32,56},... | collective-permute-start | bytes 1179656 | tf_op jit(solution)/shard_map/ppermute | solution.py:31
  73.6 4.9 %collective-permute-start.24 = (f32[2,8,512]{2,1,0:T(8,128)S(1)}, f32[2,8,512]{2,1,0:T(8,128)S(1)}, u32[]{:S(2)}, u32[]{:S(2)}) collective-permute-start(f32[2,8,512]{2,1,0:T(8,128)S(1)} %pad_maximum_fusion.2), channel_id=1, source_target_pairs={{0,1},{1,2},{2,3},{3,0},{4,5},{5,6},{6,7},{7,4},{8,9},{9,10},{10,1... | collective-permute-start | bytes 98312 | tf_op jit(solution)/shard_map/ppermute | solution.py:312
  83.4 7.1 %collective-permute-start.27 = (f32[64,128]{1,0:T(8,128)S(1)}, f32[64,128]{1,0:T(8,128)S(1)}, u32[]{:S(2)}, u32[]{:S(2)}) collective-permute-start(f32[64,128]{1,0:T(8,128)S(1)} %columns.3), channel_id=1, source_target_pairs={{0,4},{4,0},{8,12},{12,8},{16,20},{20,16},{24,28},{28,24},{32,36},... | collective-permute-start | bytes 98312 | tf_op jit(solution)/shard_map/ppermute | solution.py:31
  104.0 4.6 %collective-permute-start.35 = (f32[8,512]{1,0:T(8,128)S(1)}, f32[8,512]{1,0:T(8,128)S(1)}, u32[]{:S(2)}, u32[]{:S(2)}) collective-permute-start(f32[8,512]{1,0:T(8,128)S(1)} %rows.2.part), channel_id=1, source_target_pairs={{0,2},{1,3},{2,0},{3,1},{4,6},{5,7},{6,4},{7,5},{8,10},{9,11},{10,... | collective-permute-start | bytes 49160 | tf_op jit(solution)/shard_map/ppermute | solution.py:312
  113.1 5.9 %collective-permute-start.37 = (f32[64,128]{1,0:T(8,128)S(1)}, f32[64,128]{1,0:T(8,128)S(1)}, u32[]{:S(2)}, u32[]{:S(2)}) collective-permute-start(f32[64,128]{1,0:T(8,128)S(1)} %columns.4), channel_id=1, source_target_pairs={{0,4},{4,0},{8,12},{12,8},{16,20},{20,16},{24,28},{28,24},{32,36},... | collective-permute-start | bytes 98312 | tf_op jit(solution)/shard_map/ppermute | solution.py:31
  120.4 4.5 %collective-permute-start.39 = (f32[64,128]{1,0:T(8,128)S(1)}, f32[64,128]{1,0:T(8,128)S(1)}, u32[]{:S(2)}, u32[]{:S(2)}) collective-permute-start(f32[64,128]{1,0:T(8,128)S(1)} %add.55), channel_id=1, source_target_pairs={{0,16},{4,20},{8,24},{12,28},{16,0},{20,4},{24,8},{28,12},{32,48},... | collective-permute-start | bytes 98312 | tf_op jit(solution)/shard_map/ppermute | solution.py:31
  (46 other events, 170.6 us)

commit v7 on v6

--- a/solution.py
+++ b/solution.py
@@ -61,7 +61,7 @@
     return stages
 
 
-SLOTS, DEST, SEGMENTS, LIVES, ORDER, ALIVE, COUNTS, TABLE = 0, 24, 88, 96, 120, 216, 312, 320
+SLOTS, DEST, SEGMENTS, LIVES, ORDER, USERS, COUNTS, USES, TABLE = 0, 24, 88, 96, 120, 216, 312, 320, 344
 
 
 def score_kernel(stage, listed, table, source, *refs):
@@ -207,18 +207,22 @@
     for g in range(blocks // SHARE):
 
         def one_entry(k, carry):
-            def one_source(s, acc):
+            entry = g * listed + k
+
+            def one_source(t, acc):
+                s = table[USERS + entry * SHARE + t]
                 w = weights[s, pl.ds(k, 1), :]
                 spread = [jnp.broadcast_to(w[:, 128 * l : 128 * l + 128], (8, 128)) for l in range(lanes)]
-                return tuple(
-                    sum((matrix[s, k, 8 * j : 8 * j + 8, 128 * l : 128 * l + 128] * spread[l] for l in range(lanes)), a)
-                    for j, a in enumerate(acc)
-                )
+                out = []
+                for j, a in enumerate(acc):
+                    parts = [
+                        matrix[s, k, 8 * j : 8 * j + 8, 128 * l : 128 * l + 128] * spread[l] for l in range(lanes)
+                    ]
+                    out.append(a + (sum(parts[: lanes // 2]) + sum(parts[lanes // 2 :])))
+                return tuple(out)
 
             acc = tuple(jnp.zeros((8, 128), jnp.float32) for _ in range(rows // 8))
-            for s in range(g * SHARE, (g + 1) * SHARE):
-                live = table[ALIVE + s * listed + k] > 0
-                acc = lax.cond(live, functools.partial(one_source, s), lambda acc: acc, acc)
+            acc = lax.fori_loop(0, table[USES + entry], one_source, acc)
             for j, a in enumerate(acc):
                 columns[g * listed + k, 8 * j : 8 * j + 8, :] = a
             return carry
@@ -368,8 +372,14 @@
             for place in range(listed):
                 live = jnp.where(listing[place] < count, 1, 0)
                 table[ORDER + s * listed + turn] = place
-                table[ALIVE + s * listed + place] = live
                 turn = turn + live
+        for place in range(listed):
+            entry = g * listed + place
+            used = jnp.int32(0)
+            for s in range(g * SHARE, (g + 1) * SHARE):
+                table[USERS + entry * SHARE + used] = s
+                used = used + jnp.where(listing[place] < counts[s], 1, 0)
+            table[USES + entry] = used
     for copy in copies:
         copy.wait()
 

time: 161 us -> 162 us (level)
  transfers between devices with their start and end apart: 47 -> 47, of which waited for: 30 -> 30; matrix products, arithmetic and copies ran while one was open for 0% -> 0% of each run, Pallas kernels for 13% -> 11%
where the time goes in v7:
time: 162 us
  starting transfers between devices  65.3 us (40%)
  Pallas kernels  42.8 us (26%)
  waiting for transfers between devices  29.6 us (18%)
  blocking collectives  17.2 us (11%)
  local copies, waits for them, and re-layouts  5.66 us (3%)
    ppermute x38, starting transfers between devices, send(): return lax.ppermute(x, 'row', row_perm(dz, dy, dc))  53.4 us
    ppermute x38, waiting for transfers between devices, send(): return lax.ppermute(x, 'row', row_perm(dz, dy, dc))  24 us
    pallas_call x3, Pallas kernels, score_stage(): pl.pallas_call(functools.partial(score_kernel, stage, listed), in_specs=[...  22.5 us
    all_to_all x1, blocking collectives, shards(): lax.all_to_all(sums.reshape(row_count, target_blocks, quarter), 'row', sp...  17.2 us
    ppermute x9, starting transfers between devices, from_columns(): lax.ppermute(x, 'col', [(i, (i + d) % 4) for i in range(4)])  11.9 us
    pallas_call x3, Pallas kernels, column_pass(): pl.pallas_call(functools.partial(column_kernel, final), in_specs=[smem] +...  10.2 us
    pallas_call x2, Pallas kernels, row_pass(): pl.pallas_call(row_kernel, in_specs=[smem] + [vmem] * 4, out_specs=vmem,...  6.04 us
    ppermute x9, waiting for transfers between devices, from_columns(): lax.ppermute(x, 'col', [(i, (i + d) % 4) for i in range(4)])  5.63 us
  transfers between devices with their start and end apart: 47, of which 30 were waited for; matrix products, arithmetic and copies ran while one was open for 0% of the time, Pallas kernels for 11%

profile of v7, /device:TPU:1, one launch (start us, length us, event | category | flops | bytes accessed | tf_op | source)
XLA Modules:
  0.0 162.5 jit_solution(934359210792356918)
XLA Ops:
  1.7 2.2 %collective-permute-start = (bf16[1,128,768]{2,1,0:T(8,128)(2,1)S(1)}, bf16[1,128,768]{2,1,0:T(8,128)(2,1)S(1)}, u32[]{:S(2)}, u32[]{:S(2)}) collective-permute-start(bf16[1,128,768]{2,1,0:T(8,128)(2,1)S(1)} %get-tuple-element.69), channel_id=1, source_target_pairs={{0,8},{4,12},{8,16},{12,20},{16,24},{20,28},{24,0},{28,4},{32,40},... | collective-permute-start | bytes 589832 | tf_op jit(solution)/shard_map/ppermute | solution.py:31
  10.7 2.6 %collective-permute-start.5 = (bf16[1,128,768]{2,1,0:T(8,128)(2,1)S(1)}, bf16[1,128,768]{2,1,0:T(8,128)(2,1)S(1)}, u32[]{:S(2)}, u32[]{:S(2)}) collective-permute-start(bf16[1,128,768]{2,1,0:T(8,128)(2,1)S(1)} %get-tuple-element.68), channel_id=1, source_target_pairs={{0,64},{4,68},{8,72},{12,76},{16,80},{20,84},{24,88},{28,92},{32,9... | collective-permute-start | bytes 589832 | tf_op jit(solution)/shard_map/ppermute | solution.py:31
  15.3 4.1 %tables.1 = (s32[344]{0:T(512)S(1)}, bf16[8,512,768]{2,1,0:T(8,128)(2,1)S(1)}) custom-call(s32[1]{0:T(128)} %bitcast.me, s32[8,12]{1,0:T(8,128)S(1)} %copy-done, s32[8]{0:T(128)S(1)} %copy-done.1, s32[64]{0:T(128)S(1)} %copy-done.2, bf16[8,512,768]{2,1,0:T(8,128)(2,1)} %source.1), custom_call_target="tpu_custom_call" | custom-call | tf_op jit(solution)/shard_map/tables/pallas_call | solution.py:391
  19.6 2.5 %collective-permute-start.11 = (bf16[4,128,768]{2,1,0:T(8,128)(2,1)S(1)}, bf16[4,128,768]{2,1,0:T(8,128)(2,1)S(1)}, u32[]{:S(2)}, u32[]{:S(2)}) collective-permute-start(bf16[4,128,768]{2,1,0:T(8,128)(2,1)S(1)} %pad_maximum_fusion.1.refs_1_), channel_id=1, source_target_pairs={{0,4},{4,0},{8,12},{12,8},{16,20},{20,16},{24,28},{28,24},{32,36},... | collective-permute-start | bytes 2359304 | tf_op jit(solution)/shard_map/ppermute | solution.py:31
  22.8 2.3 %collective-permute-start.9 = (bf16[4,128,768]{2,1,0:T(8,128)(2,1)S(1)}, bf16[4,128,768]{2,1,0:T(8,128)(2,1)S(1)}, u32[]{:S(2)}, u32[]{:S(2)}) collective-permute-start(bf16[4,128,768]{2,1,0:T(8,128)(2,1)S(1)} %pad_maximum_fusion.1.refs_1_), channel_id=1, source_target_pairs={{0,24},{4,28},{8,0},{12,4},{16,8},{20,12},{24,16},{28,20},{32,56},... | collective-permute-start | bytes 2359304 | tf_op jit(solution)/shard_map/ppermute | solution.py:31
  28.7 6.7 %scores.3 = (f32[8,12,128,512]{3,2,1,0:T(8,128)S(1)}, f32[8,16,512]{2,1,0:T(8,128)S(1)}, f32[8,16,512]{2,1,0:T(8,128)S(1)}) custom-call(s32[344]{0:T(512)S(1)} %get-tuple-element.36.table, bf16[8,512,768]{2,1,0:T(8,128)(2,1)S(1)} %get-tuple-element.37.source, bf16[4,128,768]{2,1,0:T(8,128)(2,1)} %copy-done.4, bf16[4,128,768]{2,1,0:T(8,128)(2,1)} %copy-done.3, ...), custom_call_target="tpu_custom_call" | custom-call | flops 2415919104 | bytes 6291456 | tf_op jit(solution)/shard_map/scores/pallas_call | solution.py:173
  35.5 6.9 %collective-permute-done.8.refs_2_ = bf16[4,128,768]{2,1,0:T(8,128)(2,1)S(1)} collective-permute-done((bf16[4,128,768]{2,1,0:T(8,128)(2,1)S(1)}, bf16[4,128,768]{2,1,0:T(8,128)(2,1)S(1)}, u32[]{:S(2)}, u32[]{:S(2)}) %collective-permute-start.8) | collective-permute-done | bytes 786464 | tf_op jit(solution)/shard_map/ppermute | solution.py:31
  48.3 2.6 %collective-permute-start.13 = (bf16[2,128,768]{2,1,0:T(8,128)(2,1)S(1)}, bf16[2,128,768]{2,1,0:T(8,128)(2,1)S(1)}, u32[]{:S(2)}, u32[]{:S(2)}) collective-permute-start(bf16[2,128,768]{2,1,0:T(8,128)(2,1)S(1)} %slice.42), channel_id=1, source_target_pairs={{0,96},{4,100},{8,104},{12,108},{16,112},{20,116},{24,120},{28,124... | collective-permute-start | bytes 1179656 | tf_op jit(solution)/shard_map/ppermute | solution.py:31
  54.8 7.2 %scores.4 = (f32[8,12,128,512]{3,2,1,0:T(8,128)S(1)}, f32[8,16,512]{2,1,0:T(8,128)S(1)}, f32[8,16,512]{2,1,0:T(8,128)S(1)}) custom-call(s32[344]{0:T(512)S(1)} %get-tuple-element.36.table, bf16[8,512,768]{2,1,0:T(8,128)(2,1)S(1)} %get-tuple-element.37.source, ...), custom_call_target="tpu_custom_call", output_to_operand_aliasing={{0}: (10, {}), {1}: (11, {}), {2}: (12, {})} | custom-call | flops 4831838208 | bytes 12582912 | tf_op jit(solution)/shard_map/scores/pallas_call | solution.py:173
  62.7 4.8 %collective-permute-start.20 = (bf16[2,128,768]{2,1,0:T(8,128)(2,1)S(1)}, bf16[2,128,768]{2,1,0:T(8,128)(2,1)S(1)}, u32[]{:S(2)}, u32[]{:S(2)}) collective-permute-start(bf16[2,128,768]{2,1,0:T(8,128)(2,1)S(1)} %collective-permute-done.12.refs_0_), channel_id=1, source_target_pairs={{0,4},{4,0},{8,12},{12,8},{16,20},{20,16},{24,28},{28,24},{32,36},... | collective-permute-start | bytes 1179656 | tf_op jit(solution)/shard_map/ppermute | solution.py:31
  71.3 8.6 %scores.5 = (f32[8,12,128,512]{3,2,1,0:T(8,128)S(1)}, f32[8,16,512]{2,1,0:T(8,128)S(1)}, f32[8,16,512]{2,1,0:T(8,128)S(1)}, f32[8,512]{1,0:T(8,128)S(1)}, f32[8,512]{1,0:T(8,128)S(1)}) custom-call(s32[344]{0:T(512)S(1)} %get-tuple-element.36.table, ...), custom_call_target="tpu_custom_call", output_to_operand_aliasing={{0}: (10, {}), {1}: (11, {}), {2}: (12, {})} | custom-call | flops 2415919104 | bytes 6291456 | tf_op jit(solution)/shard_map/scores/pallas_call | solution.py:173
  81.2 2.5 %collective-permute-start.25 = (f32[2,8,512]{2,1,0:T(8,128)S(1)}, f32[2,8,512]{2,1,0:T(8,128)S(1)}, u32[]{:S(2)}, u32[]{:S(2)}) collective-permute-start(f32[2,8,512]{2,1,0:T(8,128)S(1)} %pad_maximum_fusion.2), channel_id=1, source_target_pairs={{0,2},{1,3},{2,0},{3,1},{4,6},{5,7},{6,4},{7,5},{8,10},{9,11},{10,... | collective-permute-start | bytes 98312 | tf_op jit(solution)/shard_map/ppermute | solution.py:316
  86.4 3.4 %columns.3 = f32[64,128]{1,0:T(8,128)S(1)} custom-call(s32[344]{0:T(512)S(1)} %get-tuple-element.36.table, f32[8,512]{1,0:T(8,128)S(1)} %get-tuple-element.67.level, f32[8,512]{1,0:T(8,128)S(1)} %get-tuple-element.72.part, f32[8,512]{1,0:T(8,128)S(1)} %get-tuple-element.71.near, f32[8,512]{1,0:T(8,128)S(1)} %get-tuple-element.70.far, ...), custom_call_target="tpu_custom_call" | custom-call | tf_op jit(solution)/shard_map/columns/pallas_call | solution.py:251
  92.4 2.5 %collective-permute-start.30 = (f32[64,128]{1,0:T(8,128)S(1)}, f32[64,128]{1,0:T(8,128)S(1)}, u32[]{:S(2)}, u32[]{:S(2)}) collective-permute-start(f32[64,128]{1,0:T(8,128)S(1)} %add.48), channel_id=1, source_target_pairs={{0,24},{4,28},{8,0},{12,4},{16,8},{20,12},{24,16},{28,20},{32,56},... | collective-permute-start | bytes 98312 | tf_op jit(solution)/shard_map/ppermute | solution.py:31
  101.6 3.0 %rows.2.part = f32[8,512]{1,0:T(8,128)S(1)} custom-call(s32[344]{0:T(512)S(1)} %get-tuple-element.36.table, f32[8,512]{1,0:T(8,128)S(1)} %get-tuple-element.67.level, f32[64,128]{1,0:T(8,128)S(1)} %add_add_fusion.2.sums, f32[8,12,128,512]{3,2,1,0:T(8,128)S(1)} %get-tuple-element.62.matrix, f32[8,16,512]{2,1,0:T(8,128)S(1)} %get-tuple-element.63.peaks), custom_call_target="tpu_custom_call" | custom-call | tf_op jit(solution)/shard_map/rows/pallas_call | solution.py:300
  104.7 3.5 %collective-permute-start.35 = (f32[8,512]{1,0:T(8,128)S(1)}, f32[8,512]{1,0:T(8,128)S(1)}, u32[]{:S(2)}, u32[]{:S(2)}) collective-permute-start(f32[8,512]{1,0:T(8,128)S(1)} %rows.2.part), channel_id=1, source_target_pairs={{0,2},{1,3},{2,0},{3,1},{4,6},{5,7},{6,4},{7,5},{8,10},{9,11},{10,... | collective-permute-start | bytes 49160 | tf_op jit(solution)/shard_map/ppermute | solution.py:316
  110.9 3.4 %columns.4 = f32[64,128]{1,0:T(8,128)S(1)} custom-call(s32[344]{0:T(512)S(1)} %get-tuple-element.36.table, f32[8,512]{1,0:T(8,128)S(1)} %get-tuple-element.67.level, f32[8,512]{1,0:T(8,128)S(1)} %rows.2.part, f32[8,512]{1,0:T(8,128)S(1)} %collective-permute-done.34.near, f32[8,512]{1,0:T(8,128)S(1)} %collective-permute-done.35.far, ...), custom_call_target="tpu_custom_call" | custom-call | tf_op jit(solution)/shard_map/columns/pallas_call | solution.py:251
  114.2 5.4 %collective-permute-start.37 = (f32[64,128]{1,0:T(8,128)S(1)}, f32[64,128]{1,0:T(8,128)S(1)}, u32[]{:S(2)}, u32[]{:S(2)}) collective-permute-start(f32[64,128]{1,0:T(8,128)S(1)} %columns.4), channel_id=1, source_target_pairs={{0,4},{4,0},{8,12},{12,8},{16,20},{20,16},{24,28},{28,24},{32,36},... | collective-permute-start | bytes 98312 | tf_op jit(solution)/shard_map/ppermute | solution.py:31
  120.6 3.2 %collective-permute-start.39 = (f32[64,128]{1,0:T(8,128)S(1)}, f32[64,128]{1,0:T(8,128)S(1)}, u32[]{:S(2)}, u32[]{:S(2)}) collective-permute-start(f32[64,128]{1,0:T(8,128)S(1)} %add.55), channel_id=1, source_target_pairs={{0,16},{4,20},{8,24},{12,28},{16,0},{20,4},{24,8},{28,12},{32,48},... | collective-permute-start | bytes 98312 | tf_op jit(solution)/shard_map/ppermute | solution.py:31
  128.0 2.6 %collective-permute-start.42 = (f32[64,128]{1,0:T(8,128)S(1)}, f32[64,128]{1,0:T(8,128)S(1)}, u32[]{:S(2)}, u32[]{:S(2)}) collective-permute-start(f32[64,128]{1,0:T(8,128)S(1)} %add_add_fusion.1), channel_id=1, source_target_pairs={{0,64},{4,68},{8,72},{12,76},{16,80},{20,84},{24,88},{28,92},{32,9... | collective-permute-start | bytes 98312 | tf_op jit(solution)/shard_map/ppermute | solution.py:31
  133.4 3.0 %rows.3.part = f32[8,512]{1,0:T(8,128)S(1)} custom-call(s32[344]{0:T(512)S(1)} %get-tuple-element.36.table, f32[8,512]{1,0:T(8,128)S(1)} %get-tuple-element.67.level, f32[64,128]{1,0:T(8,128)S(1)} %add_add_fusion.sums, f32[8,12,128,512]{3,2,1,0:T(8,128)S(1)} %get-tuple-element.62.matrix, f32[8,16,512]{2,1,0:T(8,128)S(1)} %get-tuple-element.63.peaks), custom_call_target="tpu_custom_call" | custom-call | tf_op jit(solution)/shard_map/rows/pallas_call | solution.py:300
  136.5 2.1 %collective-permute-start.45 = (f32[8,512]{1,0:T(8,128)S(1)}, f32[8,512]{1,0:T(8,128)S(1)}, u32[]{:S(2)}, u32[]{:S(2)}) collective-permute-start(f32[8,512]{1,0:T(8,128)S(1)} %rows.3.part), channel_id=1, source_target_pairs={{0,2},{1,3},{2,0},{3,1},{4,6},{5,7},{6,4},{7,5},{8,10},{9,11},{10,... | collective-permute-start | bytes 49160 | tf_op jit(solution)/shard_map/ppermute | solution.py:316
  141.2 3.5 %columns.5 = (f32[64,128]{1,0:T(8,128)S(1)}, f32[8,512]{1,0:T(8,128)}) custom-call(s32[344]{0:T(512)S(1)} %get-tuple-element.36.table, f32[8,512]{1,0:T(8,128)S(1)} %get-tuple-element.67.level, f32[8,512]{1,0:T(8,128)S(1)} %rows.3.part, f32[8,512]{1,0:T(8,128)S(1)} %collective-permute-done.44.near, f32[8,512]{1,0:T(8,128)S(1)} %collective-permute-done.45.far, ...), custom_call_target="tpu_custom_call" | custom-call | tf_op jit(solution)/shard_map/columns/pallas_call | solution.py:251
  144.7 17.2 %all_to_all.5 = f32[32,2,128]{2,1,0:T(2,128)S(1)} all-to-all(f32[32,2,128]{2,1,0:T(2,128)S(1)} %bitcast.39), channel_id=1, replica_groups=mesh['row'=32,'col'=4] {'row'}, dimensions={0} | all-to-all | bytes 65536 | tf_op jit(solution)/shard_map/all_to_all | solution.py:454
  (144 shorter events, 55.8 us)
Async XLA Ops:
  1.7 9.0 %collective-permute-start = (bf16[1,128,768]{2,1,0:T(8,128)(2,1)S(1)}, bf16[1,128,768]{2,1,0:T(8,128)(2,1)S(1)}, u32[]{:S(2)}, u32[]{:S(2)}) collective-permute-start(bf16[1,128,768]{2,1,0:T(8,128)(2,1)S(1)} %get-tuple-element.69), channel_id=1, source_target_pairs={{0,8},{4,12},{8,16},{12,20},{16,24},{20,28},{24,0},{28,4},{32,40},... | collective-permute-start | bytes 589832 | tf_op jit(solution)/shard_map/ppermute | solution.py:31
  3.9 15.5 %collective-permute-start.1 = (bf16[1,128,768]{2,1,0:T(8,128)(2,1)S(1)}, bf16[1,128,768]{2,1,0:T(8,128)(2,1)S(1)}, u32[]{:S(2)}, u32[]{:S(2)}) collective-permute-start(bf16[1,128,768]{2,1,0:T(8,128)(2,1)S(1)} %get-tuple-element.69), channel_id=1, source_target_pairs={{0,24},{4,28},{8,0},{12,4},{16,8},{20,12},{24,16},{28,20},{32,56},... | collective-permute-start | bytes 589832 | tf_op jit(solution)/shard_map/ppermute | solution.py:31
  5.4 14.0 %collective-permute-start.2 = (bf16[1,128,768]{2,1,0:T(8,128)(2,1)S(1)}, bf16[1,128,768]{2,1,0:T(8,128)(2,1)S(1)}, u32[]{:S(2)}, u32[]{:S(2)}) collective-permute-start(bf16[1,128,768]{2,1,0:T(8,128)(2,1)S(1)} %get-tuple-element.69), channel_id=1, source_target_pairs={{0,16},{4,20},{8,24},{12,28},{16,0},{20,4},{24,8},{28,12},{32,48},... | collective-permute-start | bytes 589832 | tf_op jit(solution)/shard_map/ppermute | solution.py:31
  7.0 12.4 %collective-permute-start.3 = (bf16[1,128,768]{2,1,0:T(8,128)(2,1)S(1)}, bf16[1,128,768]{2,1,0:T(8,128)(2,1)S(1)}, u32[]{:S(2)}, u32[]{:S(2)}) collective-permute-start(bf16[1,128,768]{2,1,0:T(8,128)(2,1)S(1)} %get-tuple-element.68), channel_id=1, source_target_pairs={{0,32},{4,36},{8,40},{12,44},{16,48},{20,52},{24,56},{28,60},{32,6... | collective-permute-start | bytes 589832 | tf_op jit(solution)/shard_map/ppermute | solution.py:31
  8.6 10.8 %collective-permute-start.4 = (bf16[1,128,768]{2,1,0:T(8,128)(2,1)S(1)}, bf16[1,128,768]{2,1,0:T(8,128)(2,1)S(1)}, u32[]{:S(2)}, u32[]{:S(2)}) collective-permute-start(bf16[1,128,768]{2,1,0:T(8,128)(2,1)S(1)} %get-tuple-element.68), channel_id=1, source_target_pairs={{0,96},{4,100},{8,104},{12,108},{16,112},{20,116},{24,120},{28,124... | collective-permute-start | bytes 589832 | tf_op jit(solution)/shard_map/ppermute | solution.py:31
  10.7 8.8 %collective-permute-start.5 = (bf16[1,128,768]{2,1,0:T(8,128)(2,1)S(1)}, bf16[1,128,768]{2,1,0:T(8,128)(2,1)S(1)}, u32[]{:S(2)}, u32[]{:S(2)}) collective-permute-start(bf16[1,128,768]{2,1,0:T(8,128)(2,1)S(1)} %get-tuple-element.68), channel_id=1, source_target_pairs={{0,64},{4,68},{8,72},{12,76},{16,80},{20,84},{24,88},{28,92},{32,9... | collective-permute-start | bytes 589832 | tf_op jit(solution)/shard_map/ppermute | solution.py:31
  19.6 6.3 %collective-permute-start.11 = (bf16[4,128,768]{2,1,0:T(8,128)(2,1)S(1)}, bf16[4,128,768]{2,1,0:T(8,128)(2,1)S(1)}, u32[]{:S(2)}, u32[]{:S(2)}) collective-permute-start(bf16[4,128,768]{2,1,0:T(8,128)(2,1)S(1)} %pad_maximum_fusion.1.refs_1_), channel_id=1, source_target_pairs={{0,4},{4,0},{8,12},{12,8},{16,20},{20,16},{24,28},{28,24},{32,36},... | collective-permute-start | bytes 2359304 | tf_op jit(solution)/shard_map/ppermute | solution.py:31
  22.3 5.5 %collective-permute-start.10 = (bf16[4,128,768]{2,1,0:T(8,128)(2,1)S(1)}, bf16[4,128,768]{2,1,0:T(8,128)(2,1)S(1)}, u32[]{:S(2)}, u32[]{:S(2)}) collective-permute-start(bf16[4,128,768]{2,1,0:T(8,128)(2,1)S(1)} %pad_maximum_fusion.refs_0_), channel_id=1, source_target_pairs={{0,4},{4,0},{8,12},{12,8},{16,20},{20,16},{24,28},{28,24},{32,36},... | collective-permute-start | bytes 2359304 | tf_op jit(solution)/shard_map/ppermute | solution.py:31
  22.4 20.0 %collective-permute-start.8 = (bf16[4,128,768]{2,1,0:T(8,128)(2,1)S(1)}, bf16[4,128,768]{2,1,0:T(8,128)(2,1)S(1)}, u32[]{:S(2)}, u32[]{:S(2)}) collective-permute-start(bf16[4,128,768]{2,1,0:T(8,128)(2,1)S(1)} %pad_maximum_fusion.1.refs_1_), channel_id=1, source_target_pairs={{0,8},{4,12},{8,16},{12,20},{16,24},{20,28},{24,0},{28,4},{32,40},... | collective-permute-start | bytes 2359304 | tf_op jit(solution)/shard_map/ppermute | solution.py:31
  22.8 21.6 %collective-permute-start.9 = (bf16[4,128,768]{2,1,0:T(8,128)(2,1)S(1)}, bf16[4,128,768]{2,1,0:T(8,128)(2,1)S(1)}, u32[]{:S(2)}, u32[]{:S(2)}) collective-permute-start(bf16[4,128,768]{2,1,0:T(8,128)(2,1)S(1)} %pad_maximum_fusion.1.refs_1_), channel_id=1, source_target_pairs={{0,24},{4,28},{8,0},{12,4},{16,8},{20,12},{24,16},{28,20},{32,56},... | collective-permute-start | bytes 2359304 | tf_op jit(solution)/shard_map/ppermute | solution.py:31
  25.1 19.3 %collective-permute-start.6 = (bf16[4,128,768]{2,1,0:T(8,128)(2,1)S(1)}, bf16[4,128,768]{2,1,0:T(8,128)(2,1)S(1)}, u32[]{:S(2)}, u32[]{:S(2)}) collective-permute-start(bf16[4,128,768]{2,1,0:T(8,128)(2,1)S(1)} %pad_maximum_fusion.refs_0_), channel_id=1, source_target_pairs={{0,32},{4,36},{8,40},{12,44},{16,48},{20,52},{24,56},{28,60},{32,6... | collective-permute-start | bytes 2359304 | tf_op jit(solution)/shard_map/ppermute | solution.py:31
  26.0 18.4 %collective-permute-start.7 = (bf16[4,128,768]{2,1,0:T(8,128)(2,1)S(1)}, bf16[4,128,768]{2,1,0:T(8,128)(2,1)S(1)}, u32[]{:S(2)}, u32[]{:S(2)}) collective-permute-start(bf16[4,128,768]{2,1,0:T(8,128)(2,1)S(1)} %pad_maximum_fusion.refs_0_), channel_id=1, source_target_pairs={{0,96},{4,100},{8,104},{12,108},{16,112},{20,116},{24,120},{28,124... | collective-permute-start | bytes 2359304 | tf_op jit(solution)/shard_map/ppermute | solution.py:31
  46.4 4.5 %collective-permute-start.17 = (bf16[4,128,768]{2,1,0:T(8,128)(2,1)S(1)}, bf16[4,128,768]{2,1,0:T(8,128)(2,1)S(1)}, u32[]{:S(2)}, u32[]{:S(2)}) collective-permute-start(bf16[4,128,768]{2,1,0:T(8,128)(2,1)S(1)} %collective-permute-done.7.refs_1_), channel_id=1, source_target_pairs={{0,4},{4,0},{8,12},{12,8},{16,20},{20,16},{24,28},{28,24},{32,36},... | collective-permute-start | bytes 2359304 | tf_op jit(solution)/shard_map/ppermute | solution.py:31
  46.5 6.5 %collective-permute-start.18 = (bf16[4,128,768]{2,1,0:T(8,128)(2,1)S(1)}, bf16[4,128,768]{2,1,0:T(8,128)(2,1)S(1)}, u32[]{:S(2)}, u32[]{:S(2)}) collective-permute-start(bf16[4,128,768]{2,1,0:T(8,128)(2,1)S(1)} %collective-permute-done.8.refs_2_), channel_id=1, source_target_pairs={{0,4},{4,0},{8,12},{12,8},{16,20},{20,16},{24,28},{28,24},{32,36},... | collective-permute-start | bytes 2359304 | tf_op jit(solution)/shard_map/ppermute | solution.py:31
  46.9 7.1 %collective-permute-start.19 = (bf16[4,128,768]{2,1,0:T(8,128)(2,1)S(1)}, bf16[4,128,768]{2,1,0:T(8,128)(2,1)S(1)}, u32[]{:S(2)}, u32[]{:S(2)}) collective-permute-start(bf16[4,128,768]{2,1,0:T(8,128)(2,1)S(1)} %collective-permute-done.9.refs_3_), channel_id=1, source_target_pairs={{0,4},{4,0},{8,12},{12,8},{16,20},{20,16},{24,28},{28,24},{32,36},... | collective-permute-start | bytes 2359304 | tf_op jit(solution)/shard_map/ppermute | solution.py:31
  47.1 14.9 %collective-permute-start.12 = (bf16[2,128,768]{2,1,0:T(8,128)(2,1)S(1)}, bf16[2,128,768]{2,1,0:T(8,128)(2,1)S(1)}, u32[]{:S(2)}, u32[]{:S(2)}) collective-permute-start(bf16[2,128,768]{2,1,0:T(8,128)(2,1)S(1)} %slice.41), channel_id=1, source_target_pairs={{0,32},{4,36},{8,40},{12,44},{16,48},{20,52},{24,56},{28,60},{32,6... | collective-permute-start | bytes 1179656 | tf_op jit(solution)/shard_map/ppermute | solution.py:31
  48.3 13.7 %collective-permute-start.13 = (bf16[2,128,768]{2,1,0:T(8,128)(2,1)S(1)}, bf16[2,128,768]{2,1,0:T(8,128)(2,1)S(1)}, u32[]{:S(2)}, u32[]{:S(2)}) collective-permute-start(bf16[2,128,768]{2,1,0:T(8,128)(2,1)S(1)} %slice.42), channel_id=1, source_target_pairs={{0,96},{4,100},{8,104},{12,108},{16,112},{20,116},{24,120},{28,124... | collective-permute-start | bytes 1179656 | tf_op jit(solution)/shard_map/ppermute | solution.py:31
  50.9 11.4 %collective-permute-start.14 = (bf16[2,128,768]{2,1,0:T(8,128)(2,1)S(1)}, bf16[2,128,768]{2,1,0:T(8,128)(2,1)S(1)}, u32[]{:S(2)}, u32[]{:S(2)}) collective-permute-start(bf16[2,128,768]{2,1,0:T(8,128)(2,1)S(1)} %slice.43), channel_id=1, source_target_pairs={{0,8},{4,12},{8,16},{12,20},{16,24},{20,28},{24,0},{28,4},{32,40},... | collective-permute-start | bytes 1179656 | tf_op jit(solution)/shard_map/ppermute | solution.py:31
  53.0 9.7 %collective-permute-start.15 = (bf16[2,128,768]{2,1,0:T(8,128)(2,1)S(1)}, bf16[2,128,768]{2,1,0:T(8,128)(2,1)S(1)}, u32[]{:S(2)}, u32[]{:S(2)}) collective-permute-start(bf16[2,128,768]{2,1,0:T(8,128)(2,1)S(1)} %slice.44), channel_id=1, source_target_pairs={{0,24},{4,28},{8,0},{12,4},{16,8},{20,12},{24,16},{28,20},{32,56},... | collective-permute-start | bytes 1179656 | tf_op jit(solution)/shard_map/ppermute | solution.py:31
  62.7 6.2 %collective-permute-start.20 = (bf16[2,128,768]{2,1,0:T(8,128)(2,1)S(1)}, bf16[2,128,768]{2,1,0:T(8,128)(2,1)S(1)}, u32[]{:S(2)}, u32[]{:S(2)}) collective-permute-start(bf16[2,128,768]{2,1,0:T(8,128)(2,1)S(1)} %collective-permute-done.12.refs_0_), channel_id=1, source_target_pairs={{0,4},{4,0},{8,12},{12,8},{16,20},{20,16},{24,28},{28,24},{32,36},... | collective-permute-start | bytes 1179656 | tf_op jit(solution)/shard_map/ppermute | solution.py:31
  79.9 4.9 %collective-permute-start.24 = (f32[2,8,512]{2,1,0:T(8,128)S(1)}, f32[2,8,512]{2,1,0:T(8,128)S(1)}, u32[]{:S(2)}, u32[]{:S(2)}) collective-permute-start(f32[2,8,512]{2,1,0:T(8,128)S(1)} %pad_maximum_fusion.2), channel_id=1, source_target_pairs={{0,1},{1,2},{2,3},{3,0},{4,5},{5,6},{6,7},{7,4},{8,9},{9,10},{10,1... | collective-permute-start | bytes 98312 | tf_op jit(solution)/shard_map/ppermute | solution.py:316
  104.7 4.8 %collective-permute-start.35 = (f32[8,512]{1,0:T(8,128)S(1)}, f32[8,512]{1,0:T(8,128)S(1)}, u32[]{:S(2)}, u32[]{:S(2)}) collective-permute-start(f32[8,512]{1,0:T(8,128)S(1)} %rows.2.part), channel_id=1, source_target_pairs={{0,2},{1,3},{2,0},{3,1},{4,6},{5,7},{6,4},{7,5},{8,10},{9,11},{10,... | collective-permute-start | bytes 49160 | tf_op jit(solution)/shard_map/ppermute | solution.py:316
  114.2 6.3 %collective-permute-start.37 = (f32[64,128]{1,0:T(8,128)S(1)}, f32[64,128]{1,0:T(8,128)S(1)}, u32[]{:S(2)}, u32[]{:S(2)}) collective-permute-start(f32[64,128]{1,0:T(8,128)S(1)} %columns.4), channel_id=1, source_target_pairs={{0,4},{4,0},{8,12},{12,8},{16,20},{20,16},{24,28},{28,24},{32,36},... | collective-permute-start | bytes 98312 | tf_op jit(solution)/shard_map/ppermute | solution.py:31
  120.6 4.9 %collective-permute-start.39 = (f32[64,128]{1,0:T(8,128)S(1)}, f32[64,128]{1,0:T(8,128)S(1)}, u32[]{:S(2)}, u32[]{:S(2)}) collective-permute-start(f32[64,128]{1,0:T(8,128)S(1)} %add.55), channel_id=1, source_target_pairs={{0,16},{4,20},{8,24},{12,28},{16,0},{20,4},{24,8},{28,12},{32,48},... | collective-permute-start | bytes 98312 | tf_op jit(solution)/shard_map/ppermute | solution.py:31
  (46 other events, 185.3 us)

commit v8 on v6

--- a/solution.py
+++ b/solution.py
@@ -211,7 +211,7 @@
                 w = weights[s, pl.ds(k, 1), :]
                 spread = [jnp.broadcast_to(w[:, 128 * l : 128 * l + 128], (8, 128)) for l in range(lanes)]
                 return tuple(
-                    sum((matrix[s, k, 8 * j : 8 * j + 8, 128 * l : 128 * l + 128] * spread[l] for l in range(lanes)), a)
+                    a + sum(matrix[s, k, 8 * j : 8 * j + 8, 128 * l : 128 * l + 128] * spread[l] for l in range(lanes))
                     for j, a in enumerate(acc)
                 )
 

time: 161 us -> 162 us (level)
  Pallas kernels: 41.2 us -> 44.9 us
  starting transfers between devices: 66.2 us -> 63.9 us
    pallas_call x3, Pallas kernels: 21.3 us -> 23.7 us  [score_stage(): pl.pallas_call(functools.partial(score_kernel, stage, listed), in_specs=[...]
    ppermute x38, starting transfers between devices: 54.4 us -> 52 us  [send(): return lax.ppermute(x, 'row', row_perm(dz, dy, dc))]
  transfers between devices with their start and end apart: 47 -> 47, of which waited for: 30 -> 29; matrix products, arithmetic and copies ran while one was open for 0% -> 0% of each run, Pallas kernels for 13% -> 13%
where the time goes in v8:
time: 162 us
  starting transfers between devices  63.9 us (39%)
  Pallas kernels  44.9 us (28%)
  waiting for transfers between devices  29.1 us (18%)
  blocking collectives  16.4 us (10%)
  local copies, waits for them, and re-layouts  5.66 us (3%)
    ppermute x38, starting transfers between devices, send(): return lax.ppermute(x, 'row', row_perm(dz, dy, dc))  52 us
    pallas_call x3, Pallas kernels, score_stage(): pl.pallas_call(functools.partial(score_kernel, stage, listed), in_specs=[...  23.7 us
    ppermute x38, waiting for transfers between devices, send(): return lax.ppermute(x, 'row', row_perm(dz, dy, dc))  23.5 us
    all_to_all x1, blocking collectives, shards(): lax.all_to_all(sums.reshape(row_count, target_blocks, quarter), 'row', sp...  16.4 us
    ppermute x9, starting transfers between devices, from_columns(): lax.ppermute(x, 'col', [(i, (i + d) % 4) for i in range(4)])  11.9 us
    pallas_call x3, Pallas kernels, column_pass(): pl.pallas_call(functools.partial(column_kernel, final), in_specs=[smem] +...  10.6 us
    pallas_call x2, Pallas kernels, row_pass(): pl.pallas_call(row_kernel, in_specs=[smem] + [vmem] * 4, out_specs=vmem,...  6.52 us
    ppermute x9, waiting for transfers between devices, from_columns(): lax.ppermute(x, 'col', [(i, (i + d) % 4) for i in range(4)])  5.62 us
  transfers between devices with their start and end apart: 47, of which 29 were waited for; matrix products, arithmetic and copies ran while one was open for 0% of the time, Pallas kernels for 13%

profile of v8, /device:TPU:1, one launch (start us, length us, event | category | flops | bytes accessed | tf_op | source)
XLA Modules:
  0.0 162.0 jit_solution(16879716026093136320)
XLA Ops:
  1.7 2.2 %collective-permute-start = (bf16[1,128,768]{2,1,0:T(8,128)(2,1)S(1)}, bf16[1,128,768]{2,1,0:T(8,128)(2,1)S(1)}, u32[]{:S(2)}, u32[]{:S(2)}) collective-permute-start(bf16[1,128,768]{2,1,0:T(8,128)(2,1)S(1)} %get-tuple-element.69), channel_id=1, source_target_pairs={{0,8},{4,12},{8,16},{12,20},{16,24},{20,28},{24,0},{28,4},{32,40},... | collective-permute-start | bytes 589832 | tf_op jit(solution)/shard_map/ppermute | solution.py:31
  8.6 2.1 %collective-permute-start.4 = (bf16[1,128,768]{2,1,0:T(8,128)(2,1)S(1)}, bf16[1,128,768]{2,1,0:T(8,128)(2,1)S(1)}, u32[]{:S(2)}, u32[]{:S(2)}) collective-permute-start(bf16[1,128,768]{2,1,0:T(8,128)(2,1)S(1)} %get-tuple-element.68), channel_id=1, source_target_pairs={{0,96},{4,100},{8,104},{12,108},{16,112},{20,116},{24,120},{28,124... | collective-permute-start | bytes 589832 | tf_op jit(solution)/shard_map/ppermute | solution.py:31
  10.7 2.6 %collective-permute-start.5 = (bf16[1,128,768]{2,1,0:T(8,128)(2,1)S(1)}, bf16[1,128,768]{2,1,0:T(8,128)(2,1)S(1)}, u32[]{:S(2)}, u32[]{:S(2)}) collective-permute-start(bf16[1,128,768]{2,1,0:T(8,128)(2,1)S(1)} %get-tuple-element.68), channel_id=1, source_target_pairs={{0,64},{4,68},{8,72},{12,76},{16,80},{20,84},{24,88},{28,92},{32,9... | collective-permute-start | bytes 589832 | tf_op jit(solution)/shard_map/ppermute | solution.py:31
  15.3 4.1 %tables.1 = (s32[320]{0:T(512)S(1)}, bf16[8,512,768]{2,1,0:T(8,128)(2,1)S(1)}) custom-call(s32[1]{0:T(128)} %bitcast.me, s32[8,12]{1,0:T(8,128)S(1)} %copy-done, s32[8]{0:T(128)S(1)} %copy-done.1, s32[64]{0:T(128)S(1)} %copy-done.2, bf16[8,512,768]{2,1,0:T(8,128)(2,1)} %source.1), custom_call_target="tpu_custom_call" | custom-call | tf_op jit(solution)/shard_map/tables/pallas_call | solution.py:381
  19.6 2.5 %collective-permute-start.11 = (bf16[4,128,768]{2,1,0:T(8,128)(2,1)S(1)}, bf16[4,128,768]{2,1,0:T(8,128)(2,1)S(1)}, u32[]{:S(2)}, u32[]{:S(2)}) collective-permute-start(bf16[4,128,768]{2,1,0:T(8,128)(2,1)S(1)} %pad_maximum_fusion.1.refs_1_), channel_id=1, source_target_pairs={{0,4},{4,0},{8,12},{12,8},{16,20},{20,16},{24,28},{28,24},{32,36},... | collective-permute-start | bytes 2359304 | tf_op jit(solution)/shard_map/ppermute | solution.py:31
  22.8 2.3 %collective-permute-start.9 = (bf16[4,128,768]{2,1,0:T(8,128)(2,1)S(1)}, bf16[4,128,768]{2,1,0:T(8,128)(2,1)S(1)}, u32[]{:S(2)}, u32[]{:S(2)}) collective-permute-start(bf16[4,128,768]{2,1,0:T(8,128)(2,1)S(1)} %pad_maximum_fusion.1.refs_1_), channel_id=1, source_target_pairs={{0,24},{4,28},{8,0},{12,4},{16,8},{20,12},{24,16},{28,20},{32,56},... | collective-permute-start | bytes 2359304 | tf_op jit(solution)/shard_map/ppermute | solution.py:31
  28.7 6.0 %scores.3 = (f32[8,12,128,512]{3,2,1,0:T(8,128)S(1)}, f32[8,16,512]{2,1,0:T(8,128)S(1)}, f32[8,16,512]{2,1,0:T(8,128)S(1)}) custom-call(s32[320]{0:T(512)S(1)} %get-tuple-element.36.table, bf16[8,512,768]{2,1,0:T(8,128)(2,1)S(1)} %get-tuple-element.37.source, bf16[4,128,768]{2,1,0:T(8,128)(2,1)} %copy-done.4, bf16[4,128,768]{2,1,0:T(8,128)(2,1)} %copy-done.3, ...), custom_call_target="tpu_custom_call" | custom-call | flops 2415919104 | bytes 6291456 | tf_op jit(solution)/shard_map/scores/pallas_call | solution.py:173
  34.8 7.6 %collective-permute-done.8.refs_2_ = bf16[4,128,768]{2,1,0:T(8,128)(2,1)S(1)} collective-permute-done((bf16[4,128,768]{2,1,0:T(8,128)(2,1)S(1)}, bf16[4,128,768]{2,1,0:T(8,128)(2,1)S(1)}, u32[]{:S(2)}, u32[]{:S(2)}) %collective-permute-start.8) | collective-permute-done | bytes 786464 | tf_op jit(solution)/shard_map/ppermute | solution.py:31
  48.3 2.6 %collective-permute-start.13 = (bf16[2,128,768]{2,1,0:T(8,128)(2,1)S(1)}, bf16[2,128,768]{2,1,0:T(8,128)(2,1)S(1)}, u32[]{:S(2)}, u32[]{:S(2)}) collective-permute-start(bf16[2,128,768]{2,1,0:T(8,128)(2,1)S(1)} %slice.42), channel_id=1, source_target_pairs={{0,96},{4,100},{8,104},{12,108},{16,112},{20,116},{24,120},{28,124... | collective-permute-start | bytes 1179656 | tf_op jit(solution)/shard_map/ppermute | solution.py:31
  50.9 2.1 %collective-permute-start.14 = (bf16[2,128,768]{2,1,0:T(8,128)(2,1)S(1)}, bf16[2,128,768]{2,1,0:T(8,128)(2,1)S(1)}, u32[]{:S(2)}, u32[]{:S(2)}) collective-permute-start(bf16[2,128,768]{2,1,0:T(8,128)(2,1)S(1)} %slice.43), channel_id=1, source_target_pairs={{0,8},{4,12},{8,16},{12,20},{16,24},{20,28},{24,0},{28,4},{32,40},... | collective-permute-start | bytes 1179656 | tf_op jit(solution)/shard_map/ppermute | solution.py:31
  54.8 10.4 %scores.4 = (f32[8,12,128,512]{3,2,1,0:T(8,128)S(1)}, f32[8,16,512]{2,1,0:T(8,128)S(1)}, f32[8,16,512]{2,1,0:T(8,128)S(1)}) custom-call(s32[320]{0:T(512)S(1)} %get-tuple-element.36.table, bf16[8,512,768]{2,1,0:T(8,128)(2,1)S(1)} %get-tuple-element.37.source, ...), custom_call_target="tpu_custom_call", output_to_operand_aliasing={{0}: (10, {}), {1}: (11, {}), {2}: (12, {})} | custom-call | flops 4831838208 | bytes 12582912 | tf_op jit(solution)/shard_map/scores/pallas_call | solution.py:173
  69.5 7.3 %scores.5 = (f32[8,12,128,512]{3,2,1,0:T(8,128)S(1)}, f32[8,16,512]{2,1,0:T(8,128)S(1)}, f32[8,16,512]{2,1,0:T(8,128)S(1)}, f32[8,512]{1,0:T(8,128)S(1)}, f32[8,512]{1,0:T(8,128)S(1)}) custom-call(s32[320]{0:T(512)S(1)} %get-tuple-element.36.table, ...), custom_call_target="tpu_custom_call", output_to_operand_aliasing={{0}: (10, {}), {1}: (11, {}), {2}: (12, {})} | custom-call | flops 2415919104 | bytes 6291456 | tf_op jit(solution)/shard_map/scores/pallas_call | solution.py:173
  78.2 2.5 %collective-permute-start.25 = (f32[2,8,512]{2,1,0:T(8,128)S(1)}, f32[2,8,512]{2,1,0:T(8,128)S(1)}, u32[]{:S(2)}, u32[]{:S(2)}) collective-permute-start(f32[2,8,512]{2,1,0:T(8,128)S(1)} %pad_maximum_fusion.2), channel_id=1, source_target_pairs={{0,2},{1,3},{2,0},{3,1},{4,6},{5,7},{6,4},{7,5},{8,10},{9,11},{10,... | collective-permute-start | bytes 98312 | tf_op jit(solution)/shard_map/ppermute | solution.py:312
  83.4 3.5 %columns.3 = f32[64,128]{1,0:T(8,128)S(1)} custom-call(s32[320]{0:T(512)S(1)} %get-tuple-element.36.table, f32[8,512]{1,0:T(8,128)S(1)} %get-tuple-element.67.level, f32[8,512]{1,0:T(8,128)S(1)} %get-tuple-element.72.part, f32[8,512]{1,0:T(8,128)S(1)} %get-tuple-element.71.near, f32[8,512]{1,0:T(8,128)S(1)} %get-tuple-element.70.far, ...), custom_call_target="tpu_custom_call" | custom-call | tf_op jit(solution)/shard_map/columns/pallas_call | solution.py:247
  86.9 3.4 %collective-permute-start.27 = (f32[64,128]{1,0:T(8,128)S(1)}, f32[64,128]{1,0:T(8,128)S(1)}, u32[]{:S(2)}, u32[]{:S(2)}) collective-permute-start(f32[64,128]{1,0:T(8,128)S(1)} %columns.3), channel_id=1, source_target_pairs={{0,4},{4,0},{8,12},{12,8},{16,20},{20,16},{24,28},{28,24},{32,36},... | collective-permute-start | bytes 98312 | tf_op jit(solution)/shard_map/ppermute | solution.py:31
  101.4 3.3 %rows.2.part = f32[8,512]{1,0:T(8,128)S(1)} custom-call(s32[320]{0:T(512)S(1)} %get-tuple-element.36.table, f32[8,512]{1,0:T(8,128)S(1)} %get-tuple-element.67.level, f32[64,128]{1,0:T(8,128)S(1)} %add_add_fusion.2.sums, f32[8,12,128,512]{3,2,1,0:T(8,128)S(1)} %get-tuple-element.62.matrix, f32[8,16,512]{2,1,0:T(8,128)S(1)} %get-tuple-element.63.peaks), custom_call_target="tpu_custom_call" | custom-call | tf_op jit(solution)/shard_map/rows/pallas_call | solution.py:296
  104.7 3.5 %collective-permute-start.35 = (f32[8,512]{1,0:T(8,128)S(1)}, f32[8,512]{1,0:T(8,128)S(1)}, u32[]{:S(2)}, u32[]{:S(2)}) collective-permute-start(f32[8,512]{1,0:T(8,128)S(1)} %rows.2.part), channel_id=1, source_target_pairs={{0,2},{1,3},{2,0},{3,1},{4,6},{5,7},{6,4},{7,5},{8,10},{9,11},{10,... | collective-permute-start | bytes 49160 | tf_op jit(solution)/shard_map/ppermute | solution.py:312
  110.8 3.5 %columns.4 = f32[64,128]{1,0:T(8,128)S(1)} custom-call(s32[320]{0:T(512)S(1)} %get-tuple-element.36.table, f32[8,512]{1,0:T(8,128)S(1)} %get-tuple-element.67.level, f32[8,512]{1,0:T(8,128)S(1)} %rows.2.part, f32[8,512]{1,0:T(8,128)S(1)} %collective-permute-done.34.near, f32[8,512]{1,0:T(8,128)S(1)} %collective-permute-done.35.far, ...), custom_call_target="tpu_custom_call" | custom-call | tf_op jit(solution)/shard_map/columns/pallas_call | solution.py:247
  114.3 5.0 %collective-permute-start.37 = (f32[64,128]{1,0:T(8,128)S(1)}, f32[64,128]{1,0:T(8,128)S(1)}, u32[]{:S(2)}, u32[]{:S(2)}) collective-permute-start(f32[64,128]{1,0:T(8,128)S(1)} %columns.4), channel_id=1, source_target_pairs={{0,4},{4,0},{8,12},{12,8},{16,20},{20,16},{24,28},{28,24},{32,36},... | collective-permute-start | bytes 98312 | tf_op jit(solution)/shard_map/ppermute | solution.py:31
  121.0 3.2 %collective-permute-start.39 = (f32[64,128]{1,0:T(8,128)S(1)}, f32[64,128]{1,0:T(8,128)S(1)}, u32[]{:S(2)}, u32[]{:S(2)}) collective-permute-start(f32[64,128]{1,0:T(8,128)S(1)} %add.55), channel_id=1, source_target_pairs={{0,16},{4,20},{8,24},{12,28},{16,0},{20,4},{24,8},{28,12},{32,48},... | collective-permute-start | bytes 98312 | tf_op jit(solution)/shard_map/ppermute | solution.py:31
  133.3 3.3 %rows.3.part = f32[8,512]{1,0:T(8,128)S(1)} custom-call(s32[320]{0:T(512)S(1)} %get-tuple-element.36.table, f32[8,512]{1,0:T(8,128)S(1)} %get-tuple-element.67.level, f32[64,128]{1,0:T(8,128)S(1)} %add_add_fusion.sums, f32[8,12,128,512]{3,2,1,0:T(8,128)S(1)} %get-tuple-element.62.matrix, f32[8,16,512]{2,1,0:T(8,128)S(1)} %get-tuple-element.63.peaks), custom_call_target="tpu_custom_call" | custom-call | tf_op jit(solution)/shard_map/rows/pallas_call | solution.py:296
  136.6 2.1 %collective-permute-start.45 = (f32[8,512]{1,0:T(8,128)S(1)}, f32[8,512]{1,0:T(8,128)S(1)}, u32[]{:S(2)}, u32[]{:S(2)}) collective-permute-start(f32[8,512]{1,0:T(8,128)S(1)} %rows.3.part), channel_id=1, source_target_pairs={{0,2},{1,3},{2,0},{3,1},{4,6},{5,7},{6,4},{7,5},{8,10},{9,11},{10,... | collective-permute-start | bytes 49160 | tf_op jit(solution)/shard_map/ppermute | solution.py:312
  141.3 3.6 %columns.5 = (f32[64,128]{1,0:T(8,128)S(1)}, f32[8,512]{1,0:T(8,128)}) custom-call(s32[320]{0:T(512)S(1)} %get-tuple-element.36.table, f32[8,512]{1,0:T(8,128)S(1)} %get-tuple-element.67.level, f32[8,512]{1,0:T(8,128)S(1)} %rows.3.part, f32[8,512]{1,0:T(8,128)S(1)} %collective-permute-done.44.near, f32[8,512]{1,0:T(8,128)S(1)} %collective-permute-done.45.far, ...), custom_call_target="tpu_custom_call" | custom-call | tf_op jit(solution)/shard_map/columns/pallas_call | solution.py:247
  144.9 16.4 %all_to_all.5 = f32[32,2,128]{2,1,0:T(2,128)S(1)} all-to-all(f32[32,2,128]{2,1,0:T(2,128)S(1)} %bitcast.39), channel_id=1, replica_groups=mesh['row'=32,'col'=4] {'row'}, dimensions={0} | all-to-all | bytes 65536 | tf_op jit(solution)/shard_map/all_to_all | solution.py:444
  (144 shorter events, 55.9 us)
Async XLA Ops:
  1.7 9.0 %collective-permute-start = (bf16[1,128,768]{2,1,0:T(8,128)(2,1)S(1)}, bf16[1,128,768]{2,1,0:T(8,128)(2,1)S(1)}, u32[]{:S(2)}, u32[]{:S(2)}) collective-permute-start(bf16[1,128,768]{2,1,0:T(8,128)(2,1)S(1)} %get-tuple-element.69), channel_id=1, source_target_pairs={{0,8},{4,12},{8,16},{12,20},{16,24},{20,28},{24,0},{28,4},{32,40},... | collective-permute-start | bytes 589832 | tf_op jit(solution)/shard_map/ppermute | solution.py:31
  3.9 15.5 %collective-permute-start.1 = (bf16[1,128,768]{2,1,0:T(8,128)(2,1)S(1)}, bf16[1,128,768]{2,1,0:T(8,128)(2,1)S(1)}, u32[]{:S(2)}, u32[]{:S(2)}) collective-permute-start(bf16[1,128,768]{2,1,0:T(8,128)(2,1)S(1)} %get-tuple-element.69), channel_id=1, source_target_pairs={{0,24},{4,28},{8,0},{12,4},{16,8},{20,12},{24,16},{28,20},{32,56},... | collective-permute-start | bytes 589832 | tf_op jit(solution)/shard_map/ppermute | solution.py:31
  5.4 14.0 %collective-permute-start.2 = (bf16[1,128,768]{2,1,0:T(8,128)(2,1)S(1)}, bf16[1,128,768]{2,1,0:T(8,128)(2,1)S(1)}, u32[]{:S(2)}, u32[]{:S(2)}) collective-permute-start(bf16[1,128,768]{2,1,0:T(8,128)(2,1)S(1)} %get-tuple-element.69), channel_id=1, source_target_pairs={{0,16},{4,20},{8,24},{12,28},{16,0},{20,4},{24,8},{28,12},{32,48},... | collective-permute-start | bytes 589832 | tf_op jit(solution)/shard_map/ppermute | solution.py:31
  7.0 12.4 %collective-permute-start.3 = (bf16[1,128,768]{2,1,0:T(8,128)(2,1)S(1)}, bf16[1,128,768]{2,1,0:T(8,128)(2,1)S(1)}, u32[]{:S(2)}, u32[]{:S(2)}) collective-permute-start(bf16[1,128,768]{2,1,0:T(8,128)(2,1)S(1)} %get-tuple-element.68), channel_id=1, source_target_pairs={{0,32},{4,36},{8,40},{12,44},{16,48},{20,52},{24,56},{28,60},{32,6... | collective-permute-start | bytes 589832 | tf_op jit(solution)/shard_map/ppermute | solution.py:31
  8.6 10.8 %collective-permute-start.4 = (bf16[1,128,768]{2,1,0:T(8,128)(2,1)S(1)}, bf16[1,128,768]{2,1,0:T(8,128)(2,1)S(1)}, u32[]{:S(2)}, u32[]{:S(2)}) collective-permute-start(bf16[1,128,768]{2,1,0:T(8,128)(2,1)S(1)} %get-tuple-element.68), channel_id=1, source_target_pairs={{0,96},{4,100},{8,104},{12,108},{16,112},{20,116},{24,120},{28,124... | collective-permute-start | bytes 589832 | tf_op jit(solution)/shard_map/ppermute | solution.py:31
  10.7 8.8 %collective-permute-start.5 = (bf16[1,128,768]{2,1,0:T(8,128)(2,1)S(1)}, bf16[1,128,768]{2,1,0:T(8,128)(2,1)S(1)}, u32[]{:S(2)}, u32[]{:S(2)}) collective-permute-start(bf16[1,128,768]{2,1,0:T(8,128)(2,1)S(1)} %get-tuple-element.68), channel_id=1, source_target_pairs={{0,64},{4,68},{8,72},{12,76},{16,80},{20,84},{24,88},{28,92},{32,9... | collective-permute-start | bytes 589832 | tf_op jit(solution)/shard_map/ppermute | solution.py:31
  19.6 6.3 %collective-permute-start.11 = (bf16[4,128,768]{2,1,0:T(8,128)(2,1)S(1)}, bf16[4,128,768]{2,1,0:T(8,128)(2,1)S(1)}, u32[]{:S(2)}, u32[]{:S(2)}) collective-permute-start(bf16[4,128,768]{2,1,0:T(8,128)(2,1)S(1)} %pad_maximum_fusion.1.refs_1_), channel_id=1, source_target_pairs={{0,4},{4,0},{8,12},{12,8},{16,20},{20,16},{24,28},{28,24},{32,36},... | collective-permute-start | bytes 2359304 | tf_op jit(solution)/shard_map/ppermute | solution.py:31
  22.3 5.5 %collective-permute-start.10 = (bf16[4,128,768]{2,1,0:T(8,128)(2,1)S(1)}, bf16[4,128,768]{2,1,0:T(8,128)(2,1)S(1)}, u32[]{:S(2)}, u32[]{:S(2)}) collective-permute-start(bf16[4,128,768]{2,1,0:T(8,128)(2,1)S(1)} %pad_maximum_fusion.refs_0_), channel_id=1, source_target_pairs={{0,4},{4,0},{8,12},{12,8},{16,20},{20,16},{24,28},{28,24},{32,36},... | collective-permute-start | bytes 2359304 | tf_op jit(solution)/shard_map/ppermute | solution.py:31
  22.4 20.0 %collective-permute-start.8 = (bf16[4,128,768]{2,1,0:T(8,128)(2,1)S(1)}, bf16[4,128,768]{2,1,0:T(8,128)(2,1)S(1)}, u32[]{:S(2)}, u32[]{:S(2)}) collective-permute-start(bf16[4,128,768]{2,1,0:T(8,128)(2,1)S(1)} %pad_maximum_fusion.1.refs_1_), channel_id=1, source_target_pairs={{0,8},{4,12},{8,16},{12,20},{16,24},{20,28},{24,0},{28,4},{32,40},... | collective-permute-start | bytes 2359304 | tf_op jit(solution)/shard_map/ppermute | solution.py:31
  22.8 21.6 %collective-permute-start.9 = (bf16[4,128,768]{2,1,0:T(8,128)(2,1)S(1)}, bf16[4,128,768]{2,1,0:T(8,128)(2,1)S(1)}, u32[]{:S(2)}, u32[]{:S(2)}) collective-permute-start(bf16[4,128,768]{2,1,0:T(8,128)(2,1)S(1)} %pad_maximum_fusion.1.refs_1_), channel_id=1, source_target_pairs={{0,24},{4,28},{8,0},{12,4},{16,8},{20,12},{24,16},{28,20},{32,56},... | collective-permute-start | bytes 2359304 | tf_op jit(solution)/shard_map/ppermute | solution.py:31
  25.1 19.3 %collective-permute-start.6 = (bf16[4,128,768]{2,1,0:T(8,128)(2,1)S(1)}, bf16[4,128,768]{2,1,0:T(8,128)(2,1)S(1)}, u32[]{:S(2)}, u32[]{:S(2)}) collective-permute-start(bf16[4,128,768]{2,1,0:T(8,128)(2,1)S(1)} %pad_maximum_fusion.refs_0_), channel_id=1, source_target_pairs={{0,32},{4,36},{8,40},{12,44},{16,48},{20,52},{24,56},{28,60},{32,6... | collective-permute-start | bytes 2359304 | tf_op jit(solution)/shard_map/ppermute | solution.py:31
  26.0 18.4 %collective-permute-start.7 = (bf16[4,128,768]{2,1,0:T(8,128)(2,1)S(1)}, bf16[4,128,768]{2,1,0:T(8,128)(2,1)S(1)}, u32[]{:S(2)}, u32[]{:S(2)}) collective-permute-start(bf16[4,128,768]{2,1,0:T(8,128)(2,1)S(1)} %pad_maximum_fusion.refs_0_), channel_id=1, source_target_pairs={{0,96},{4,100},{8,104},{12,108},{16,112},{20,116},{24,120},{28,124... | collective-permute-start | bytes 2359304 | tf_op jit(solution)/shard_map/ppermute | solution.py:31
  46.4 4.5 %collective-permute-start.17 = (bf16[4,128,768]{2,1,0:T(8,128)(2,1)S(1)}, bf16[4,128,768]{2,1,0:T(8,128)(2,1)S(1)}, u32[]{:S(2)}, u32[]{:S(2)}) collective-permute-start(bf16[4,128,768]{2,1,0:T(8,128)(2,1)S(1)} %collective-permute-done.7.refs_1_), channel_id=1, source_target_pairs={{0,4},{4,0},{8,12},{12,8},{16,20},{20,16},{24,28},{28,24},{32,36},... | collective-permute-start | bytes 2359304 | tf_op jit(solution)/shard_map/ppermute | solution.py:31
  46.5 6.5 %collective-permute-start.18 = (bf16[4,128,768]{2,1,0:T(8,128)(2,1)S(1)}, bf16[4,128,768]{2,1,0:T(8,128)(2,1)S(1)}, u32[]{:S(2)}, u32[]{:S(2)}) collective-permute-start(bf16[4,128,768]{2,1,0:T(8,128)(2,1)S(1)} %collective-permute-done.8.refs_2_), channel_id=1, source_target_pairs={{0,4},{4,0},{8,12},{12,8},{16,20},{20,16},{24,28},{28,24},{32,36},... | collective-permute-start | bytes 2359304 | tf_op jit(solution)/shard_map/ppermute | solution.py:31
  46.9 7.1 %collective-permute-start.19 = (bf16[4,128,768]{2,1,0:T(8,128)(2,1)S(1)}, bf16[4,128,768]{2,1,0:T(8,128)(2,1)S(1)}, u32[]{:S(2)}, u32[]{:S(2)}) collective-permute-start(bf16[4,128,768]{2,1,0:T(8,128)(2,1)S(1)} %collective-permute-done.9.refs_3_), channel_id=1, source_target_pairs={{0,4},{4,0},{8,12},{12,8},{16,20},{20,16},{24,28},{28,24},{32,36},... | collective-permute-start | bytes 2359304 | tf_op jit(solution)/shard_map/ppermute | solution.py:31
  47.1 18.1 %collective-permute-start.12 = (bf16[2,128,768]{2,1,0:T(8,128)(2,1)S(1)}, bf16[2,128,768]{2,1,0:T(8,128)(2,1)S(1)}, u32[]{:S(2)}, u32[]{:S(2)}) collective-permute-start(bf16[2,128,768]{2,1,0:T(8,128)(2,1)S(1)} %slice.41), channel_id=1, source_target_pairs={{0,32},{4,36},{8,40},{12,44},{16,48},{20,52},{24,56},{28,60},{32,6... | collective-permute-start | bytes 1179656 | tf_op jit(solution)/shard_map/ppermute | solution.py:31
  48.3 17.0 %collective-permute-start.13 = (bf16[2,128,768]{2,1,0:T(8,128)(2,1)S(1)}, bf16[2,128,768]{2,1,0:T(8,128)(2,1)S(1)}, u32[]{:S(2)}, u32[]{:S(2)}) collective-permute-start(bf16[2,128,768]{2,1,0:T(8,128)(2,1)S(1)} %slice.42), channel_id=1, source_target_pairs={{0,96},{4,100},{8,104},{12,108},{16,112},{20,116},{24,120},{28,124... | collective-permute-start | bytes 1179656 | tf_op jit(solution)/shard_map/ppermute | solution.py:31
  50.9 14.4 %collective-permute-start.14 = (bf16[2,128,768]{2,1,0:T(8,128)(2,1)S(1)}, bf16[2,128,768]{2,1,0:T(8,128)(2,1)S(1)}, u32[]{:S(2)}, u32[]{:S(2)}) collective-permute-start(bf16[2,128,768]{2,1,0:T(8,128)(2,1)S(1)} %slice.43), channel_id=1, source_target_pairs={{0,8},{4,12},{8,16},{12,20},{16,24},{20,28},{24,0},{28,4},{32,40},... | collective-permute-start | bytes 1179656 | tf_op jit(solution)/shard_map/ppermute | solution.py:31
  53.0 12.3 %collective-permute-start.15 = (bf16[2,128,768]{2,1,0:T(8,128)(2,1)S(1)}, bf16[2,128,768]{2,1,0:T(8,128)(2,1)S(1)}, u32[]{:S(2)}, u32[]{:S(2)}) collective-permute-start(bf16[2,128,768]{2,1,0:T(8,128)(2,1)S(1)} %slice.44), channel_id=1, source_target_pairs={{0,24},{4,28},{8,0},{12,4},{16,8},{20,12},{24,16},{28,20},{32,56},... | collective-permute-start | bytes 1179656 | tf_op jit(solution)/shard_map/ppermute | solution.py:31
  76.9 4.9 %collective-permute-start.24 = (f32[2,8,512]{2,1,0:T(8,128)S(1)}, f32[2,8,512]{2,1,0:T(8,128)S(1)}, u32[]{:S(2)}, u32[]{:S(2)}) collective-permute-start(f32[2,8,512]{2,1,0:T(8,128)S(1)} %pad_maximum_fusion.2), channel_id=1, source_target_pairs={{0,1},{1,2},{2,3},{3,0},{4,5},{5,6},{6,7},{7,4},{8,9},{9,10},{10,1... | collective-permute-start | bytes 98312 | tf_op jit(solution)/shard_map/ppermute | solution.py:312
  96.5 4.4 %collective-permute-start.32 = (f32[64,128]{1,0:T(8,128)S(1)}, f32[64,128]{1,0:T(8,128)S(1)}, u32[]{:S(2)}, u32[]{:S(2)}) collective-permute-start(f32[64,128]{1,0:T(8,128)S(1)} %add_add_fusion.3), channel_id=1, source_target_pairs={{0,64},{4,68},{8,72},{12,76},{16,80},{20,84},{24,88},{28,92},{32,9... | collective-permute-start | bytes 98312 | tf_op jit(solution)/shard_map/ppermute | solution.py:31
  104.7 4.8 %collective-permute-start.35 = (f32[8,512]{1,0:T(8,128)S(1)}, f32[8,512]{1,0:T(8,128)S(1)}, u32[]{:S(2)}, u32[]{:S(2)}) collective-permute-start(f32[8,512]{1,0:T(8,128)S(1)} %rows.2.part), channel_id=1, source_target_pairs={{0,2},{1,3},{2,0},{3,1},{4,6},{5,7},{6,4},{7,5},{8,10},{9,11},{10,... | collective-permute-start | bytes 49160 | tf_op jit(solution)/shard_map/ppermute | solution.py:312
  114.3 5.8 %collective-permute-start.37 = (f32[64,128]{1,0:T(8,128)S(1)}, f32[64,128]{1,0:T(8,128)S(1)}, u32[]{:S(2)}, u32[]{:S(2)}) collective-permute-start(f32[64,128]{1,0:T(8,128)S(1)} %columns.4), channel_id=1, source_target_pairs={{0,4},{4,0},{8,12},{12,8},{16,20},{20,16},{24,28},{28,24},{32,36},... | collective-permute-start | bytes 98312 | tf_op jit(solution)/shard_map/ppermute | solution.py:31
  121.0 4.9 %collective-permute-start.39 = (f32[64,128]{1,0:T(8,128)S(1)}, f32[64,128]{1,0:T(8,128)S(1)}, u32[]{:S(2)}, u32[]{:S(2)}) collective-permute-start(f32[64,128]{1,0:T(8,128)S(1)} %add.55), channel_id=1, source_target_pairs={{0,16},{4,20},{8,24},{12,28},{16,0},{20,4},{24,8},{28,12},{32,48},... | collective-permute-start | bytes 98312 | tf_op jit(solution)/shard_map/ppermute | solution.py:31
  (46 other events, 166.5 us)
